TPU v7x, 32 devices: a whole 2x2x4 slice. The times are simulated.
32 devices in a mesh: ctx: 8 (over z, core), grp: 4 (over y, x).
Axes of the slice: x: 2, y: 2, z: 4, core: 2. Of those that a mesh axis runs over, the one named last changes fastest.
Arguments:
- queries: bfloat16 [1, 4096, 4096], P(None, ('ctx', 'grp')), may hold values from -200 to 200
- keyvals: bfloat16 [2, 1, 4096, 512], P(None, None, ('ctx', 'grp')), may hold values from -8 to 8
- seg_len: int32 [1, 16], replicated, may hold values from 128 to 384, as said below
- seg_task: int32 [1, 16], replicated, may hold values from 0 to 23
- task_slot: int32 [24], replicated, may hold values from 0 to 23, each once
- prefix_bank: bfloat16 [2, 24, 16, 512], P(None, 'grp'), may hold values from -9 to 9
Outputs:
- attended: bfloat16 [1, 4096, 4096], P(None, ('ctx', 'grp'))
Inputs may be any that keep to these rules, and one draw needn't show every extreme that they name: `seg_len`: the 16 lengths sum to 4096, and at least one equals 384. `task_slot`: A permutation; bank row r is held by index r // 6 of grp.
All inputs are finite; a program needn't handle non-finite values.
Results may differ from a plain program's by a relative error of at most 0.004.
Values may be sent and summed in bfloat16 or wider, within the bound.
No kernel may reach another device: no remote copies, remote signals or barrier semaphores. Data moves between devices by JAX's collectives and lax.ppermute only.
A program may use at most 64 MiB of HBM per device.

v0:
```python
import math

import jax
import jax.numpy as jnp
from jax import lax
from jax.sharding import PartitionSpec as P

H = 32
KVH = 4
HD = 128
HOPS = 3


def shifted(block, axis, distance):
    devices = range(lax.axis_size(axis))
    route = [(i - distance, i) for i in devices if i - distance in devices]
    return lax.ppermute(block, axis, route)


def segment_index(starts, positions):
    return jnp.sum((starts[None, :] <= positions[:, None]).astype(jnp.int32), axis=1) - 1


def on_device(queries, keyvals, seg_len, seg_task, task_slot, prefix_bank):
    shard_len = queries.shape[1]
    groups = H // KVH
    feature_width = KVH * HD
    score_scale = 1.0 / math.sqrt(HD)
    grp_count = lax.axis_size("grp")
    shard_index = lax.axis_index("ctx") * grp_count + lax.axis_index("grp")
    task_dev = prefix_bank.shape[1]
    grouped_q = queries[0].reshape(shard_len, KVH, groups, HD)
    lengths = seg_len[0]
    row_tasks = seg_task[0]
    starts = jnp.cumsum(lengths) - lengths
    offsets = jnp.arange(shard_len, dtype=jnp.int32)
    query_pos = shard_index * shard_len + offsets
    query_seg = segment_index(starts, query_pos)

    def attend(carry_state, key_rows, value_rows, allowed):
        max_old, total_old, mixed_old = carry_state
        key_heads = key_rows.reshape(-1, KVH, HD)
        value_heads = value_rows.reshape(-1, KVH, HD)
        scores = (
            jnp.einsum("tkgd,skd->kgts", grouped_q, key_heads, preferred_element_type=jnp.float32)
            * score_scale
        )
        max_new = jnp.maximum(max_old, jnp.max(jnp.where(allowed, scores, -1e30), axis=-1))
        weights = jnp.where(allowed, jnp.exp(scores - max_new[..., None]), 0.0)
        shrink = jnp.exp(max_old - max_new)
        total_new = total_old * shrink + jnp.sum(weights, axis=-1)
        mixed_new = mixed_old * shrink[..., None] + jnp.einsum(
            "kgts,skd->kgtd",
            weights.astype(jnp.bfloat16),
            value_heads,
            preferred_element_type=jnp.float32,
        )
        return (max_new, total_new, mixed_new)

    start_state = (
        jnp.full((KVH, groups, shard_len), -1e30, jnp.float32),
        jnp.zeros((KVH, groups, shard_len), jnp.float32),
        jnp.zeros((KVH, groups, shard_len, HD), jnp.float32),
    )
    local_allowed = (query_seg[None, :] == query_seg[:, None]) & (
        query_pos[None, :] <= query_pos[:, None]
    )
    carry_state = attend(start_state, keyvals[0, 0], keyvals[1, 0], local_allowed)
    local_pair = keyvals[:, 0]
    for hop_count in range(1, HOPS + 1):
        kv_piece = shifted(local_pair, ("ctx", "grp"), hop_count)
        key_pos = (shard_index - hop_count) * shard_len + offsets
        key_seg = segment_index(starts, key_pos)
        remote_allowed = query_seg[:, None] == key_seg[None, :]
        carry_state = attend(carry_state, kv_piece[0], kv_piece[1], remote_allowed)
    slot_seg = jnp.stack(
        [query_seg[0], jnp.where(query_seg[-1] != query_seg[0], query_seg[-1], -1)]
    )
    seg_pick = jnp.arange(row_tasks.shape[0])[None, :] == slot_seg[:, None]
    slot_task = jnp.sum(jnp.where(seg_pick, row_tasks[None, :], 0), axis=1)
    task_pick = jnp.arange(task_slot.shape[0])[None, :] == slot_task[:, None]
    bank_row = jnp.sum(jnp.where(task_pick, task_slot[None, :], 0), axis=1)
    owner_grp = bank_row // task_dev
    local_row = bank_row % task_dev
    slot_valid = slot_seg >= 0
    from_owner = jnp.arange(grp_count)[:, None] == owner_grp[None, :]
    requests = jnp.where(from_owner & slot_valid[None, :], local_row[None, :], -1)
    onehot = (
        lax.all_to_all(requests, "grp", split_axis=0, concat_axis=0, tiled=True)[..., None]
        == jnp.arange(task_dev)
    ).astype(jnp.bfloat16)
    bank_rows = jnp.einsum(
        "gnt,ctpf->gncpf", onehot, prefix_bank, preferred_element_type=jnp.float32
    ).astype(jnp.bfloat16)
    replies = lax.all_to_all(bank_rows, "grp", split_axis=0, concat_axis=0, tiled=True)
    fetched = jnp.sum(
        jnp.where(from_owner[:, :, None, None, None], replies.astype(jnp.float32), 0.0), axis=0
    ).astype(jnp.bfloat16)
    prefix_keys = fetched[:, 0].reshape(-1, feature_width)
    prefix_values = fetched[:, 1].reshape(-1, feature_width)
    prefix_seg = jnp.repeat(slot_seg, fetched.shape[2])
    prefix_allowed = query_seg[:, None] == prefix_seg[None, :]
    carry_state = attend(carry_state, prefix_keys, prefix_values, prefix_allowed)
    max_final, total_final, mixed_final = carry_state
    result = mixed_final / total_final[..., None]
    return result.transpose(2, 0, 1, 3).reshape(1, shard_len, H * HD).astype(jnp.bfloat16)


def solution(mesh):
    in_specs = (
        P(None, ("ctx", "grp"), None),
        P(None, None, ("ctx", "grp"), None),
        P(),
        P(),
        P(),
        P(None, "grp", None, None),
    )
    out_specs = P(None, ("ctx", "grp"), None)
    return jax.shard_map(
        on_device, mesh=mesh, in_specs=in_specs, out_specs=out_specs, check_vma=False
    )
```

profile of v0, /device:TPU:0, one launch (start us, length us, event | category | flops | bytes accessed | tf_op | source)
XLA Modules:
  0.0 55.2 jit_solution(8802428752428528552)
XLA Ops:
  0.0 1.8 %copy.70 = bf16[2,1,128,512]{2,3,0,1:T(8,128)(2,1)} copy(bf16[2,1,128,512]{3,2,1,0:T(8,128)(2,1)} %param.7) | data formatting | bytes 524288 | tf_op args[1]
  1.8 6.5 %collective-permute-start.2 = (bf16[2,128,512]{1,2,0:T(8,128)(2,1)}, bf16[2,128,512]{1,2,0:T(8,128)(2,1)}, u32[]{:S(2)}, u32[]{:S(2)}) collective-permute-start(bf16[2,128,512]{1,2,0:T(8,128)(2,1)} %bitcast.9), channel_id=1, source_target_pairs={{0,3},{1,4},{2,5},{3,6},{4,7},{5,8},{6,9},{7,10},{8,11},{9,12},{10... | collective-permute-start | bytes 786440 | tf_op jit(solution)/shard_map/ppermute | solution.py:17
  8.3 2.5 %collective-permute-start.1 = (bf16[2,128,512]{1,2,0:T(8,128)(2,1)}, bf16[2,128,512]{1,2,0:T(8,128)(2,1)}, u32[]{:S(2)}, u32[]{:S(2)}) collective-permute-start(bf16[2,128,512]{1,2,0:T(8,128)(2,1)} %bitcast.9), channel_id=1, source_target_pairs={{0,2},{1,3},{2,4},{3,5},{4,6},{5,7},{6,8},{7,9},{8,10},{9,11},{10,... | collective-permute-start | bytes 786440 | tf_op jit(solution)/shard_map/ppermute | solution.py:17
  10.8 2.5 %collective-permute-start = (bf16[2,128,512]{1,2,0:T(8,128)(2,1)}, bf16[2,128,512]{1,2,0:T(8,128)(2,1)}, u32[]{:S(2)}, u32[]{:S(2)}) collective-permute-start(bf16[2,128,512]{1,2,0:T(8,128)(2,1)} %bitcast.9), channel_id=1, source_target_pairs={{0,1},{1,2},{2,3},{3,4},{4,5},{5,6},{6,7},{7,8},{8,9},{9,10},{10,1... | collective-permute-start | bytes 786440 | tf_op jit(solution)/shard_map/ppermute | solution.py:17
  13.4 0.8 %reduce-window_clone.1 = s32[1,16]{1,0:T(1,128)S(1)} reduce-window(s32[1,16]{1,0:T(1,128)} %param.8, s32[]{:T(128)} %constant.24.clone.1), window={size=1x16 pad=0_0x15_0}, to_apply=%region_0.0 | reduce-window | flops 240 | bytes 132 | tf_op jit(solution)/shard_map/reduce-window.clone
  14.2 0.7 %subtract_bitcast_fusion = s32[16]{0:T(128)S(1)} fusion(s32[1,16]{1,0:T(1,128)S(1)} %reduce-window_clone.1, s32[1,16]{1,0:T(1,128)} %param.8), kind=kLoop, calls=%fused_computation.130 | loop fusion | flops 16 | bytes 192 | tf_op jit(solution)/shard_map/le | solution.py:21
  14.9 0.1 convert_reduce_fusion
  15.0 0.7 %fusion.101 = (s32[1]{0:T(128)}, s32[1]{0:T(128)}) fusion(s32[128]{0:T(128)S(1)} %get-tuple-element.53), kind=kLoop, calls=%fused_computation.152 | loop fusion | bytes 16 | tf_op jit(solution)/shard_map/slice | solution.py:77
  17.7 0.7 %broadcast_compare_fusion.4 = (pred[2]{0:T(512)(128)(4,1)S(1)}, s32[2]{0:T(128)S(1)}) fusion(s32[1]{0:T(128)} %bitcast.36, s32[1]{0:T(128)} %get-tuple-element.38), kind=kLoop, calls=%fused_computation.131 | loop fusion | flops 4 | bytes 18 | tf_op jit(solution)/shard_map/ge | solution.py:85
  18.4 0.8 %fusion.81 = s32[2]{0:T(128)S(1)} fusion(s32[16]{0:T(128)} %bitcast.277, s32[2]{0:T(128)S(1)} %get-tuple-element.18), kind=kLoop, calls=%fused_computation.123 | loop fusion | flops 94 | bytes 80 | tf_op jit(solution)/shard_map/reduce_sum | solution.py:80
  19.3 0.8 %fusion.82 = s32[2]{0:T(128)S(1)} fusion(s32[24]{0:T(128)} %param.10, s32[2]{0:T(128)S(1)} %fusion.81), kind=kLoop, calls=%fused_computation.124 | loop fusion | flops 142 | bytes 112 | tf_op jit(solution)/shard_map/reduce_sum | solution.py:82
  20.1 0.6 %and_select_fusion = s32[4,1,2]{2,1,0:T(1,128)} fusion(pred[2]{0:T(512)(128)(4,1)S(1)} %get-tuple-element.17, s32[2]{0:T(128)S(1)} %get-tuple-element.37, s32[2]{0:T(128)S(1)} %get-tuple-element.36), kind=kLoop, calls=%fused_computation.114 | loop fusion | flops 24 | bytes 50 | tf_op jit(solution)/shard_map/jit(_where)/select_n | solution.py:87
  20.7 3.2 %all-to-all-start = ((s32[4,1,2]{2,1,0:T(1,128)}), s32[4,1,2]{2,1,0:T(1,128)S(1)}, u32[]{:S(2)}, u32[]{:S(2)}) async-start(s32[4,1,2]{2,1,0:T(1,128)} %and_select_fusion), calls=%async_computation | async-start | bytes 4096 | tf_op jit(solution)/shard_map/all_to_all | solution.py:89
  23.9 1.0 %fusion.97 = (bf16[1,1,128,512]{3,2,1,0:T(8,128)(2,1)S(1)}, bf16[1,1,128,512]{3,2,1,0:T(8,128)(2,1)S(1)}) fusion(bf16[2,1,128,512]{3,2,1,0:T(8,128)(2,1)} %param.7), kind=kLoop, calls=%fused_computation.148 | loop fusion | bytes 524288 | tf_op jit(solution)/shard_map/slice | solution.py:68
  24.9 1.4 %copy.117 = bf16[16,8,32,128]{3,2,1,0:T(8,128)(2,1)S(1)} copy(bf16[16,8,32,128]{3,1,2,0:T(8,128)(2,1)} %bitcast.264) | data formatting | bytes 2097152
  26.4 0.1 copy.116
  26.5 0.1 broadcast_in_dim.155
  26.6 0.1 eq.142
  26.7 0.7 %broadcast_compare_fusion.3 = pred[128,32]{0,1:T(8,128)(4,1)} fusion(s32[128]{0:T(128)S(1)} %get-tuple-element.53, s32[32]{0:T(128)S(1)} %eq.142), kind=kLoop, calls=%fused_computation.108 | loop fusion | flops 4096 | bytes 4736 | tf_op jit(solution)/shard_map/eq | solution.py:102
  27.3 0.1 copy.68
  27.5 0.0 copy-done.6
  27.5 0.8 %compare_and_fusion = (pred[128,128]{0,1:T(8,128)(4,1)S(1)}, pred[128,128]{0,1:T(8,128)(4,1)S(1)}, pred[128,128]{0,1:T(8,128)(4,1)}, pred[128,128]{0,1:T(8,128)(4,1)}) fusion(s32[128]{0:T(128)S(1)} %iota_add_fusion.3, s32[128]{0:T(128)S(1)} %get-tuple-element.53, s32[128]{0:T(128)S(1)} %get-tuple-element.51, s32[128]{0:T(128)S(1)} %get-tuple-element.50, ...), kind=kLoop, calls=%fused_computation.81 | loop fusion | flops 98304 | bytes 68096 | tf_op jit(solution)/shard_map/and | solution.py:65
  28.2 0.0 copy-start.1
  28.2 1.2 %fusion.15 = (f32[4,8,128]{2,1,0:T(8,128)}, f32[4,128,128,8]{2,1,3,0:T(8,128)S(1)}) fusion(pred[128,128]{0,1:T(8,128)(4,1)S(1)} %get-tuple-element.32, bf16[128,4,128,1]{0,2,3,1:T(8,128)(2,1)S(1)} %bitcast.267, bf16[128,4,8,128]{3,2,1,0:T(8,128)(2,1)S(1)} %bitcast.259), kind=kOutput, calls=%fused_computation.28 | convolution fusion | flops 135786496 | bytes 3309568 | tf_op jit(solution)/shard_map/tkgd,skd->kgts/dot_general | solution.py:45
  29.5 0.0 all-to-all-done
  29.5 0.1 copy.80
  29.6 1.2 %convolution_convert_fusion = bf16[4,2,2,16,512]{4,0,3,2,1:T(4,128)(2,1)S(1)} fusion(bf16[2,6,16,512]{3,2,1,0:T(8,128)(2,1)} %param.11, s32[4,2]{0,1:T(2,128)S(1)} %bitcast.276), kind=kOutput, calls=%fused_computation.41 | convolution fusion | flops 1703984 | bytes 458784 | tf_op jit(solution)/shard_map/gnt,ctpf->gncpf/dot_general | solution.py:92
  30.8 0.8 %copy.82 = bf16[4,2,2,16,512]{4,3,2,1,0:T(8,128)(2,1)} copy(bf16[4,2,2,16,512]{4,0,3,2,1:T(4,128)(2,1)S(1)} %convolution_convert_fusion) | data formatting | bytes 524288 | tf_op jit(solution)/shard_map/convert_element_type | solution.py:94
  31.5 0.0 copy-done.1
  31.5 4.2 %all-to-all-start.1 = ((bf16[4,2,2,16,512]{4,3,2,1,0:T(8,128)(2,1)}), bf16[4,2,2,16,512]{4,3,2,1,0:T(8,128)(2,1)S(1)}, u32[]{:S(2)}, u32[]{:S(2)}) async-start(bf16[4,2,2,16,512]{4,3,2,1,0:T(8,128)(2,1)} %copy.82), calls=%async_computation.1 | async-start | bytes 524288 | tf_op jit(solution)/shard_map/all_to_all | solution.py:95
  35.7 1.2 %iota_compare_fusion.1 = pred[4,2]{1,0:T(4,128)(4,1)} fusion(s32[2]{0:T(128)} %copy-done.6), kind=kLoop, calls=%fused_computation.118 | loop fusion | flops 8 | bytes 16 | tf_op jit(solution)/shard_map/eq | solution.py:86
  37.0 4.2 %all-to-all-done.1 = bf16[4,2,2,16,512]{4,3,2,1,0:T(8,128)(2,1)S(1)} async-done(((bf16[4,2,2,16,512]{4,3,2,1,0:T(8,128)(2,1)}), bf16[4,2,2,16,512]{4,3,2,1,0:T(8,128)(2,1)S(1)}, u32[]{:S(2)}, u32[]{:S(2)}) %all-to-all-start.1) | async-done | bytes 262176 | tf_op jit(solution)/shard_map/all_to_all | solution.py:95
  41.2 0.8 %select_reduce_fusion.1 = bf16[2,2,16,512]{3,2,1,0:T(8,128)(2,1)S(1)} fusion(bf16[4,2,2,16,512]{4,3,2,1,0:T(8,128)(2,1)S(1)} %all-to-all-done.1, pred[4,2]{1,0:T(4,128)(4,1)} %iota_compare_fusion.1), kind=kLoop, calls=%fused_computation.72 | loop fusion | flops 360448 | bytes 327688 | tf_op jit(solution)/shard_map/reduce_sum | solution.py:96
  42.0 0.0 copy-start.3
  42.1 1.2 %select_reduce_fusion = (f32[4,8,128]{2,1,0:T(8,128)S(1)}, f32[4,8,128,32]{2,3,1,0:T(8,128)S(1)}) fusion(pred[128,32]{0,1:T(8,128)(4,1)} %broadcast_compare_fusion.3, bf16[128,4,8,128]{3,2,1,0:T(8,128)(2,1)S(1)} %bitcast.260, bf16[32,4,128,1]{2,1,0,3:T(4,128)(2,1)S(1)} %bitcast.273), kind=kOutput, calls=%fused_computation.71 | convolution fusion | flops 33943552 | bytes 1626112 | tf_op jit(solution)/shard_map/tkgd,skd->kgts/dot_general | solution.py:45
  43.3 0.0 collective-permute-done.2
  43.3 1.0 %fusion.96 = (bf16[1,128,512]{1,2,0:T(8,128)(2,1)S(1)}, bf16[1,128,512]{1,2,0:T(8,128)(2,1)S(1)}) fusion(bf16[2,128,512]{1,2,0:T(8,128)(2,1)} %collective-permute-done.2), kind=kLoop, calls=%fused_computation.147 | loop fusion | bytes 524288 | tf_op jit(solution)/shard_map/slice | solution.py:75
  44.3 0.0 copy-done.3
  44.3 0.7 %fusion.3 = (f32[4,8,128]{2,1,0:T(8,128)S(1)}, f32[4,128,128,8]{2,1,3,0:T(8,128)S(1)}) fusion(pred[128,128]{0,1:T(8,128)(4,1)S(1)} %copy-done.3, bf16[128,4,128,1]{0,2,3,1:T(8,128)(2,1)S(1)} %bitcast.271, bf16[128,4,8,128]{3,2,1,0:T(8,128)(2,1)S(1)} %bitcast.261), kind=kOutput, calls=%fused_computation.7 | convolution fusion | flops 135786496 | bytes 3309568 | tf_op jit(solution)/shard_map/tkgd,skd->kgts/dot_general | solution.py:45
  44.9 0.0 copy-start
  45.0 0.0 collective-permute-done.1
  45.0 1.0 %fusion.99 = (bf16[1,128,512]{1,2,0:T(8,128)(2,1)S(1)}, bf16[1,128,512]{1,2,0:T(8,128)(2,1)S(1)}) fusion(bf16[2,128,512]{1,2,0:T(8,128)(2,1)} %collective-permute-done.1), kind=kLoop, calls=%fused_computation.150 | loop fusion | bytes 524288 | tf_op jit(solution)/shard_map/slice | solution.py:75
  46.0 0.7 %fusion.7 = (f32[4,8,128]{2,1,0:T(8,128)S(1)}, f32[4,128,128,8]{2,1,3,0:T(8,128)S(1)}) fusion(pred[128,128]{0,1:T(8,128)(4,1)S(1)} %get-tuple-element.33, bf16[128,4,128,1]{0,2,3,1:T(8,128)(2,1)S(1)} %bitcast.272, bf16[128,4,8,128]{3,2,1,0:T(8,128)(2,1)S(1)} %bitcast.262), kind=kOutput, calls=%fused_computation.14 | convolution fusion | flops 135786496 | bytes 3309568 | tf_op jit(solution)/shard_map/tkgd,skd->kgts/dot_general | solution.py:45
  46.6 0.0 copy-start.4
  46.6 0.0 copy-start.2
  46.7 0.0 collective-permute-done
  46.7 1.0 %fusion.98 = (bf16[1,128,512]{1,2,0:T(8,128)(2,1)S(1)}, bf16[1,128,512]{1,2,0:T(8,128)(2,1)S(1)}) fusion(bf16[2,128,512]{1,2,0:T(8,128)(2,1)} %collective-permute-done), kind=kLoop, calls=%fused_computation.149 | loop fusion | bytes 524288 | tf_op jit(solution)/shard_map/slice | solution.py:75
  47.7 0.0 copy-done
  47.7 0.7 %fusion.11 = (f32[4,8,128]{2,1,0:T(8,128)S(1)}, f32[4,128,128,8]{2,1,3,0:T(8,128)S(1)}) fusion(pred[128,128]{0,1:T(8,128)(4,1)S(1)} %copy-done, bf16[128,4,128,1]{0,2,3,1:T(8,128)(2,1)S(1)} %bitcast.270, bf16[128,4,8,128]{3,2,1,0:T(8,128)(2,1)S(1)} %bitcast.263), kind=kOutput, calls=%fused_computation.21 | convolution fusion | flops 135786496 | bytes 3309568 | tf_op jit(solution)/shard_map/tkgd,skd->kgts/dot_general | solution.py:45
  48.3 0.0 copy-done.4
  48.4 0.0 copy-done.2
  48.4 0.5 fusion.18
  48.9 0.5 fusion.32
  49.4 0.5 fusion.20
  49.9 0.5 fusion.30
  50.4 0.5 fusion.22
  50.9 0.0 copy-start.5
  50.9 0.5 fusion.28
  51.4 0.1 copy-done.5
  51.5 0.1 fusion.59
  51.7 0.5 fusion.61
  52.2 0.5 fusion.24
  52.7 1.2 %fusion.1 = bf16[128,4,8,128]{0,3,2,1:T(8,128)(2,1)S(1)} fusion(f32[4,8,128,128]{2,3,1,0:T(8,128)S(1)} %fusion.61, f32[4,8,128,128]{2,3,1,0:T(8,128)S(1)} %fusion.28, f32[4,8,128,128]{2,3,1,0:T(8,128)S(1)} %fusion.30, f32[4,8,128,128]{2,3,1,0:T(8,128)S(1)} %fusion.32, bf16[128,4,128,1]{0,2,3,1:T(8,128)(2,1)S(1)} %bitcast.274, ...), kind=kOutput, calls=%fused_computation.2 | convolution fusion | flops 142082048 | bytes 11796480 | tf_op jit(solution)/shard_map/kgts,skd->kgtd/dot_general | solution.py:52
  53.9 1.3 %copy.87 = bf16[1,128,4096]{2,1,0:T(8,128)(2,1)} copy(bf16[1,128,4096]{1,2,0:T(8,128)(2,1)S(1)} %bitcast.265) | data formatting | bytes 2097152 | tf_op jit(solution)/shard_map/convert_element_type | solution.py:106
  (13 shorter events, 0.1 us)
Async XLA Ops:
  1.8 41.5 %collective-permute-start.2 = (bf16[2,128,512]{1,2,0:T(8,128)(2,1)}, bf16[2,128,512]{1,2,0:T(8,128)(2,1)}, u32[]{:S(2)}, u32[]{:S(2)}) collective-permute-start(bf16[2,128,512]{1,2,0:T(8,128)(2,1)} %bitcast.9), channel_id=1, source_target_pairs={{0,3},{1,4},{2,5},{3,6},{4,7},{5,8},{6,9},{7,10},{8,11},{9,12},{10... | collective-permute-start | bytes 786440 | tf_op jit(solution)/shard_map/ppermute | solution.py:17
  8.3 36.7 %collective-permute-start.1 = (bf16[2,128,512]{1,2,0:T(8,128)(2,1)}, bf16[2,128,512]{1,2,0:T(8,128)(2,1)}, u32[]{:S(2)}, u32[]{:S(2)}) collective-permute-start(bf16[2,128,512]{1,2,0:T(8,128)(2,1)} %bitcast.9), channel_id=1, source_target_pairs={{0,2},{1,3},{2,4},{3,5},{4,6},{5,7},{6,8},{7,9},{8,10},{9,11},{10,... | collective-permute-start | bytes 786440 | tf_op jit(solution)/shard_map/ppermute | solution.py:17
  10.8 35.8 %collective-permute-start = (bf16[2,128,512]{1,2,0:T(8,128)(2,1)}, bf16[2,128,512]{1,2,0:T(8,128)(2,1)}, u32[]{:S(2)}, u32[]{:S(2)}) collective-permute-start(bf16[2,128,512]{1,2,0:T(8,128)(2,1)} %bitcast.9), channel_id=1, source_target_pairs={{0,1},{1,2},{2,3},{3,4},{4,5},{5,6},{6,7},{7,8},{8,9},{9,10},{10,1... | collective-permute-start | bytes 786440 | tf_op jit(solution)/shard_map/ppermute | solution.py:17
  20.1 7.4 %copy-start.6 = (s32[2]{0:T(128)}, s32[2]{0:T(128)S(1)}, u32[]{:S(2)}) copy-start(s32[2]{0:T(128)S(1)} %get-tuple-element.36) | copy-start | bytes 28
  20.7 8.8 %all-to-all-start = ((s32[4,1,2]{2,1,0:T(1,128)}), s32[4,1,2]{2,1,0:T(1,128)S(1)}, u32[]{:S(2)}, u32[]{:S(2)}) async-start(s32[4,1,2]{2,1,0:T(1,128)} %and_select_fusion), calls=%async_computation | async-start | bytes 4096 | tf_op jit(solution)/shard_map/all_to_all | solution.py:89
  28.2 3.3 %copy-start.1 = (pred[128,128]{0,1:T(8,128)(4,1)}, pred[128,128]{0,1:T(8,128)(4,1)S(1)}, u32[]{:S(2)}) copy-start(pred[128,128]{0,1:T(8,128)(4,1)S(1)} %get-tuple-element.32) | copy-start | bytes 49156
  31.5 9.7 %all-to-all-start.1 = ((bf16[4,2,2,16,512]{4,3,2,1,0:T(8,128)(2,1)}), bf16[4,2,2,16,512]{4,3,2,1,0:T(8,128)(2,1)S(1)}, u32[]{:S(2)}, u32[]{:S(2)}) async-start(bf16[4,2,2,16,512]{4,3,2,1,0:T(8,128)(2,1)} %copy.82), calls=%async_computation.1 | async-start | bytes 524288 | tf_op jit(solution)/shard_map/all_to_all | solution.py:95
  42.0 2.3 %copy-start.3 = (pred[128,128]{0,1:T(8,128)(4,1)S(1)}, pred[128,128]{0,1:T(8,128)(4,1)}, u32[]{:S(2)}) copy-start(pred[128,128]{0,1:T(8,128)(4,1)} %get-tuple-element.34) | copy-start | bytes 49156
  44.9 2.7 %copy-start = (pred[128,128]{0,1:T(8,128)(4,1)S(1)}, pred[128,128]{0,1:T(8,128)(4,1)}, u32[]{:S(2)}) copy-start(pred[128,128]{0,1:T(8,128)(4,1)} %get-tuple-element.35) | copy-start | bytes 49156
  46.6 1.7 %copy-start.4 = (f32[4,8,128]{2,1,0:T(8,128)S(1)}, f32[4,8,128]{2,1,0:T(8,128)}, u32[]{:S(2)}) copy-start(f32[4,8,128]{2,1,0:T(8,128)} %get-tuple-element.48) | copy-start | bytes 49156
  46.6 1.7 %copy-start.2 = (pred[128,128]{0,1:T(8,128)(4,1)S(1)}, pred[128,128]{0,1:T(8,128)(4,1)}, u32[]{:S(2)}) copy-start(pred[128,128]{0,1:T(8,128)(4,1)} %copy-done.1) | copy-start | bytes 49156
  50.9 0.7 %copy-start.5 = (pred[128,32]{0,1:T(8,128)(4,1)S(1)}, pred[128,32]{0,1:T(8,128)(4,1)}, u32[]{:S(2)}) copy-start(pred[128,32]{0,1:T(8,128)(4,1)} %broadcast_compare_fusion.3) | copy-start | bytes 12292
where the time goes:
time: 55.8 us; the launch traced here: 55.2 us
  starting transfers between devices  19 us (34%)
  local copies, waits for them, and re-layouts  10.6 us (19%)
  other arithmetic  10.1 us (18%)
  matrix products  8.86 us (16%)
  waiting for transfers between devices  4.23 us (8%)
  between operations  2.35 us (4%)
    ppermute x3, starting transfers between devices, shifted(): return lax.ppermute(block, axis, route)  11.6 us
    dot_general x5, matrix products, attend(): jnp.einsum('tkgd,skd->kgts', grouped_q, key_heads, preferred_element_type...  4.45 us
    all_to_all x1, waiting for transfers between devices, on_device(): lax.all_to_all(bank_rows, 'grp', split_axis=0, concat_axis=0, tiled=True)  4.22 us
    all_to_all x1, starting transfers between devices, on_device(): lax.all_to_all(bank_rows, 'grp', split_axis=0, concat_axis=0, tiled=True)  4.19 us
    unnamed x17, local copies, waits for them, and re-layouts  3.52 us
    all_to_all x1, starting transfers between devices, on_device(): lax.all_to_all(requests, 'grp', split_axis=0, concat_axis=0, tiled=True)  3.23 us
    dot_general x5, matrix products, attend(): jnp.einsum('kgts,skd->kgtd', weights.astype(jnp.bfloat16), value_heads, p...  3.2 us
    slice x3, local copies, waits for them, and re-layouts, on_device(): carry_state = attend(carry_state, kv_piece[0], kv_piece[1], remote_allowed)  2.96 us
  transfers between devices with their start and end apart: 5, of which 1 were waited for; matrix products, arithmetic and copies ran while one was open for 35% of the time, Pallas kernels for 0%

commit v1 on v0

v1 whole, which is shorter than its diff:
```python
import functools
import math

import jax
import jax.numpy as jnp
from jax import lax
from jax.experimental import pallas as pl
from jax.experimental.pallas import tpu as pltpu
from jax.sharding import PartitionSpec as P

HD = 128
HOPS = 3
FAR = -1e30
AXES = ("ctx", "grp")
VMEM = pl.BlockSpec(memory_space=pltpu.VMEM)
SMEM = pl.BlockSpec(memory_space=pltpu.SMEM)
PARAMS = pltpu.CompilerParams(vmem_limit_bytes=40 * 2**20)


def shift_route(count, distance):
    return [(i, (i + distance) % count) for i in range(count)]


def flip_route(ctx_count, grp_count, flip):
    count = ctx_count * grp_count
    return [
        (i, (i + ((i % grp_count ^ flip) - i % grp_count) % grp_count) % count)
        for i in range(count)
    ]


def compose_route(wanted, first):
    holder = dict(first)
    return [(holder[s], d) for s, d in wanted]


def shard_segments(len_ref, firsts, shard_len):
    def step(s, carry):
        start, found = carry
        out = []
        for first, (seg_a, start_a, seg_b, start_b) in zip(firsts, found):
            in_a = start <= first
            in_b = start <= first + (shard_len - 1)
            out.append(
                (
                    jnp.where(in_a, s, seg_a),
                    jnp.where(in_a, start, start_a),
                    jnp.where(in_b, s, seg_b),
                    jnp.where(in_b, start, start_b),
                )
            )
        return start + len_ref[0, s], out

    zero = jnp.int32(0)
    _, found = lax.fori_loop(
        0, len_ref.shape[1], step, (zero, [(zero, zero, zero, zero)] * len(firsts))
    )
    return found


def bank_rows(task_ref, slot_ref, found):
    seg_a, _, seg_b, _ = found
    return slot_ref[task_ref[0, seg_a]], slot_ref[task_ref[0, seg_b]]


def pick_kernel(shard_len, offsets, len_ref, task_ref, slot_ref, bank_ref, *out_refs):
    grp_count = lax.axis_size("grp")
    me = lax.axis_index("grp")
    row_base = lax.axis_index("ctx") * grp_count
    held = bank_ref.shape[1]
    firsts = [(row_base + (me ^ k)) * shard_len for k in offsets]
    for out_ref, found in zip(out_refs, shard_segments(len_ref, firsts, shard_len)):
        for slot, row in enumerate(bank_rows(task_ref, slot_ref, found)):
            local = jnp.clip(row - me * held, 0, held - 1)
            for kind in range(2):
                out_ref[slot, kind] = bank_ref[kind, local]


def attend(q_ref, head, groups, keys, values, masks):
    t = q_ref.shape[1]
    cols = [q_ref[0, :, pl.ds((head * groups + g) * HD, HD)] for g in range(groups)]
    eye = (
        lax.broadcasted_iota(jnp.int32, (t, t), 0) == lax.broadcasted_iota(jnp.int32, (t, t), 1)
    ).astype(jnp.float32).astype(jnp.bfloat16)
    q = jnp.concatenate(cols, axis=0)
    q = jnp.concatenate([q, jnp.concatenate([eye] * groups, axis=0)], axis=1)
    k = jnp.concatenate([keys, masks], axis=1)
    s = lax.dot_general(q, k, (((1,), (1,)), ((), ())), preferred_element_type=jnp.float32)
    top = jnp.max(s, axis=1, keepdims=True)
    w = jnp.exp2((s - top) * (math.log2(math.e) / math.sqrt(HD))).astype(jnp.bfloat16)
    v = jnp.concatenate([values, jnp.ones(values.shape, jnp.bfloat16)], axis=1)
    o = jnp.dot(w, v, preferred_element_type=jnp.float32)
    return top, o[:, :HD], o[:, HD:]


def block_mask(first, hop, start_a, start_b, shard_len):
    shape = (shard_len, shard_len)
    key = lax.broadcasted_iota(jnp.int32, shape, 0) - hop * shard_len
    query = lax.broadcasted_iota(jnp.int32, shape, 1)
    from_b = start_b - first
    start = jnp.where(query >= from_b, from_b, start_a - first)
    allowed = (key >= start) & (key <= query)
    return jnp.where(allowed, 0.0, FAR).astype(jnp.bfloat16)


def hop_of(kind, grp_count):
    me = lax.axis_index("grp")
    if kind[0] == "shift":
        return kind[1]
    return (me - (me ^ kind[1])) & (grp_count - 1)


def early_kernel(kinds, groups, len_ref, q_ref, *refs):
    kv_refs = refs[: len(kinds)]
    acc_ref, sum_ref, top_ref = refs[len(kinds) :]
    t = q_ref.shape[1]
    kv_heads = kv_refs[0].shape[-1] // HD
    grp_count = lax.axis_size("grp")
    first = (lax.axis_index("ctx") * grp_count + lax.axis_index("grp")) * t
    (_, start_a, _, start_b), = shard_segments(len_ref, [first], t)
    masks = jnp.concatenate(
        [block_mask(first, hop_of(kind, grp_count), start_a, start_b, t) for kind in kinds], axis=0
    )
    for head in range(kv_heads):
        lanes = pl.ds(head * HD, HD)
        keys = jnp.concatenate([r[0, 0, :, lanes] for r in kv_refs], axis=0)
        values = jnp.concatenate([r[1, 0, :, lanes] for r in kv_refs], axis=0)
        top, acc, total = attend(q_ref, head, groups, keys, values, masks)
        for g in range(groups):
            rows = slice(g * t, (g + 1) * t)
            out = pl.ds((head * groups + g) * HD, HD)
            acc_ref[:, out] = acc[rows]
            sum_ref[:, out] = total[rows]
            top_ref[:, out] = jnp.broadcast_to(top[rows], (t, HD))


def late_kernel(kind, groups, len_ref, task_ref, slot_ref, q_ref, k_ref, v_ref, *refs):
    prefix_refs = refs[:-4]
    acc_ref, sum_ref, top_ref, out_ref = refs[-4:]
    t = q_ref.shape[1]
    kv_heads = k_ref.shape[-1] // HD
    grp_count = lax.axis_size("grp")
    me = lax.axis_index("grp")
    first = (lax.axis_index("ctx") * grp_count + me) * t
    found, = shard_segments(len_ref, [first], t)
    _, start_a, _, start_b = found
    prefix_len, width = prefix_refs[0].shape[2:]
    held = slot_ref.shape[0] // grp_count
    picked = []
    for slot, row in enumerate(bank_rows(task_ref, slot_ref, found)):
        pair = []
        for part in range(2):
            if len(prefix_refs) == 1:
                pair.append(prefix_refs[0][slot, part])
                continue
            place = (row // held) ^ me
            value = prefix_refs[0][slot, part]
            for k in range(1, len(prefix_refs)):
                value = jnp.where(place == k, prefix_refs[k][slot, part], value)
            pair.append(value)
        picked.append(pair)
    shape = (prefix_len, t)
    is_b = lax.broadcasted_iota(jnp.int32, shape, 1) >= start_b - first
    mask_a = jnp.where(is_b, FAR, 0.0).astype(jnp.bfloat16)
    mask_b = jnp.where(is_b, 0.0, FAR).astype(jnp.bfloat16)
    masks = jnp.concatenate(
        [block_mask(first, hop_of(kind, grp_count), start_a, start_b, t), mask_a, mask_b], axis=0
    )
    scale = math.log2(math.e) / math.sqrt(HD)
    for head in range(kv_heads):
        lanes = pl.ds(head * HD, HD)
        cut = slice(head * HD, (head + 1) * HD)
        keys = jnp.concatenate([k_ref[0, 0, :, lanes]] + [p[0][:, cut] for p in picked], axis=0)
        values = jnp.concatenate([v_ref[0, 0, :, lanes]] + [p[1][:, cut] for p in picked], axis=0)
        top, acc, total = attend(q_ref, head, groups, keys, values, masks)
        for g in range(groups):
            rows = slice(g * t, (g + 1) * t)
            at = pl.ds((head * groups + g) * HD, HD)
            old = top_ref[:, at]
            new = jnp.broadcast_to(top[rows], (t, HD))
            best = jnp.maximum(old, new)
            keep = jnp.exp2((old - best) * scale)
            take = jnp.exp2((new - best) * scale)
            mixed = acc_ref[:, at] * keep + acc[rows] * take
            out_ref[0, :, at] = (mixed / (sum_ref[:, at] * keep + total[rows] * take)).astype(
                out_ref.dtype
            )


def on_device(queries, keyvals, seg_len, seg_task, task_slot, prefix_bank):
    ctx_count, grp_count = (lax.axis_size(a) for a in AXES)
    count = ctx_count * grp_count
    t = queries.shape[1]
    groups = queries.shape[2] // keyvals.shape[3]
    prefix_shape = (2, 2) + prefix_bank.shape[2:]
    plane = grp_count == HOPS + 1

    if plane:
        kinds = [("flip", k) for k in (1, 2, 3)]
        near, side, far = (flip_route(ctx_count, grp_count, k) for k in (1, 2, 3))
        got_near = lax.ppermute(keyvals, AXES, near)
        got_side = lax.ppermute(keyvals, AXES, side)
        far_keys = lax.ppermute(got_side[0:1], AXES, compose_route(far, side))
        far_values = lax.ppermute(got_near[1:2], AXES, compose_route(far, near))
        offsets = range(grp_count)
        prefix = pl.pallas_call(
            functools.partial(pick_kernel, t, offsets),
            out_shape=[jax.ShapeDtypeStruct(prefix_shape, prefix_bank.dtype)] * grp_count,
            in_specs=[SMEM] * 3 + [VMEM],
            out_specs=[VMEM] * grp_count,
            compiler_params=PARAMS,
            name="pick_prefix",
        )(seg_len, seg_task, task_slot, prefix_bank)
        prefix = [prefix[0]] + [
            lax.ppermute(prefix[k], "grp", [(i, i ^ k) for i in range(grp_count)])
            for k in offsets[1:]
        ]
    else:
        kinds = [("shift", d) for d in range(1, HOPS + 1)]
        got_near, got_side, got_far = (
            lax.ppermute(keyvals, AXES, shift_route(count, d)) for d in range(1, HOPS + 1)
        )
        far_keys, far_values = got_far[0:1], got_far[1:2]
        prefix = [fetch_prefix(seg_len, seg_task, task_slot, prefix_bank, t)]

    wide = jax.ShapeDtypeStruct(queries.shape[1:], jnp.float32)
    early = [("shift", 0)] + kinds[:2]
    cost = 2 * 2 * queries.size * t
    state = pl.pallas_call(
        functools.partial(early_kernel, early, groups),
        out_shape=[wide] * 3,
        in_specs=[SMEM] + [VMEM] * 4,
        out_specs=[VMEM] * 3,
        compiler_params=PARAMS,
        cost_estimate=pl.CostEstimate(
            flops=3 * cost, bytes_accessed=2 * queries.size, transcendentals=3 * queries.size
        ),
        name="attend_near",
    )(seg_len, queries, keyvals, got_near, got_side)
    return pl.pallas_call(
        functools.partial(late_kernel, kinds[2], groups),
        out_shape=jax.ShapeDtypeStruct(queries.shape, queries.dtype),
        in_specs=[SMEM] * 3 + [VMEM] * (6 + len(prefix)),
        out_specs=VMEM,
        compiler_params=PARAMS,
        cost_estimate=pl.CostEstimate(
            flops=cost, bytes_accessed=4 * queries.size, transcendentals=queries.size
        ),
        name="attend_far",
    )(seg_len, seg_task, task_slot, queries, far_keys, far_values, *prefix, *state)


def fetch_prefix(seg_len, seg_task, task_slot, prefix_bank, t):
    grp_count = lax.axis_size("grp")
    me = lax.axis_index("grp")
    held = prefix_bank.shape[1]
    starts = jnp.cumsum(seg_len[0]) - seg_len[0]
    shards = lax.axis_index("ctx") * grp_count + jnp.arange(grp_count, dtype=jnp.int32)
    ends = shards[:, None] * t + jnp.array([0, t - 1], jnp.int32)
    segs = jnp.sum((starts[None, None, :] <= ends[:, :, None]).astype(jnp.int32), axis=2) - 1
    rows = task_slot[seg_task[0][segs]]
    local = jnp.clip(rows - me * held, 0, held - 1)
    pieces = jnp.swapaxes(prefix_bank, 0, 1)[local]
    got = lax.all_to_all(pieces, "grp", split_axis=0, concat_axis=0, tiled=True)
    owner = rows[me] // held
    return jnp.stack([got[owner[s], s] for s in range(2)])


def solution(mesh):
    in_specs = (
        P(None, AXES, None),
        P(None, None, AXES, None),
        P(),
        P(),
        P(),
        P(None, "grp", None, None),
    )
    return jax.shard_map(
        on_device, mesh=mesh, in_specs=in_specs, out_specs=P(None, AXES, None), check_vma=False
    )
```

time: 55.8 us -> 31.6 us (0.57)
  other arithmetic: 10.1 us -> 0 us
  matrix products: 8.86 us -> 0 us
  Pallas kernels: 0 us -> 8.41 us
  starting transfers between devices: 19 us -> 12.4 us
  local copies, waits for them, and re-layouts: 10.6 us -> 5.09 us
  between operations: 2.35 us -> 0.1 us
  waiting for transfers between devices: 4.23 us -> 5.37 us
    dot_general x11 -> x0, matrix products: 8.86 us -> none  [the longest x5 4.45 us: attend(): jnp.einsum('tkgd,skd->kgts', grouped_q, key_heads, preferred_element_type...]
    pallas_call x0 -> x3, Pallas kernels: none -> 8.41 us  [the longest x1 4.02 us: on_device(): pl.pallas_call(functools.partial(late_kernel, kinds[2], groups), out_shap...]
    all_to_all x2 -> x0, starting transfers between devices: 7.43 us -> none  [the longest x1 4.19 us: on_device(): lax.all_to_all(bank_rows, 'grp', split_axis=0, concat_axis=0, tiled=True)]
    ppermute x3 -> x7, waiting for transfers between devices: 0.01 us -> 5.37 us  [the longest x1 5.36 us: on_device(): got_side = lax.ppermute(keyvals, AXES, side)]
    slice x7 -> x2, local copies, waits for them, and re-layouts: 4.74 us -> 0.02 us  [the longest x1 0.01 us: on_device(): far_values = lax.ppermute(got_near[1:2], AXES, compose_route(far, near))]
    reduce_sum x9 -> x0, other arithmetic: 4.57 us -> none  [the longest x5 2.02 us: attend(): total_new = total_old * shrink + jnp.sum(weights, axis=-1)]
    all_to_all x2 -> x0, waiting for transfers between devices: 4.22 us -> none  [the longest x1 4.22 us: on_device(): lax.all_to_all(bank_rows, 'grp', split_axis=0, concat_axis=0, tiled=True)]
    convert_element_type x2 -> x0, local copies, waits for them, and re-layouts: 2.07 us -> none  [the longest x1 1.31 us: on_device(): result.transpose(2, 0, 1, 3).reshape(1, shard_len, H * HD)]
  transfers between devices with their start and end apart: 5 -> 7, of which waited for: 1 -> 1; matrix products, arithmetic and copies ran while one was open for 35% -> 0% of each run, Pallas kernels for 0% -> 14%
where the time goes in v1:
time: 31.6 us; the launch traced here: 31.3 us
  starting transfers between devices  12.4 us (39%)
  Pallas kernels  8.41 us (27%)
  waiting for transfers between devices  5.37 us (17%)
  local copies, waits for them, and re-layouts  5.09 us (16%)
    ppermute x1, waiting for transfers between devices, on_device(): got_side = lax.ppermute(keyvals, AXES, side)  5.36 us
    unnamed x18, local copies, waits for them, and re-layouts  5.08 us
    pallas_call x1, Pallas kernels, on_device(): pl.pallas_call(functools.partial(late_kernel, kinds[2], groups), out_shap...  4.02 us
    pallas_call x1, Pallas kernels, on_device(): pl.pallas_call(functools.partial(early_kernel, early, groups), out_shape=...  3.56 us
    ppermute x3, starting transfers between devices, on_device(): lax.ppermute(prefix[k], 'grp', [(i, i ^ k) for i in range(grp_count)])  3.55 us
    ppermute x1, starting transfers between devices, on_device(): got_side = lax.ppermute(keyvals, AXES, side)  2.97 us
    ppermute x1, starting transfers between devices, on_device(): far_values = lax.ppermute(got_near[1:2], AXES, compose_route(far, near))  2.35 us
    ppermute x1, starting transfers between devices, on_device(): far_keys = lax.ppermute(got_side[0:1], AXES, compose_route(far, side))  2 us
  transfers between devices with their start and end apart: 7, of which 1 were waited for; matrix products, arithmetic and copies ran while one was open for 0% of the time, Pallas kernels for 14%

profile of v1, /device:TPU:0, one launch (start us, length us, event | category | flops | bytes accessed | tf_op | source)
XLA Modules:
  0.0 31.3 jit_solution(6316512951835857011)
XLA Ops:
  0.0 0.0 copy-start.7
  0.0 0.0 copy-start.5
  0.0 3.0 %collective-permute-start = (bf16[2,1,128,512]{3,2,1,0:T(8,128)(2,1)}, bf16[2,1,128,512]{3,2,1,0:T(8,128)(2,1)S(1)}, u32[]{:S(2)}, u32[]{:S(2)}) collective-permute-start(bf16[2,1,128,512]{3,2,1,0:T(8,128)(2,1)} %refs_0_.1), channel_id=1, source_target_pairs={{0,2},{1,3},{2,4},{3,5},{4,6},{5,7},{6,8},{7,9},{8,10},{9,11},{10,... | collective-permute-start | bytes 786440 | tf_op jit(solution)/shard_map/ppermute | solution.py:202
  3.0 1.5 %collective-permute-start.2 = (bf16[2,1,128,512]{3,2,1,0:T(8,128)(2,1)}, bf16[2,1,128,512]{3,2,1,0:T(8,128)(2,1)S(1)}, u32[]{:S(2)}, u32[]{:S(2)}) collective-permute-start(bf16[2,1,128,512]{3,2,1,0:T(8,128)(2,1)} %refs_0_.1), channel_id=1, source_target_pairs={{0,1},{1,4},{2,3},{3,6},{4,5},{5,8},{6,7},{7,10},{8,9},{9,12},{10,... | collective-permute-start | bytes 786440 | tf_op jit(solution)/shard_map/ppermute | solution.py:201
  4.5 5.4 %collective-permute-done.refs_2_ = bf16[2,1,128,512]{3,2,1,0:T(8,128)(2,1)S(1)} collective-permute-done((bf16[2,1,128,512]{3,2,1,0:T(8,128)(2,1)}, bf16[2,1,128,512]{3,2,1,0:T(8,128)(2,1)S(1)}, u32[]{:S(2)}, u32[]{:S(2)}) %collective-permute-start) | collective-permute-done | bytes 262176 | tf_op jit(solution)/shard_map/ppermute | solution.py:202
  9.8 2.0 %collective-permute-start.1 = (bf16[1,1,128,512]{3,2,1,0:T(8,128)(2,1)S(1)}, bf16[1,1,128,512]{3,2,1,0:T(8,128)(2,1)S(1)}, u32[]{:S(2)}, u32[]{:S(2)}) collective-permute-start(bf16[1,1,128,512]{3,2,1,0:T(8,128)(2,1)S(1)} %slice.8), channel_id=1, source_target_pairs={{2,3},{3,2},{4,5},{5,4},{6,7},{7,6},{8,9},{9,8},{10,11},{11,10},{1... | collective-permute-start | bytes 393224 | tf_op jit(solution)/shard_map/ppermute | solution.py:203
  11.8 0.0 collective-permute-done.2.refs_1_
  11.9 2.4 %collective-permute-start.3 = (bf16[1,1,128,512]{3,2,1,0:T(8,128)(2,1)S(1)}, bf16[1,1,128,512]{3,2,1,0:T(8,128)(2,1)S(1)}, u32[]{:S(2)}, u32[]{:S(2)}) collective-permute-start(bf16[1,1,128,512]{3,2,1,0:T(8,128)(2,1)S(1)} %slice.9), channel_id=1, source_target_pairs={{1,3},{4,2},{3,5},{6,4},{5,7},{8,6},{7,9},{10,8},{9,11},{12,10},{1... | collective-permute-start | bytes 393224 | tf_op jit(solution)/shard_map/ppermute | solution.py:204
  14.2 0.0 copy-start.2
  14.2 0.9 %copy-done.2 = bf16[2,6,16,512]{3,2,1,0:T(8,128)(2,1)S(1)} copy-done((bf16[2,6,16,512]{3,2,1,0:T(8,128)(2,1)S(1)}, bf16[2,6,16,512]{3,2,1,0:T(8,128)(2,1)}, u32[]{:S(2)}) %copy-start.2) | copy-done | bytes 196632
  15.1 0.0 copy-start.3
  15.1 0.7 %copy-done.3 = s32[1,16]{1,0:T(1,128)S(1)} copy-done((s32[1,16]{1,0:T(1,128)S(1)}, s32[1,16]{1,0:T(1,128)}, u32[]{:S(2)}) %copy-start.3) | copy-done | bytes 88
  15.8 0.0 copy-start.4
  15.8 0.7 %copy-done.4 = s32[1,16]{1,0:T(1,128)S(1)} copy-done((s32[1,16]{1,0:T(1,128)S(1)}, s32[1,16]{1,0:T(1,128)}, u32[]{:S(2)}) %copy-start.4) | copy-done | bytes 88
  16.4 0.0 copy-start.6
  16.4 0.7 %copy-done.6 = s32[24]{0:T(128)S(1)} copy-done((s32[24]{0:T(128)S(1)}, s32[24]{0:T(128)}, u32[]{:S(2)}) %copy-start.6) | copy-done | bytes 120
  17.1 0.8 %pick_prefix.1 = (bf16[2,2,16,512]{3,2,1,0:T(8,128)(2,1)S(1)}, bf16[2,2,16,512]{3,2,1,0:T(8,128)(2,1)S(1)}, bf16[2,2,16,512]{3,2,1,0:T(8,128)(2,1)S(1)}, bf16[2,2,16,512]{3,2,1,0:T(8,128)(2,1)S(1)}) custom-call(s32[1,16]{1,0:T(1,128)S(1)} %copy-done.3, s32[1,16]{1,0:T(1,128)S(1)} %copy-done.4, s32[24]{0:T(128)S(1)} %copy-done.6, ...), custom_call_target="tpu_custom_call" | custom-call | tf_op jit(solution)/shard_map/pick_prefix/pallas_call | solution.py:206
  17.9 0.1 collective-permute-start.4
  18.0 0.6 %collective-permute-start.5 = (bf16[2,2,16,512]{3,2,1,0:T(8,128)(2,1)S(1)}, bf16[2,2,16,512]{3,2,1,0:T(8,128)(2,1)S(1)}, u32[]{:S(2)}, u32[]{:S(2)}) collective-permute-start(bf16[2,2,16,512]{3,2,1,0:T(8,128)(2,1)S(1)} %get-tuple-element.14), channel_id=1, source_target_pairs={{0,2},{1,3},{2,0},{3,1},{4,6},{5,7},{6,4},{7,5},{8,10},{9,11},{10,... | collective-permute-start | bytes 196616 | tf_op jit(solution)/shard_map/ppermute | solution.py:215
  18.6 2.9 %collective-permute-start.6 = (bf16[2,2,16,512]{3,2,1,0:T(8,128)(2,1)S(1)}, bf16[2,2,16,512]{3,2,1,0:T(8,128)(2,1)S(1)}, u32[]{:S(2)}, u32[]{:S(2)}) collective-permute-start(bf16[2,2,16,512]{3,2,1,0:T(8,128)(2,1)S(1)} %get-tuple-element.15), channel_id=1, source_target_pairs={{0,3},{1,2},{2,1},{3,0},{4,7},{5,6},{6,5},{7,4},{8,11},{9,10},{10,... | collective-permute-start | bytes 196616 | tf_op jit(solution)/shard_map/ppermute | solution.py:215
  21.5 0.0 copy-start
  21.5 1.2 %copy-done = bf16[1,128,4096]{2,1,0:T(8,128)(2,1)S(1)} copy-done((bf16[1,128,4096]{2,1,0:T(8,128)(2,1)S(1)}, bf16[1,128,4096]{2,1,0:T(8,128)(2,1)}, u32[]{:S(2)}) %copy-start) | copy-done | bytes 1048600
  22.7 0.0 copy-start.8
  22.7 0.9 %copy-done.8 = bf16[2,1,128,512]{3,2,1,0:T(8,128)(2,1)S(1)} copy-done((bf16[2,1,128,512]{3,2,1,0:T(8,128)(2,1)S(1)}, bf16[2,1,128,512]{3,2,1,0:T(8,128)(2,1)}, u32[]{:S(2)}) %copy-start.8) | copy-done | bytes 262168
  23.7 0.0 copy-start.1
  23.7 3.6 %attend_near.1 = (f32[128,4096]{1,0:T(8,128)S(1)}, f32[128,4096]{1,0:T(8,128)S(1)}, f32[128,4096]{1,0:T(8,128)S(1)}) custom-call(s32[1,16]{1,0:T(1,128)S(1)} %copy-done.3, bf16[1,128,4096]{2,1,0:T(8,128)(2,1)S(1)} %copy-done, bf16[2,1,128,512]{3,2,1,0:T(8,128)(2,1)S(1)} %copy-done.8, bf16[2,1,128,512]{3,2,1,0:T(8,128)(2,1)S(1)} %collective-permute-done.2.refs_1_, ...), custom_call_target="tpu_custom_call" | custom-call | flops 805306368 | bytes 1048576 | tf_op jit(solution)/shard_map/attend_near/pallas_call | solution.py:229
  27.2 0.0 collective-permute-done.4.refs_1_
  27.2 0.0 collective-permute-done.5.refs_2_
  27.2 0.0 collective-permute-done.6.refs_3_
  27.3 0.0 collective-permute-done.1.k_ref
  27.3 0.0 collective-permute-done.3.v_ref
  27.3 0.0 copy-done.7
  27.3 0.0 copy-done.5
  27.3 0.0 copy-done.1
  27.3 4.0 %attend_far.1 = bf16[1,128,4096]{2,1,0:T(8,128)(2,1)} custom-call(s32[1,16]{1,0:T(1,128)S(1)} %copy-done.3, s32[1,16]{1,0:T(1,128)S(1)} %copy-done.5, s32[24]{0:T(128)S(1)} %copy-done.7, bf16[1,128,4096]{2,1,0:T(8,128)(2,1)S(1)} %copy-done.1, bf16[1,1,128,512]{3,2,1,0:T(8,128)(2,1)S(1)} %collective-permute-done.1.k_ref, ...), custom_call_target="tpu_custom_call" | custom-call | flops 268435456 | bytes 2097152 | tf_op jit(solution)/shard_map/attend_far/pallas_call | solution.py:240
  (2 shorter events, 0.0 us)
Async XLA Ops:
  0.0 27.3 %copy-start.7 = (s32[24]{0:T(128)S(1)}, s32[24]{0:T(128)}, u32[]{:S(2)}) copy-start(s32[24]{0:T(128)} %slot_ref.3) | copy-start | bytes 292
  0.0 27.3 %copy-start.5 = (s32[1,16]{1,0:T(1,128)S(1)}, s32[1,16]{1,0:T(1,128)}, u32[]{:S(2)}) copy-start(s32[1,16]{1,0:T(1,128)} %task_ref.3) | copy-start | bytes 196
  0.0 9.8 %collective-permute-start = (bf16[2,1,128,512]{3,2,1,0:T(8,128)(2,1)}, bf16[2,1,128,512]{3,2,1,0:T(8,128)(2,1)S(1)}, u32[]{:S(2)}, u32[]{:S(2)}) collective-permute-start(bf16[2,1,128,512]{3,2,1,0:T(8,128)(2,1)} %refs_0_.1), channel_id=1, source_target_pairs={{0,2},{1,3},{2,4},{3,5},{4,6},{5,7},{6,8},{7,9},{8,10},{9,11},{10,... | collective-permute-start | bytes 786440 | tf_op jit(solution)/shard_map/ppermute | solution.py:202
  3.0 8.9 %collective-permute-start.2 = (bf16[2,1,128,512]{3,2,1,0:T(8,128)(2,1)}, bf16[2,1,128,512]{3,2,1,0:T(8,128)(2,1)S(1)}, u32[]{:S(2)}, u32[]{:S(2)}) collective-permute-start(bf16[2,1,128,512]{3,2,1,0:T(8,128)(2,1)} %refs_0_.1), channel_id=1, source_target_pairs={{0,1},{1,4},{2,3},{3,6},{4,5},{5,8},{6,7},{7,10},{8,9},{9,12},{10,... | collective-permute-start | bytes 786440 | tf_op jit(solution)/shard_map/ppermute | solution.py:201
  9.8 17.4 %collective-permute-start.1 = (bf16[1,1,128,512]{3,2,1,0:T(8,128)(2,1)S(1)}, bf16[1,1,128,512]{3,2,1,0:T(8,128)(2,1)S(1)}, u32[]{:S(2)}, u32[]{:S(2)}) collective-permute-start(bf16[1,1,128,512]{3,2,1,0:T(8,128)(2,1)S(1)} %slice.8), channel_id=1, source_target_pairs={{2,3},{3,2},{4,5},{5,4},{6,7},{7,6},{8,9},{9,8},{10,11},{11,10},{1... | collective-permute-start | bytes 393224 | tf_op jit(solution)/shard_map/ppermute | solution.py:203
  11.9 15.4 %collective-permute-start.3 = (bf16[1,1,128,512]{3,2,1,0:T(8,128)(2,1)S(1)}, bf16[1,1,128,512]{3,2,1,0:T(8,128)(2,1)S(1)}, u32[]{:S(2)}, u32[]{:S(2)}) collective-permute-start(bf16[1,1,128,512]{3,2,1,0:T(8,128)(2,1)S(1)} %slice.9), channel_id=1, source_target_pairs={{1,3},{4,2},{3,5},{6,4},{5,7},{8,6},{7,9},{10,8},{9,11},{12,10},{1... | collective-permute-start | bytes 393224 | tf_op jit(solution)/shard_map/ppermute | solution.py:204
  14.2 0.9 %copy-start.2 = (bf16[2,6,16,512]{3,2,1,0:T(8,128)(2,1)S(1)}, bf16[2,6,16,512]{3,2,1,0:T(8,128)(2,1)}, u32[]{:S(2)}) copy-start(bf16[2,6,16,512]{3,2,1,0:T(8,128)(2,1)} %bank_ref.1) | copy-start | bytes 589828
  15.1 0.7 %copy-start.3 = (s32[1,16]{1,0:T(1,128)S(1)}, s32[1,16]{1,0:T(1,128)}, u32[]{:S(2)}) copy-start(s32[1,16]{1,0:T(1,128)} %len_ref.5) | copy-start | bytes 196
  15.8 0.7 %copy-start.4 = (s32[1,16]{1,0:T(1,128)S(1)}, s32[1,16]{1,0:T(1,128)}, u32[]{:S(2)}) copy-start(s32[1,16]{1,0:T(1,128)} %task_ref.3) | copy-start | bytes 196
  16.4 0.7 %copy-start.6 = (s32[24]{0:T(128)S(1)}, s32[24]{0:T(128)}, u32[]{:S(2)}) copy-start(s32[24]{0:T(128)} %slot_ref.3) | copy-start | bytes 292
  17.9 9.3 %collective-permute-start.4 = (bf16[2,2,16,512]{3,2,1,0:T(8,128)(2,1)S(1)}, bf16[2,2,16,512]{3,2,1,0:T(8,128)(2,1)S(1)}, u32[]{:S(2)}, u32[]{:S(2)}) collective-permute-start(bf16[2,2,16,512]{3,2,1,0:T(8,128)(2,1)S(1)} %get-tuple-element.13), channel_id=1, source_target_pairs={{0,1},{1,0},{2,3},{3,2},{4,5},{5,4},{6,7},{7,6},{8,9},{9,8},{10,11... | collective-permute-start | bytes 196616 | tf_op jit(solution)/shard_map/ppermute | solution.py:215
  18.0 9.2 %collective-permute-start.5 = (bf16[2,2,16,512]{3,2,1,0:T(8,128)(2,1)S(1)}, bf16[2,2,16,512]{3,2,1,0:T(8,128)(2,1)S(1)}, u32[]{:S(2)}, u32[]{:S(2)}) collective-permute-start(bf16[2,2,16,512]{3,2,1,0:T(8,128)(2,1)S(1)} %get-tuple-element.14), channel_id=1, source_target_pairs={{0,2},{1,3},{2,0},{3,1},{4,6},{5,7},{6,4},{7,5},{8,10},{9,11},{10,... | collective-permute-start | bytes 196616 | tf_op jit(solution)/shard_map/ppermute | solution.py:215
  18.6 8.7 %collective-permute-start.6 = (bf16[2,2,16,512]{3,2,1,0:T(8,128)(2,1)S(1)}, bf16[2,2,16,512]{3,2,1,0:T(8,128)(2,1)S(1)}, u32[]{:S(2)}, u32[]{:S(2)}) collective-permute-start(bf16[2,2,16,512]{3,2,1,0:T(8,128)(2,1)S(1)} %get-tuple-element.15), channel_id=1, source_target_pairs={{0,3},{1,2},{2,1},{3,0},{4,7},{5,6},{6,5},{7,4},{8,11},{9,10},{10,... | collective-permute-start | bytes 196616 | tf_op jit(solution)/shard_map/ppermute | solution.py:215
  21.5 1.2 %copy-start = (bf16[1,128,4096]{2,1,0:T(8,128)(2,1)S(1)}, bf16[1,128,4096]{2,1,0:T(8,128)(2,1)}, u32[]{:S(2)}) copy-start(bf16[1,128,4096]{2,1,0:T(8,128)(2,1)} %q_ref.3) | copy-start | bytes 3145732
  22.7 0.9 %copy-start.8 = (bf16[2,1,128,512]{3,2,1,0:T(8,128)(2,1)S(1)}, bf16[2,1,128,512]{3,2,1,0:T(8,128)(2,1)}, u32[]{:S(2)}) copy-start(bf16[2,1,128,512]{3,2,1,0:T(8,128)(2,1)} %refs_0_.1) | copy-start | bytes 786436
  23.7 3.6 %copy-start.1 = (bf16[1,128,4096]{2,1,0:T(8,128)(2,1)S(1)}, bf16[1,128,4096]{2,1,0:T(8,128)(2,1)}, u32[]{:S(2)}) copy-start(bf16[1,128,4096]{2,1,0:T(8,128)(2,1)} %q_ref.3) | copy-start | bytes 3145732

commit v2 on v1

v2 whole, which is shorter than its diff:
```python
import functools
import math

import jax
import jax.numpy as jnp
from jax import lax
from jax.experimental import pallas as pl
from jax.experimental.pallas import tpu as pltpu
from jax.sharding import PartitionSpec as P

HD = 128
HOPS = 3
FAR = -1e30
AXES = ("ctx", "grp")
VMEM = pl.BlockSpec(memory_space=pltpu.VMEM)
HBM = pl.BlockSpec(memory_space=pltpu.HBM)
SCALE = math.log2(math.e) / math.sqrt(HD)
PARAMS = pltpu.CompilerParams(vmem_limit_bytes=40 * 2**20)


def shift_route(count, distance):
    return [(i, (i + distance) % count) for i in range(count)]


def flip_route(ctx_count, grp_count, flip):
    count = ctx_count * grp_count
    return [
        (i, (i + ((i % grp_count ^ flip) - i % grp_count) % grp_count) % count)
        for i in range(count)
    ]


def compose_route(wanted, first):
    holder = dict(first)
    return [(holder[s], d) for s, d in wanted]


def shard_segments(len_ref, firsts, shard_len):
    def step(s, carry):
        start, found = carry
        out = []
        for first, (seg_a, start_a, seg_b, start_b) in zip(firsts, found):
            in_a = start <= first
            in_b = start <= first + (shard_len - 1)
            out.append(
                (
                    jnp.where(in_a, s, seg_a),
                    jnp.where(in_a, start, start_a),
                    jnp.where(in_b, s, seg_b),
                    jnp.where(in_b, start, start_b),
                )
            )
        return start + len_ref[0, s], out

    zero = jnp.int32(0)
    _, found = lax.fori_loop(
        0, len_ref.shape[1], step, (zero, [(zero, zero, zero, zero)] * len(firsts))
    )
    return found


def bank_rows(task_ref, slot_ref, found):
    seg_a, _, seg_b, _ = found
    return slot_ref[task_ref[0, seg_a]], slot_ref[task_ref[0, seg_b]]


def block_mask(first, hop, start_a, start_b, t):
    key = lax.broadcasted_iota(jnp.int32, (t, t), 0) - hop * t
    query = lax.broadcasted_iota(jnp.int32, (t, t), 1)
    from_b = start_b - first
    start = jnp.where(query >= from_b, from_b, start_a - first)
    return jnp.where((key >= start) & (key <= query), 0.0, FAR).astype(jnp.bfloat16)


def hop_of(kind, grp_count):
    me = lax.axis_index("grp")
    if kind[0] == "shift":
        return kind[1]
    return (me - (me ^ kind[1])) & (grp_count - 1)


def plan_kernel(t, kinds, sends, len_hbm, task_hbm, slot_hbm, bank_hbm, *refs):
    mask_ref, place_ref, out_refs = refs[0], refs[1], refs[2 : 2 + len(sends)]
    len_ref, task_ref, slot_ref, bank_ref, sems = refs[2 + len(sends) :]
    pairs = ((len_hbm, len_ref), (task_hbm, task_ref), (slot_hbm, slot_ref), (bank_hbm, bank_ref))
    copies = [pltpu.make_async_copy(a, b, sems.at[i]) for i, (a, b) in enumerate(pairs)]
    for copy in copies:
        copy.start()
    for copy in copies[:3]:
        copy.wait()
    grp_count = lax.axis_size("grp")
    me = lax.axis_index("grp")
    row_base = lax.axis_index("ctx") * grp_count
    held = bank_ref.shape[1]
    shards = [row_base + me] + [row_base + (me ^ k) for k in sends[1:]]
    found = shard_segments(len_ref, [s * t for s in shards], t)
    first = shards[0] * t
    _, start_a, _, start_b = found[0]
    size = bank_ref.shape[2]
    is_b = lax.broadcasted_iota(jnp.int32, (size, t), 1) >= start_b - first
    blocks = [block_mask(first, hop_of(k, grp_count), start_a, start_b, t) for k in kinds]
    blocks[-1:-1] = [jnp.where(is_b, a, b).astype(jnp.bfloat16) for a, b in ((FAR, 0.0), (0.0, FAR))]
    mask_ref[...] = jnp.concatenate(blocks, axis=0)
    rows = [bank_rows(task_ref, slot_ref, f) for f in found]
    for slot, row in enumerate(rows[0]):
        place_ref[slot] = jnp.full(place_ref.shape[1:], (row // held) ^ me, jnp.int32)
    copies[3].wait()
    for out_ref, pair in zip(out_refs, rows):
        for slot, row in enumerate(pair):
            local = jnp.clip(row - me * held, 0, held - 1)
            for part in range(2):
                out_ref[slot, part] = bank_ref[part, local]


def eye(t):
    a, b = (lax.broadcasted_iota(jnp.int32, (t, t), i) for i in range(2))
    return (a == b).astype(jnp.float32).astype(jnp.bfloat16)


def staged(count, score, weigh, mix):
    scores, weights = {}, {}
    for i in range(count + 2):
        if i < count:
            scores[i] = score(i)
        if 0 <= i - 1 < count:
            weights[i - 1] = weigh(i - 1, scores.pop(i - 1))
        if 0 <= i - 2 < count:
            mix(i - 2, weights.pop(i - 2))


def score(keys, masks, q, ones):
    return jnp.dot(
        jnp.concatenate([keys, masks], axis=1),
        jnp.concatenate([q, ones], axis=0),
        preferred_element_type=jnp.float32,
    )


def mix(values, weights):
    v = jnp.concatenate([values.T, jnp.ones((16, values.shape[0]), jnp.bfloat16)], axis=0)
    return jnp.dot(v, weights, preferred_element_type=jnp.float32)


def pick_prefix(place_ref, prefix_refs):
    picked = [[], []]
    for part in range(2):
        for slot in range(2):
            value = prefix_refs[0][slot, part]
            for k in range(1, len(prefix_refs)):
                here = jnp.broadcast_to(place_ref[slot][:1, :1] == k, value.shape)
                value = jnp.where(here, prefix_refs[k][slot, part], value)
            picked[part].append(value)
    return picked


def near_kernel(groups, sends, mask_ref, place_ref, q_hbm, own_hbm, *refs):
    prefix_refs, kv_refs = refs[:sends], refs[sends:-8]
    qt_ref, acc_ref, sum_ref, top_ref, q_ref, own_ref, q_sems, own_sem = refs[-8:]
    own_copy = pltpu.make_async_copy(own_hbm, own_ref, own_sem)
    own_copy.start()
    q_copies = []
    for j in range(acc_ref.shape[0]):
        cols = pl.ds(j * groups * HD, groups * HD)
        q_copies.append(
            pltpu.make_async_copy(q_hbm.at[:, :, cols], q_ref.at[:, :, cols], q_sems.at[j])
        )
        q_copies[-1].start()
    kv_refs = (own_ref,) + tuple(kv_refs)
    t = q_ref.shape[1]
    picked = pick_prefix(place_ref, prefix_refs)
    masks = mask_ref[: len(kv_refs) * t + 2 * picked[0][0].shape[0], :]
    ones = jnp.concatenate([eye(t)] * groups, axis=1)
    own_copy.wait()

    def lanes(j):
        return slice(j * HD, (j + 1) * HD)

    def rows(part, j):
        return jnp.concatenate(
            [r[part, 0, :, lanes(j)] for r in kv_refs] + [p[:, lanes(j)] for p in picked[part]],
            axis=0,
        )

    def scored(j):
        q_copies[j].wait()
        q = jnp.concatenate([q_ref[0, :, lanes(j * groups + g)].T for g in range(groups)], axis=1)
        qt_ref[j] = q
        return score(rows(0, j), masks, q, ones)

    def weighed(j, s):
        top = jnp.max(s, axis=0, keepdims=True) * SCALE
        top_ref[j : j + 1, :] = top
        return jnp.exp2(s * SCALE - top).astype(jnp.bfloat16)

    def mixed(j, w):
        o = mix(rows(1, j), w)
        acc_ref[j] = o[:HD]
        sum_ref[j : j + 1, :] = o[HD : HD + 1]

    staged(acc_ref.shape[0], scored, weighed, mixed)


def far_kernel(groups, mask_ref, k_ref, v_ref, *refs):
    qt_ref, acc_ref, sum_ref, top_ref, out_hbm, out_ref, sems = refs
    t = k_ref.shape[2]
    masks = mask_ref[mask_ref.shape[0] - t :, :]
    ones = jnp.concatenate([eye(t)] * groups, axis=1)
    copies = []

    def lanes(j):
        return slice(j * HD, (j + 1) * HD)

    def scored(j):
        return score(k_ref[0, 0, :, lanes(j)], masks, qt_ref[j], ones)

    def weighed(j, s):
        old = top_ref[j : j + 1, :]
        top = jnp.maximum(jnp.max(s, axis=0, keepdims=True) * SCALE, old)
        return jnp.exp2(s * SCALE - top).astype(jnp.bfloat16), jnp.exp2(old - top)

    def mixed(j, pair):
        w, keep = pair
        o = mix(v_ref[0, 0, :, lanes(j)], w)
        total = sum_ref[j : j + 1, :] * keep + o[HD : HD + 1]
        part = 1.0 / total
        done = acc_ref[j] * (keep * part) + o[:HD] * part
        for g in range(groups):
            out_ref[0, :, lanes(j * groups + g)] = (
                done[:, g * t : (g + 1) * t].T.astype(out_ref.dtype)
            )
        cols = pl.ds(j * groups * HD, groups * HD)
        copies.append(
            pltpu.make_async_copy(out_ref.at[:, :, cols], out_hbm.at[:, :, cols], sems.at[j])
        )
        copies[-1].start()

    staged(acc_ref.shape[0], scored, weighed, mixed)
    for copy in copies:
        copy.wait()


def on_device(queries, keyvals, seg_len, seg_task, task_slot, prefix_bank):
    ctx_count, grp_count = (lax.axis_size(a) for a in AXES)
    t = queries.shape[1]
    kv_heads = keyvals.shape[3] // HD
    groups = queries.shape[2] // keyvals.shape[3]
    plane = grp_count == HOPS + 1
    prefix_shape = (2, 2) + prefix_bank.shape[2:]
    if plane:
        kinds = [("shift", 0)] + [("flip", k) for k in range(1, HOPS + 1)]
        sends = range(grp_count)
        near, side, far = (flip_route(ctx_count, grp_count, k) for k in range(1, HOPS + 1))
    else:
        kinds = [("shift", d) for d in range(HOPS + 1)]
        sends = range(0)
        near, side, far = (shift_route(ctx_count * grp_count, d) for d in range(1, HOPS + 1))

    got_near = lax.ppermute(keyvals, AXES, near)
    got_side = lax.ppermute(keyvals, AXES, side)

    def struct(shape, dtype):
        return jax.ShapeDtypeStruct(shape, dtype)

    def in_hbm(array):
        return pltpu.with_memory_space_constraint(array, pltpu.HBM)

    masks, place, *rows = pl.pallas_call(
        functools.partial(plan_kernel, t, kinds, sends),
        out_shape=[
            struct((len(kinds) * t + 2 * prefix_shape[2], t), jnp.bfloat16),
            struct((2, 8, 128), jnp.int32),
        ]
        + [struct(prefix_shape, prefix_bank.dtype)] * len(sends),
        in_specs=[HBM] * 4,
        out_specs=[VMEM] * (2 + len(sends)),
        scratch_shapes=[pltpu.SMEM(a.shape, a.dtype) for a in (seg_len, seg_task, task_slot)]
        + [pltpu.VMEM(prefix_bank.shape, prefix_bank.dtype), pltpu.SemaphoreType.DMA((4,))],
        compiler_params=PARAMS,
        name="plan",
    )(*(in_hbm(a) for a in (seg_len, seg_task, task_slot, prefix_bank)))
    if plane:
        prefix = [rows[0]] + [
            lax.ppermute(rows[k], "grp", [(i, i ^ k) for i in range(grp_count)]) for k in sends[1:]
        ]
        far_keys = lax.ppermute(got_side[0:1], AXES, compose_route(far, side))
        far_values = lax.ppermute(got_near[1:2], AXES, compose_route(far, near))
    else:
        prefix = [fetch_prefix(seg_len, seg_task, task_slot, prefix_bank, t)]
        got_far = lax.ppermute(keyvals, AXES, far)
        far_keys, far_values = got_far[0:1], got_far[1:2]

    wide = struct((kv_heads, HD, groups * t), jnp.float32)
    flat = struct((kv_heads, groups * t), jnp.float32)
    cost = 4 * queries.size * t
    state = pl.pallas_call(
        functools.partial(near_kernel, groups, len(prefix)),
        out_shape=[struct(wide.shape, queries.dtype), wide, flat, flat],
        in_specs=[VMEM, VMEM, HBM, HBM] + [VMEM] * (len(prefix) + 2),
        out_specs=[VMEM] * 4,
        scratch_shapes=[
            pltpu.VMEM(queries.shape, queries.dtype),
            pltpu.VMEM(keyvals.shape, keyvals.dtype),
            pltpu.SemaphoreType.DMA((kv_heads,)),
            pltpu.SemaphoreType.DMA,
        ],
        compiler_params=PARAMS,
        cost_estimate=pl.CostEstimate(
            flops=3 * cost, bytes_accessed=2 * queries.size, transcendentals=3 * queries.size
        ),
        name="attend_near",
    )(masks, place, in_hbm(queries), in_hbm(keyvals), *prefix, got_near, got_side)
    return pl.pallas_call(
        functools.partial(far_kernel, groups),
        out_shape=struct(queries.shape, queries.dtype),
        in_specs=[VMEM] * 7,
        out_specs=HBM,
        scratch_shapes=[
            pltpu.VMEM(queries.shape, queries.dtype),
            pltpu.SemaphoreType.DMA((kv_heads,)),
        ],
        compiler_params=PARAMS,
        cost_estimate=pl.CostEstimate(
            flops=cost, bytes_accessed=4 * queries.size, transcendentals=queries.size
        ),
        name="attend_far",
    )(masks, far_keys, far_values, *state)


def fetch_prefix(seg_len, seg_task, task_slot, prefix_bank, t):
    grp_count = lax.axis_size("grp")
    me = lax.axis_index("grp")
    held = prefix_bank.shape[1]
    starts = jnp.cumsum(seg_len[0]) - seg_len[0]
    shards = lax.axis_index("ctx") * grp_count + jnp.arange(grp_count, dtype=jnp.int32)
    ends = shards[:, None] * t + jnp.array([0, t - 1], jnp.int32)
    segs = jnp.sum((starts[None, None, :] <= ends[:, :, None]).astype(jnp.int32), axis=2) - 1
    rows = task_slot[seg_task[0][segs]]
    local = jnp.clip(rows - me * held, 0, held - 1)
    pieces = jnp.swapaxes(prefix_bank, 0, 1)[local]
    got = lax.all_to_all(pieces, "grp", split_axis=0, concat_axis=0, tiled=True)
    owner = rows[me] // held
    return jnp.stack([got[owner[s], s] for s in range(2)])


def solution(mesh):
    in_specs = (
        P(None, AXES, None),
        P(None, None, AXES, None),
        P(),
        P(),
        P(),
        P(None, "grp", None, None),
    )
    return jax.shard_map(
        on_device, mesh=mesh, in_specs=in_specs, out_specs=P(None, AXES, None), check_vma=False
    )
```

time: 31.6 us -> 23.5 us (0.74)
  local copies, waits for them, and re-layouts: 5.09 us -> 0.02 us
  waiting for transfers between devices: 5.37 us -> 3.45 us
  Pallas kernels: 8.41 us -> 7.5 us
    unnamed x18 -> x0, local copies, waits for them, and re-layouts: 5.08 us -> none
    ppermute x1, waiting for transfers between devices: 5.36 us -> 0.72 us  [on_device(): got_side = lax.ppermute(keyvals, AXES, side)]
    ppermute x3, waiting for transfers between devices: 0.01 us -> 2.72 us  [on_device(): lax.ppermute(rows[k], 'grp', [(i, i ^ k) for i in range(grp_count)])]
    pallas_call x3, Pallas kernels: 8.41 us -> 7.5 us  [the longest x1 4.47 us: on_device(): pl.pallas_call(functools.partial(near_kernel, groups, len(prefix)), out_s...]
  transfers between devices with their start and end apart: 7 -> 7, of which waited for: 1 -> 2; matrix products, arithmetic and copies ran while one was open for 0% -> 0% of each run, Pallas kernels for 14% -> 24%
where the time goes in v2:
time: 23.5 us; the launch traced here: 23.4 us
  starting transfers between devices  12.4 us (53%)
  Pallas kernels  7.5 us (32%)
  waiting for transfers between devices  3.45 us (15%)
    pallas_call x1, Pallas kernels, on_device(): pl.pallas_call(functools.partial(near_kernel, groups, len(prefix)), out_s...  4.47 us
    ppermute x3, starting transfers between devices, on_device(): lax.ppermute(rows[k], 'grp', [(i, i ^ k) for i in range(grp_count)])  3.55 us
    ppermute x1, starting transfers between devices, on_device(): got_side = lax.ppermute(keyvals, AXES, side)  2.97 us
    ppermute x3, waiting for transfers between devices, on_device(): lax.ppermute(rows[k], 'grp', [(i, i ^ k) for i in range(grp_count)])  2.72 us
    ppermute x1, starting transfers between devices, on_device(): far_values = lax.ppermute(got_near[1:2], AXES, compose_route(far, near))  2.35 us
    ppermute x1, starting transfers between devices, on_device(): far_keys = lax.ppermute(got_side[0:1], AXES, compose_route(far, side))  2 us
    pallas_call x1, Pallas kernels, on_device(): pl.pallas_call(functools.partial(far_kernel, groups), out_shape=struct(qu...  1.95 us
    ppermute x1, starting transfers between devices, on_device(): got_near = lax.ppermute(keyvals, AXES, near)  1.49 us
  transfers between devices with their start and end apart: 7, of which 2 were waited for; matrix products, arithmetic and copies ran while one was open for 0% of the time, Pallas kernels for 24%

profile of v2, /device:TPU:0, one launch (start us, length us, event | category | flops | bytes accessed | tf_op | source)
XLA Modules:
  0.0 23.4 jit_solution(1176572971064924418)
XLA Ops:
  0.0 3.0 %collective-permute-start = (bf16[2,1,128,512]{3,2,1,0:T(8,128)(2,1)}, bf16[2,1,128,512]{3,2,1,0:T(8,128)(2,1)S(1)}, u32[]{:S(2)}, u32[]{:S(2)}) collective-permute-start(bf16[2,1,128,512]{3,2,1,0:T(8,128)(2,1)} %own_hbm.1), channel_id=1, source_target_pairs={{0,2},{1,3},{2,4},{3,5},{4,6},{5,7},{6,8},{7,9},{8,10},{9,11},{10,... | collective-permute-start | bytes 786440 | tf_op jit(solution)/shard_map/ppermute | solution.py:259
  3.0 1.5 %collective-permute-start.2 = (bf16[2,1,128,512]{3,2,1,0:T(8,128)(2,1)}, bf16[2,1,128,512]{3,2,1,0:T(8,128)(2,1)S(1)}, u32[]{:S(2)}, u32[]{:S(2)}) collective-permute-start(bf16[2,1,128,512]{3,2,1,0:T(8,128)(2,1)} %own_hbm.1), channel_id=1, source_target_pairs={{0,1},{1,4},{2,3},{3,6},{4,5},{5,8},{6,7},{7,10},{8,9},{9,12},{10,... | collective-permute-start | bytes 786440 | tf_op jit(solution)/shard_map/ppermute | solution.py:258
  4.5 1.1 %plan.1 = (bf16[544,128]{1,0:T(8,128)(2,1)S(1)}, s32[2,8,128]{2,1,0:T(8,128)S(1)}, bf16[2,2,16,512]{3,2,1,0:T(8,128)(2,1)S(1)}, bf16[2,2,16,512]{3,2,1,0:T(8,128...) custom-call(s32[1,16]{1,0:T(1,128)} %len_hbm.1, s32[1,16]{1,0:T(1,128)} %task_hbm.1, ...), custom_call_target="tpu_custom_call" | custom-call | tf_op jit(solution)/shard_map/plan/pallas_call | solution.py:267
  5.5 0.1 collective-permute-start.4
  5.6 1.8 %collective-permute-start.5 = (bf16[2,2,16,512]{3,2,1,0:T(8,128)(2,1)S(1)}, bf16[2,2,16,512]{3,2,1,0:T(8,128)(2,1)S(1)}, u32[]{:S(2)}, u32[]{:S(2)}) collective-permute-start(bf16[2,2,16,512]{3,2,1,0:T(8,128)(2,1)S(1)} %get-tuple-element.19), channel_id=1, source_target_pairs={{0,2},{1,3},{2,0},{3,1},{4,6},{5,7},{6,4},{7,5},{8,10},{9,11},{10,... | collective-permute-start | bytes 196616 | tf_op jit(solution)/shard_map/ppermute | solution.py:283
  7.4 1.7 %collective-permute-start.6 = (bf16[2,2,16,512]{3,2,1,0:T(8,128)(2,1)S(1)}, bf16[2,2,16,512]{3,2,1,0:T(8,128)(2,1)S(1)}, u32[]{:S(2)}, u32[]{:S(2)}) collective-permute-start(bf16[2,2,16,512]{3,2,1,0:T(8,128)(2,1)S(1)} %get-tuple-element.20), channel_id=1, source_target_pairs={{0,3},{1,2},{2,1},{3,0},{4,7},{5,6},{6,5},{7,4},{8,11},{9,10},{10,... | collective-permute-start | bytes 196616 | tf_op jit(solution)/shard_map/ppermute | solution.py:283
  9.1 0.7 %collective-permute-done.refs_5_ = bf16[2,1,128,512]{3,2,1,0:T(8,128)(2,1)S(1)} collective-permute-done((bf16[2,1,128,512]{3,2,1,0:T(8,128)(2,1)}, bf16[2,1,128,512]{3,2,1,0:T(8,128)(2,1)S(1)}, u32[]{:S(2)}, u32[]{:S(2)}) %collective-permute-start) | collective-permute-done | bytes 262176 | tf_op jit(solution)/shard_map/ppermute | solution.py:259
  9.8 2.0 %collective-permute-start.1 = (bf16[1,1,128,512]{3,2,1,0:T(8,128)(2,1)S(1)}, bf16[1,1,128,512]{3,2,1,0:T(8,128)(2,1)S(1)}, u32[]{:S(2)}, u32[]{:S(2)}) collective-permute-start(bf16[1,1,128,512]{3,2,1,0:T(8,128)(2,1)S(1)} %slice.8), channel_id=1, source_target_pairs={{2,3},{3,2},{4,5},{5,4},{6,7},{7,6},{8,9},{9,8},{10,11},{11,10},{1... | collective-permute-start | bytes 393224 | tf_op jit(solution)/shard_map/ppermute | solution.py:285
  11.8 0.0 collective-permute-done.2.refs_4_
  11.8 2.4 %collective-permute-start.3 = (bf16[1,1,128,512]{3,2,1,0:T(8,128)(2,1)S(1)}, bf16[1,1,128,512]{3,2,1,0:T(8,128)(2,1)S(1)}, u32[]{:S(2)}, u32[]{:S(2)}) collective-permute-start(bf16[1,1,128,512]{3,2,1,0:T(8,128)(2,1)S(1)} %slice.9), channel_id=1, source_target_pairs={{1,3},{4,2},{3,5},{6,4},{5,7},{8,6},{7,9},{10,8},{9,11},{12,10},{1... | collective-permute-start | bytes 393224 | tf_op jit(solution)/shard_map/ppermute | solution.py:286
  14.2 0.0 collective-permute-done.4.refs_1_
  14.2 0.0 collective-permute-done.5.refs_2_
  14.2 2.7 %collective-permute-done.6.refs_3_ = bf16[2,2,16,512]{3,2,1,0:T(8,128)(2,1)S(1)} collective-permute-done((bf16[2,2,16,512]{3,2,1,0:T(8,128)(2,1)S(1)}, bf16[2,2,16,512]{3,2,1,0:T(8,128)(2,1)S(1)}, u32[]{:S(2)}, u32[]{:S(2)}) %collective-permute-start.6) | collective-permute-done | bytes 65568 | tf_op jit(solution)/shard_map/ppermute | solution.py:283
  16.9 4.5 %attend_near.1 = (bf16[4,128,1024]{2,1,0:T(8,128)(2,1)S(1)}, f32[4,128,1024]{2,1,0:T(8,128)S(1)}, f32[4,1024]{1,0:T(4,128)S(1)}, f32[4,1024]{1,0:T(4,128)S(1)}) custom-call(bf16[544,128]{1,0:T(8,128)(2,1)S(1)} %get-tuple-element.15.mask_ref, s32[2,8,128]{2,1,0:T(8,128)S(1)} %get-tuple-element.16.place_ref, bf16[1,128,4096]{2,1,0:T(8,128)(2,1)} %q_hbm.1, ...), custom_call_target="tpu_custom_call" | custom-call | flops 805306368 | bytes 1048576 | tf_op jit(solution)/shard_map/attend_near/pallas_call | solution.py:295
  21.4 0.0 collective-permute-done.1.k_ref
  21.4 0.0 collective-permute-done.3.v_ref
  21.4 2.0 %attend_far.1 = bf16[1,128,4096]{2,1,0:T(8,128)(2,1)} custom-call(bf16[544,128]{1,0:T(8,128)(2,1)S(1)} %get-tuple-element.15.mask_ref, bf16[1,1,128,512]{3,2,1,0:T(8,128)(2,1)S(1)} %collective-permute-done.1.k_ref, bf16[1,1,128,512]{3,2,1,0:T(8,128)(2,1)S(1)} %collective-permute-done.3.v_ref, bf16[4,128,1024]{2,1,0:T(8,128)(2,1)S(1)} %get-tuple-element.21.refs_0_, ...), custom_call_target="tpu_custom_call" | custom-call | flops 268435456 | bytes 2097152 | tf_op jit(solution)/shard_map/attend_far/pallas_call | solution.py:312
  (2 shorter events, 0.0 us)
Async XLA Ops:
  0.0 9.8 %collective-permute-start = (bf16[2,1,128,512]{3,2,1,0:T(8,128)(2,1)}, bf16[2,1,128,512]{3,2,1,0:T(8,128)(2,1)S(1)}, u32[]{:S(2)}, u32[]{:S(2)}) collective-permute-start(bf16[2,1,128,512]{3,2,1,0:T(8,128)(2,1)} %own_hbm.1), channel_id=1, source_target_pairs={{0,2},{1,3},{2,4},{3,5},{4,6},{5,7},{6,8},{7,9},{8,10},{9,11},{10,... | collective-permute-start | bytes 786440 | tf_op jit(solution)/shard_map/ppermute | solution.py:259
  3.0 8.9 %collective-permute-start.2 = (bf16[2,1,128,512]{3,2,1,0:T(8,128)(2,1)}, bf16[2,1,128,512]{3,2,1,0:T(8,128)(2,1)S(1)}, u32[]{:S(2)}, u32[]{:S(2)}) collective-permute-start(bf16[2,1,128,512]{3,2,1,0:T(8,128)(2,1)} %own_hbm.1), channel_id=1, source_target_pairs={{0,1},{1,4},{2,3},{3,6},{4,5},{5,8},{6,7},{7,10},{8,9},{9,12},{10,... | collective-permute-start | bytes 786440 | tf_op jit(solution)/shard_map/ppermute | solution.py:258
  5.5 8.7 %collective-permute-start.4 = (bf16[2,2,16,512]{3,2,1,0:T(8,128)(2,1)S(1)}, bf16[2,2,16,512]{3,2,1,0:T(8,128)(2,1)S(1)}, u32[]{:S(2)}, u32[]{:S(2)}) collective-permute-start(bf16[2,2,16,512]{3,2,1,0:T(8,128)(2,1)S(1)} %get-tuple-element.18), channel_id=1, source_target_pairs={{0,1},{1,0},{2,3},{3,2},{4,5},{5,4},{6,7},{7,6},{8,9},{9,8},{10,11... | collective-permute-start | bytes 196616 | tf_op jit(solution)/shard_map/ppermute | solution.py:283
  5.6 8.6 %collective-permute-start.5 = (bf16[2,2,16,512]{3,2,1,0:T(8,128)(2,1)S(1)}, bf16[2,2,16,512]{3,2,1,0:T(8,128)(2,1)S(1)}, u32[]{:S(2)}, u32[]{:S(2)}) collective-permute-start(bf16[2,2,16,512]{3,2,1,0:T(8,128)(2,1)S(1)} %get-tuple-element.19), channel_id=1, source_target_pairs={{0,2},{1,3},{2,0},{3,1},{4,6},{5,7},{6,4},{7,5},{8,10},{9,11},{10,... | collective-permute-start | bytes 196616 | tf_op jit(solution)/shard_map/ppermute | solution.py:283
  7.4 9.5 %collective-permute-start.6 = (bf16[2,2,16,512]{3,2,1,0:T(8,128)(2,1)S(1)}, bf16[2,2,16,512]{3,2,1,0:T(8,128)(2,1)S(1)}, u32[]{:S(2)}, u32[]{:S(2)}) collective-permute-start(bf16[2,2,16,512]{3,2,1,0:T(8,128)(2,1)S(1)} %get-tuple-element.20), channel_id=1, source_target_pairs={{0,3},{1,2},{2,1},{3,0},{4,7},{5,6},{6,5},{7,4},{8,11},{9,10},{10,... | collective-permute-start | bytes 196616 | tf_op jit(solution)/shard_map/ppermute | solution.py:283
  9.8 11.6 %collective-permute-start.1 = (bf16[1,1,128,512]{3,2,1,0:T(8,128)(2,1)S(1)}, bf16[1,1,128,512]{3,2,1,0:T(8,128)(2,1)S(1)}, u32[]{:S(2)}, u32[]{:S(2)}) collective-permute-start(bf16[1,1,128,512]{3,2,1,0:T(8,128)(2,1)S(1)} %slice.8), channel_id=1, source_target_pairs={{2,3},{3,2},{4,5},{5,4},{6,7},{7,6},{8,9},{9,8},{10,11},{11,10},{1... | collective-permute-start | bytes 393224 | tf_op jit(solution)/shard_map/ppermute | solution.py:285
  11.8 9.6 %collective-permute-start.3 = (bf16[1,1,128,512]{3,2,1,0:T(8,128)(2,1)S(1)}, bf16[1,1,128,512]{3,2,1,0:T(8,128)(2,1)S(1)}, u32[]{:S(2)}, u32[]{:S(2)}) collective-permute-start(bf16[1,1,128,512]{3,2,1,0:T(8,128)(2,1)S(1)} %slice.9), channel_id=1, source_target_pairs={{1,3},{4,2},{3,5},{6,4},{5,7},{8,6},{7,9},{10,8},{9,11},{12,10},{1... | collective-permute-start | bytes 393224 | tf_op jit(solution)/shard_map/ppermute | solution.py:286

commit v3 on v2

v3 whole, which is shorter than its diff:
```python
import functools
import math

import jax
import jax.numpy as jnp
from jax import lax
from jax.experimental import pallas as pl
from jax.experimental.pallas import tpu as pltpu
from jax.sharding import PartitionSpec as P

HD = 128
HOPS = 3
FAR = -1e30
AXES = ("ctx", "grp")
VMEM = pl.BlockSpec(memory_space=pltpu.VMEM)
HBM = pl.BlockSpec(memory_space=pltpu.HBM)
SCALE = math.log2(math.e) / math.sqrt(HD)
PARAMS = pltpu.CompilerParams(vmem_limit_bytes=40 * 2**20)


def shift_route(count, distance):
    return [(i, (i + distance) % count) for i in range(count)]


def flip_route(ctx_count, grp_count, flip):
    count = ctx_count * grp_count
    return [
        (i, (i + ((i % grp_count ^ flip) - i % grp_count) % grp_count) % count)
        for i in range(count)
    ]


def compose_route(wanted, first):
    holder = dict(first)
    return [(holder[s], d) for s, d in wanted]


def segments_at(len_ref, positions):
    def step(s, carry):
        start, found = carry
        out = []
        for position, (seg, begin) in zip(positions, found):
            reached = start <= position
            out.append((jnp.where(reached, s, seg), jnp.where(reached, start, begin)))
        return start + len_ref[0, s], out

    zero = jnp.int32(0)
    steps = len_ref.shape[1]
    return lax.fori_loop(0, steps, step, (zero, [(zero, zero)] * len(positions)))[1]


def block_mask(first, hop, start_a, start_b, t):
    key = lax.broadcasted_iota(jnp.int32, (t, t), 0) - hop * t
    query = lax.broadcasted_iota(jnp.int32, (t, t), 1)
    from_b = start_b - first
    start = jnp.where(query >= from_b, from_b, start_a - first)
    return jnp.where((key >= start) & (key <= query), 0.0, FAR).astype(jnp.bfloat16)


def hop_of(kind, grp_count):
    me = lax.axis_index("grp")
    if kind[0] == "shift":
        return kind[1]
    return (me - (me ^ kind[1])) & (grp_count - 1)


def plan_kernel(t, kinds, plane, len_hbm, task_hbm, slot_hbm, bank_hbm, mask_ref, *refs):
    (len_ref, task_ref, slot_ref, bank_ref, sems) = refs[-5:]
    pairs = ((len_hbm, len_ref), (task_hbm, task_ref), (slot_hbm, slot_ref), (bank_hbm, bank_ref))
    copies = [pltpu.make_async_copy(a, b, sems.at[i]) for i, (a, b) in enumerate(pairs)]
    for copy in copies:
        copy.start()
    for copy in copies[:3]:
        copy.wait()
    grp_count = lax.axis_size("grp")
    me = lax.axis_index("grp")
    row_base = lax.axis_index("ctx") * grp_count
    held = bank_ref.shape[1]
    first = (row_base + me) * t
    positions = [first, first + (t - 1)]
    groups = []
    if plane:
        across = me ^ 2
        groups = [[me, me + 1], [me ^ 1, (me ^ 1) + 1], [(across & 2) + k for k in range(3)]]
        positions += [(row_base + k) * t for group in groups for k in group]
    found = segments_at(len_ref, positions)
    (_, start_a), (_, start_b) = found[:2]
    size = bank_ref.shape[2]
    query = lax.broadcasted_iota(jnp.int32, (size, t), 1)
    from_b = start_b - first
    is_b = (query >= from_b) & (from_b > 0)
    blocks = [block_mask(first, hop_of(k, grp_count), start_a, start_b, t) for k in kinds]
    blocks[-1:-1] = [
        jnp.where(is_b, a, b).astype(jnp.bfloat16) for a, b in ((FAR, 0.0), (0.0, FAR))
    ]
    mask_ref[...] = jnp.concatenate(blocks, axis=0)
    if not plane:
        copies[3].wait()
        return
    place_ref, out_refs = refs[0], refs[1:-5]
    rows = [slot_ref[task_ref[0, seg]] for seg, _ in found[2:]]
    for i, row in enumerate(rows[:4]):
        place_ref[i] = jnp.full(place_ref.shape[1:], (row // held) ^ me, jnp.int32)
    copies[3].wait()
    for group, out_ref in zip(groups, out_refs):
        for i in range(len(group)):
            local = jnp.clip(rows.pop(0) - me * held, 0, held - 1)
            for part in range(2):
                out_ref[i, part] = bank_ref[part, local]


def here(place_ref, i, place, shape):
    return jnp.broadcast_to(place_ref[i][:1, :1] == place, shape)


def relay_kernel(place_ref, mine_ref, got_ref, out_ref):
    at = (lax.axis_index("grp") ^ 1) & 1
    for slot in range(2):
        for part in range(2):
            got = got_ref[at + slot, part]
            own = here(place_ref, 2 + slot, 0, got.shape)
            out_ref[slot, part] = jnp.where(own, mine_ref[slot, part], got)


def eye(t):
    a, b = (lax.broadcasted_iota(jnp.int32, (t, t), i) for i in range(2))
    return (a == b).astype(jnp.float32).astype(jnp.bfloat16)


def staged(count, score, weigh, mix):
    scores, weights = {}, {}
    for i in range(count + 2):
        if i < count:
            scores[i] = score(i)
        if 0 <= i - 1 < count:
            weights[i - 1] = weigh(i - 1, scores.pop(i - 1))
        if 0 <= i - 2 < count:
            mix(i - 2, weights.pop(i - 2))


def score(keys, masks, q):
    t = masks.shape[1]
    ones = jnp.concatenate([eye(t)] * (q.shape[1] // t), axis=1)
    return jnp.dot(
        jnp.concatenate([keys, masks], axis=1),
        jnp.concatenate([q, ones], axis=0),
        preferred_element_type=jnp.float32,
    )


def mix(values, weights):
    v = jnp.concatenate([values.T, jnp.ones((16, values.shape[0]), jnp.bfloat16)], axis=0)
    return jnp.dot(v, weights, preferred_element_type=jnp.float32)


def lanes(j):
    return slice(j * HD, (j + 1) * HD)


def own_kernel(groups, mask_ref, q_hbm, own_hbm, *refs):
    qt_ref, acc_ref, sum_ref, top_ref, q_ref, own_ref, q_sems, own_sem = refs
    own_copy = pltpu.make_async_copy(own_hbm, own_ref, own_sem)
    own_copy.start()
    q_copies = []
    for j in range(acc_ref.shape[0]):
        cols = pl.ds(j * groups * HD, groups * HD)
        q_copies.append(
            pltpu.make_async_copy(q_hbm.at[:, :, cols], q_ref.at[:, :, cols], q_sems.at[j])
        )
        q_copies[-1].start()
    t = q_ref.shape[1]
    masks = mask_ref[:t, :]
    own_copy.wait()

    def scored(j):
        q_copies[j].wait()
        q = jnp.concatenate([q_ref[0, :, lanes(j * groups + g)].T for g in range(groups)], axis=1)
        qt_ref[j] = q
        return score(own_ref[0, 0, :, lanes(j)], masks, q)

    def weighed(j, s):
        top = jnp.max(s, axis=0, keepdims=True) * SCALE
        top_ref[j : j + 1, :] = top
        return jnp.exp2(s * SCALE - top).astype(jnp.bfloat16)

    def mixed(j, w):
        o = mix(own_ref[1, 0, :, lanes(j)], w)
        acc_ref[j] = o[:HD]
        sum_ref[j : j + 1, :] = o[HD : HD + 1]

    staged(acc_ref.shape[0], scored, weighed, mixed)


def merge(rows, masks, qt_ref, old, finish):
    acc_ref, sum_ref, top_ref = old

    def scored(j):
        return score(rows(0, j), masks, qt_ref[j])

    def weighed(j, s):
        before = top_ref[j : j + 1, :]
        top = jnp.maximum(jnp.max(s, axis=0, keepdims=True) * SCALE, before)
        return jnp.exp2(s * SCALE - top).astype(jnp.bfloat16), jnp.exp2(before - top), top

    def mixed(j, step):
        w, keep, top = step
        o = mix(rows(1, j), w)
        finish(j, acc_ref[j], o[:HD], keep, sum_ref[j : j + 1, :] * keep + o[HD : HD + 1], top)

    staged(acc_ref.shape[0], scored, weighed, mixed)


def near_kernel(mask_ref, qt_ref, *refs):
    kv_refs, old, new = refs[:-6], refs[-6:-3], refs[-3:]
    acc_ref, sum_ref, top_ref = new
    t = mask_ref.shape[1]

    def rows(part, j):
        return jnp.concatenate([r[part, 0, :, lanes(j)] for r in kv_refs], axis=0)

    def finish(j, acc, more, keep, total, top):
        acc_ref[j] = acc * keep + more
        sum_ref[j : j + 1, :] = total
        top_ref[j : j + 1, :] = top

    merge(rows, mask_ref[t : (1 + len(kv_refs)) * t, :], qt_ref, old, finish)


def far_kernel(groups, plane, mask_ref, qt_ref, k_ref, v_ref, *refs):
    prefix_refs, old, (out_hbm, out_ref, sems) = refs[:-6], refs[-6:-3], refs[-3:]
    t = mask_ref.shape[1]
    size = prefix_refs[-1].shape[2]
    picked = [[], []]
    for part in range(2):
        for slot in range(2):
            value = prefix_refs[-1][slot, part]
            if plane:
                place_ref, own_ref, got_ref = prefix_refs[:3]
                got = got_ref[(lax.axis_index("grp") & 1) + slot, part]
                value = jnp.where(here(place_ref, slot, 2, value.shape), got, value)
                value = jnp.where(here(place_ref, slot, 0, value.shape), own_ref[slot, part], value)
            picked[part].append(value)
    copies = []

    def rows(part, j):
        block = (k_ref, v_ref)[part][0, 0, :, lanes(j)]
        return jnp.concatenate([p[:, lanes(j)] for p in picked[part]] + [block], axis=0)

    def finish(j, acc, more, keep, total, top):
        part = 1.0 / total
        done = acc * (keep * part) + more * part
        for g in range(groups):
            out_ref[0, :, lanes(j * groups + g)] = (
                done[:, g * t : (g + 1) * t].T.astype(out_ref.dtype)
            )
        cols = pl.ds(j * groups * HD, groups * HD)
        copies.append(
            pltpu.make_async_copy(out_ref.at[:, :, cols], out_hbm.at[:, :, cols], sems.at[j])
        )
        copies[-1].start()

    merge(rows, mask_ref[mask_ref.shape[0] - t - 2 * size :, :], qt_ref, old, finish)
    for copy in copies:
        copy.wait()


def on_device(queries, keyvals, seg_len, seg_task, task_slot, prefix_bank):
    ctx_count, grp_count = (lax.axis_size(a) for a in AXES)
    t = queries.shape[1]
    kv_heads = keyvals.shape[3] // HD
    groups = queries.shape[2] // keyvals.shape[3]
    plane = grp_count == HOPS + 1
    row_shape = (2,) + prefix_bank.shape[2:]
    if plane:
        kinds = [("shift", 0)] + [("flip", k) for k in range(1, HOPS + 1)]
        near, side, far = (flip_route(ctx_count, grp_count, k) for k in range(1, HOPS + 1))
    else:
        kinds = [("shift", d) for d in range(HOPS + 1)]
        near, side, far = (shift_route(ctx_count * grp_count, d) for d in range(1, HOPS + 1))

    def struct(shape, dtype):
        return jax.ShapeDtypeStruct(shape, dtype)

    def in_hbm(array):
        return pltpu.with_memory_space_constraint(array, pltpu.HBM)

    def rows_of(count):
        return struct((count,) + row_shape, prefix_bank.dtype)

    def flip(array, k):
        return lax.ppermute(array, "grp", [(i, i ^ k) for i in range(grp_count)])

    def cost(blocks):
        return pl.CostEstimate(
            flops=4 * blocks * queries.size * t,
            bytes_accessed=2 * queries.size,
            transcendentals=blocks * queries.size,
        )

    got_near = lax.ppermute(keyvals, AXES, near)
    got_side = lax.ppermute(keyvals, AXES, side)

    extra = [struct((4, 8, 128), jnp.int32)] + [rows_of(n) for n in (2, 2, 3)] if plane else []
    masks, *planned = pl.pallas_call(
        functools.partial(plan_kernel, t, kinds, plane),
        out_shape=[struct((len(kinds) * t + 2 * row_shape[1], t), jnp.bfloat16)] + extra,
        in_specs=[HBM] * 4,
        out_specs=[VMEM] * (1 + len(extra)),
        scratch_shapes=[pltpu.SMEM(a.shape, a.dtype) for a in (seg_len, seg_task, task_slot)]
        + [pltpu.VMEM(prefix_bank.shape, prefix_bank.dtype), pltpu.SemaphoreType.DMA((4,))],
        compiler_params=PARAMS,
        name="plan",
    )(*(in_hbm(a) for a in (seg_len, seg_task, task_slot, prefix_bank)))

    wide = struct((kv_heads, HD, groups * t), jnp.float32)
    flat = struct((kv_heads, groups * t), jnp.float32)
    turned, *state = pl.pallas_call(
        functools.partial(own_kernel, groups),
        out_shape=[struct(wide.shape, queries.dtype), wide, flat, flat],
        in_specs=[VMEM, HBM, HBM],
        out_specs=[VMEM] * 4,
        scratch_shapes=[
            pltpu.VMEM(queries.shape, queries.dtype),
            pltpu.VMEM(keyvals.shape, keyvals.dtype),
            pltpu.SemaphoreType.DMA((kv_heads,)),
            pltpu.SemaphoreType.DMA,
        ],
        compiler_params=PARAMS,
        cost_estimate=cost(1),
        name="attend_own",
    )(masks, in_hbm(queries), in_hbm(keyvals))

    if plane:
        place, own_rows, near_rows, side_rows = planned
        got_rows = flip(side_rows, 2)
        ready, _ = lax.optimization_barrier((got_side, state[-1]))
        far_keys = lax.ppermute(ready[0:1], AXES, compose_route(far, side))
        far_values = lax.ppermute(got_near[1:2], AXES, compose_route(far, near))
        relayed = pl.pallas_call(
            relay_kernel,
            out_shape=rows_of(2),
            in_specs=[VMEM] * 3,
            out_specs=VMEM,
            compiler_params=PARAMS,
            name="relay_rows",
        )(place, near_rows, got_rows)
        prefix = [place, own_rows, got_rows, flip(relayed, 1)]
    else:
        prefix = [fetch_prefix(seg_len, seg_task, task_slot, prefix_bank, t)]
        got_far = lax.ppermute(keyvals, AXES, far)
        far_keys, far_values = got_far[0:1], got_far[1:2]

    state = pl.pallas_call(
        near_kernel,
        out_shape=[wide, flat, flat],
        in_specs=[VMEM] * 7,
        out_specs=[VMEM] * 3,
        compiler_params=PARAMS,
        cost_estimate=cost(2),
        name="attend_near",
    )(masks, turned, got_near, got_side, *state)
    return pl.pallas_call(
        functools.partial(far_kernel, groups, plane),
        out_shape=struct(queries.shape, queries.dtype),
        in_specs=[VMEM] * (7 + len(prefix)),
        out_specs=HBM,
        scratch_shapes=[
            pltpu.VMEM(queries.shape, queries.dtype),
            pltpu.SemaphoreType.DMA((kv_heads,)),
        ],
        compiler_params=PARAMS,
        cost_estimate=cost(1),
        name="attend_far",
    )(masks, turned, far_keys, far_values, *prefix, *state)


def fetch_prefix(seg_len, seg_task, task_slot, prefix_bank, t):
    grp_count = lax.axis_size("grp")
    me = lax.axis_index("grp")
    held = prefix_bank.shape[1]
    starts = jnp.cumsum(seg_len[0]) - seg_len[0]
    shards = lax.axis_index("ctx") * grp_count + jnp.arange(grp_count, dtype=jnp.int32)
    ends = shards[:, None] * t + jnp.array([0, t - 1], jnp.int32)
    segs = jnp.sum((starts[None, None, :] <= ends[:, :, None]).astype(jnp.int32), axis=2) - 1
    rows = task_slot[seg_task[0][segs]]
    local = jnp.clip(rows - me * held, 0, held - 1)
    pieces = jnp.swapaxes(prefix_bank, 0, 1)[local]
    got = lax.all_to_all(pieces, "grp", split_axis=0, concat_axis=0, tiled=True)
    owner = rows[me] // held
    return jnp.stack([got[owner[s], s] for s in range(2)])


def solution(mesh):
    in_specs = (
        P(None, AXES, None),
        P(None, None, AXES, None),
        P(),
        P(),
        P(),
        P(None, "grp", None, None),
    )
    return jax.shard_map(
        on_device, mesh=mesh, in_specs=in_specs, out_specs=P(None, AXES, None), check_vma=False
    )
```

time: 23.5 us -> 21.2 us (0.902)
  starting transfers between devices: 12.4 us -> 9.12 us
  Pallas kernels: 7.5 us -> 8.03 us
  waiting for transfers between devices: 3.45 us -> 3.8 us
    ppermute x4 -> x3, starting transfers between devices: 5.55 us -> 2.31 us  [the longest x1 1.91 us: on_device(): far_keys = lax.ppermute(ready[0:1], AXES, compose_route(far, side))]
    ppermute x1, waiting for transfers between devices: 0.72 us -> 1.32 us  [on_device(): got_side = lax.ppermute(keyvals, AXES, side)]
    pallas_call x3 -> x5, Pallas kernels: 7.5 us -> 8.03 us  [the longest x1 2.97 us: on_device(): pl.pallas_call(functools.partial(own_kernel, groups), out_shape=[struct(w...]
    ppermute x4 -> x3, waiting for transfers between devices: 2.73 us -> 2.48 us  [the longest x2 2.47 us: flip(): return lax.ppermute(array, 'grp', [(i, i ^ k) for i in range(grp_count)])]
  transfers between devices with their start and end apart: 7 -> 6, of which waited for: 2 -> 2; matrix products, arithmetic and copies ran while one was open for 0% -> 0% of each run, Pallas kernels for 24% -> 28%
where the time goes in v3:
time: 21.2 us; the launch traced here: 21 us
  starting transfers between devices  9.12 us (43%)
  Pallas kernels  8.03 us (38%)
  waiting for transfers between devices  3.8 us (18%)
    ppermute x1, starting transfers between devices, on_device(): got_side = lax.ppermute(keyvals, AXES, side)  2.97 us
    pallas_call x1, Pallas kernels, on_device(): pl.pallas_call(functools.partial(own_kernel, groups), out_shape=[struct(w...  2.97 us
    ppermute x2, waiting for transfers between devices, flip(): return lax.ppermute(array, 'grp', [(i, i ^ k) for i in range(grp_count)])  2.47 us
    ppermute x1, starting transfers between devices, on_device(): far_values = lax.ppermute(got_near[1:2], AXES, compose_route(far, near))  2.35 us
    pallas_call x1, Pallas kernels, on_device(): pl.pallas_call(functools.partial(far_kernel, groups, plane), out_shape=st...  2.11 us
    ppermute x1, starting transfers between devices, on_device(): far_keys = lax.ppermute(ready[0:1], AXES, compose_route(far, side))  1.91 us
    pallas_call x1, Pallas kernels, on_device(): pl.pallas_call(near_kernel, out_shape=[wide, flat, flat], in_specs=[VMEM]...  1.85 us
    ppermute x1, starting transfers between devices, on_device(): got_near = lax.ppermute(keyvals, AXES, near)  1.49 us
  transfers between devices with their start and end apart: 6, of which 2 were waited for; matrix products, arithmetic and copies ran while one was open for 0% of the time, Pallas kernels for 28%

profile of v3, /device:TPU:0, one launch (start us, length us, event | category | flops | bytes accessed | tf_op | source)
XLA Modules:
  0.0 21.0 jit_solution(13483047012181795191)
XLA Ops:
  0.0 3.0 %collective-permute-start = (bf16[2,1,128,512]{3,2,1,0:T(8,128)(2,1)}, bf16[2,1,128,512]{3,2,1,0:T(8,128)(2,1)S(1)}, u32[]{:S(2)}, u32[]{:S(2)}) collective-permute-start(bf16[2,1,128,512]{3,2,1,0:T(8,128)(2,1)} %own_hbm.1), channel_id=1, source_target_pairs={{0,2},{1,3},{2,4},{3,5},{4,6},{5,7},{6,8},{7,9},{8,10},{9,11},{10,... | collective-permute-start | bytes 786440 | tf_op jit(solution)/shard_map/ppermute | solution.py:301
  3.0 1.5 %collective-permute-start.2 = (bf16[2,1,128,512]{3,2,1,0:T(8,128)(2,1)}, bf16[2,1,128,512]{3,2,1,0:T(8,128)(2,1)S(1)}, u32[]{:S(2)}, u32[]{:S(2)}) collective-permute-start(bf16[2,1,128,512]{3,2,1,0:T(8,128)(2,1)} %own_hbm.1), channel_id=1, source_target_pairs={{0,1},{1,4},{2,3},{3,6},{4,5},{5,8},{6,7},{7,10},{8,9},{9,12},{10,... | collective-permute-start | bytes 786440 | tf_op jit(solution)/shard_map/ppermute | solution.py:300
  4.5 1.1 %plan.1 = (bf16[544,128]{1,0:T(8,128)(2,1)S(1)}, s32[4,8,128]{2,1,0:T(8,128)S(1)}, bf16[2,2,16,512]{3,2,1,0:T(8,128)(2,1)S(1)}, bf16[2,2,16,512]{3,2,1,0:T(8,128)(2,1)S(1)}, bf16[3,2,16,512]{3,2,1,0:T(8,128)(2,1)S(1)}) custom-call(s32[1,16]{1,0:T(1,128)} %len_hbm.1, s32[1,16]{1,0:T(1,128)} %task_hbm.1, s32[24]{0:T(128)} %slot_hbm.1, ...), custom_call_target="tpu_custom_call" | custom-call | tf_op jit(solution)/shard_map/plan/pallas_call | solution.py:304
  5.5 0.1 collective-permute-start.4
  5.6 3.0 %attend_own.1 = (bf16[4,128,1024]{2,1,0:T(8,128)(2,1)S(1)}, f32[4,128,1024]{2,1,0:T(8,128)S(1)}, f32[4,1024]{1,0:T(4,128)S(1)}, f32[4,1024]{1,0:T(4,128)S(1)}) custom-call(bf16[544,128]{1,0:T(8,128)(2,1)S(1)} %get-tuple-element.18.mask_ref, bf16[1,128,4096]{2,1,0:T(8,128)(2,1)} %q_hbm.1, bf16[2,1,128,512]{3,2,1,0:T(8,128)(2,1)} %own_hbm.1), custom_call_target="tpu_custom_call" | custom-call | flops 268435456 | bytes 1048576 | tf_op jit(solution)/shard_map/attend_own/pallas_call | solution.py:317
  8.6 1.3 %collective-permute-done.refs_1_ = bf16[2,1,128,512]{3,2,1,0:T(8,128)(2,1)S(1)} collective-permute-done((bf16[2,1,128,512]{3,2,1,0:T(8,128)(2,1)}, bf16[2,1,128,512]{3,2,1,0:T(8,128)(2,1)S(1)}, u32[]{:S(2)}, u32[]{:S(2)}) %collective-permute-start) | collective-permute-done | bytes 262176 | tf_op jit(solution)/shard_map/ppermute | solution.py:301
  9.9 1.9 %collective-permute-start.1 = (bf16[1,1,128,512]{3,2,1,0:T(8,128)(2,1)S(1)}, bf16[1,1,128,512]{3,2,1,0:T(8,128)(2,1)S(1)}, u32[]{:S(2)}, u32[]{:S(2)}) collective-permute-start(bf16[1,1,128,512]{3,2,1,0:T(8,128)(2,1)S(1)} %slice.6), channel_id=1, source_target_pairs={{2,3},{3,2},{4,5},{5,4},{6,7},{7,6},{8,9},{9,8},{10,11},{11,10},{1... | collective-permute-start | bytes 393224 | tf_op jit(solution)/shard_map/ppermute | solution.py:337
  11.8 0.0 collective-permute-done.2.refs_0_
  11.8 2.4 %collective-permute-start.3 = (bf16[1,1,128,512]{3,2,1,0:T(8,128)(2,1)S(1)}, bf16[1,1,128,512]{3,2,1,0:T(8,128)(2,1)S(1)}, u32[]{:S(2)}, u32[]{:S(2)}) collective-permute-start(bf16[1,1,128,512]{3,2,1,0:T(8,128)(2,1)S(1)} %slice.8), channel_id=1, source_target_pairs={{1,3},{4,2},{3,5},{6,4},{5,7},{8,6},{7,9},{10,8},{9,11},{12,10},{1... | collective-permute-start | bytes 393224 | tf_op jit(solution)/shard_map/ppermute | solution.py:338
  14.2 0.0 collective-permute-done.4.got_ref.refs_2_
  14.3 0.3 %collective-permute-start.5 = (bf16[2,2,16,512]{3,2,1,0:T(8,128)(2,1)S(1)}, bf16[2,2,16,512]{3,2,1,0:T(8,128)(2,1)S(1)}, u32[]{:S(2)}, u32[]{:S(2)}) collective-permute-start(bf16[2,2,16,512]{3,2,1,0:T(8,128)(2,1)S(1)} %relay_rows.1), channel_id=1, source_target_pairs={{0,1},{1,0},{2,3},{3,2},{4,5},{5,4},{6,7},{7,6},{8,9},{9,8},{10,11... | collective-permute-start | bytes 196616 | tf_op jit(solution)/shard_map/ppermute | solution.py:291
  14.6 1.9 %attend_near.1 = (f32[4,128,1024]{2,1,0:T(8,128)S(1)}, f32[4,1024]{1,0:T(4,128)S(1)}, f32[4,1024]{1,0:T(4,128)S(1)}) custom-call(bf16[544,128]{1,0:T(8,128)(2,1)S(1)} %get-tuple-element.18.mask_ref, bf16[4,128,1024]{2,1,0:T(8,128)(2,1)S(1)} %get-tuple-element.19.qt_ref, bf16[2,1,128,512]{3,2,1,0:T(8,128)(2,1)S(1)} %collective-permute-done.2.refs_0_, ...), custom_call_target="tpu_custom_call" | custom-call | flops 536870912 | bytes 1048576 | tf_op jit(solution)/shard_map/attend_near/pallas_call | solution.py:353
  16.4 2.5 %collective-permute-done.5.refs_3_ = bf16[2,2,16,512]{3,2,1,0:T(8,128)(2,1)S(1)} collective-permute-done((bf16[2,2,16,512]{3,2,1,0:T(8,128)(2,1)S(1)}, bf16[2,2,16,512]{3,2,1,0:T(8,128)(2,1)S(1)}, u32[]{:S(2)}, u32[]{:S(2)}) %collective-permute-start.5) | collective-permute-done | bytes 65568 | tf_op jit(solution)/shard_map/ppermute | solution.py:291
  18.9 0.0 collective-permute-done.1.k_ref
  18.9 0.0 collective-permute-done.3.v_ref
  18.9 2.1 %attend_far.1 = bf16[1,128,4096]{2,1,0:T(8,128)(2,1)} custom-call(bf16[544,128]{1,0:T(8,128)(2,1)S(1)} %get-tuple-element.18.mask_ref, bf16[4,128,1024]{2,1,0:T(8,128)(2,1)S(1)} %get-tuple-element.19.qt_ref, bf16[1,1,128,512]{3,2,1,0:T(8,128)(2,1)S(1)} %collective-permute-done.1.k_ref, bf16[1,1,128,512]{3,2,1,0:T(8,128)(2,1)S(1)} %collective-permute-done.3.v_ref, ...), custom_call_target="tpu_custom_call" | custom-call | flops 268435456 | bytes 1048576 | tf_op jit(solution)/shard_map/attend_far/pallas_call | solution.py:362
  (3 shorter events, 0.1 us)
Async XLA Ops:
  0.0 9.9 %collective-permute-start = (bf16[2,1,128,512]{3,2,1,0:T(8,128)(2,1)}, bf16[2,1,128,512]{3,2,1,0:T(8,128)(2,1)S(1)}, u32[]{:S(2)}, u32[]{:S(2)}) collective-permute-start(bf16[2,1,128,512]{3,2,1,0:T(8,128)(2,1)} %own_hbm.1), channel_id=1, source_target_pairs={{0,2},{1,3},{2,4},{3,5},{4,6},{5,7},{6,8},{7,9},{8,10},{9,11},{10,... | collective-permute-start | bytes 786440 | tf_op jit(solution)/shard_map/ppermute | solution.py:301
  3.0 8.9 %collective-permute-start.2 = (bf16[2,1,128,512]{3,2,1,0:T(8,128)(2,1)}, bf16[2,1,128,512]{3,2,1,0:T(8,128)(2,1)S(1)}, u32[]{:S(2)}, u32[]{:S(2)}) collective-permute-start(bf16[2,1,128,512]{3,2,1,0:T(8,128)(2,1)} %own_hbm.1), channel_id=1, source_target_pairs={{0,1},{1,4},{2,3},{3,6},{4,5},{5,8},{6,7},{7,10},{8,9},{9,12},{10,... | collective-permute-start | bytes 786440 | tf_op jit(solution)/shard_map/ppermute | solution.py:300
  5.5 8.7 %collective-permute-start.4 = (bf16[3,2,16,512]{3,2,1,0:T(8,128)(2,1)S(1)}, bf16[3,2,16,512]{3,2,1,0:T(8,128)(2,1)S(1)}, u32[]{:S(2)}, u32[]{:S(2)}) collective-permute-start(bf16[3,2,16,512]{3,2,1,0:T(8,128)(2,1)S(1)} %get-tuple-element.24), channel_id=1, source_target_pairs={{0,2},{1,3},{2,0},{3,1},{4,6},{5,7},{6,4},{7,5},{8,10},{9,11},{10,... | collective-permute-start | bytes 294920 | tf_op jit(solution)/shard_map/ppermute | solution.py:291
  9.9 9.0 %collective-permute-start.1 = (bf16[1,1,128,512]{3,2,1,0:T(8,128)(2,1)S(1)}, bf16[1,1,128,512]{3,2,1,0:T(8,128)(2,1)S(1)}, u32[]{:S(2)}, u32[]{:S(2)}) collective-permute-start(bf16[1,1,128,512]{3,2,1,0:T(8,128)(2,1)S(1)} %slice.6), channel_id=1, source_target_pairs={{2,3},{3,2},{4,5},{5,4},{6,7},{7,6},{8,9},{9,8},{10,11},{11,10},{1... | collective-permute-start | bytes 393224 | tf_op jit(solution)/shard_map/ppermute | solution.py:337
  11.8 7.1 %collective-permute-start.3 = (bf16[1,1,128,512]{3,2,1,0:T(8,128)(2,1)S(1)}, bf16[1,1,128,512]{3,2,1,0:T(8,128)(2,1)S(1)}, u32[]{:S(2)}, u32[]{:S(2)}) collective-permute-start(bf16[1,1,128,512]{3,2,1,0:T(8,128)(2,1)S(1)} %slice.8), channel_id=1, source_target_pairs={{1,3},{4,2},{3,5},{6,4},{5,7},{8,6},{7,9},{10,8},{9,11},{12,10},{1... | collective-permute-start | bytes 393224 | tf_op jit(solution)/shard_map/ppermute | solution.py:338
  14.3 4.7 %collective-permute-start.5 = (bf16[2,2,16,512]{3,2,1,0:T(8,128)(2,1)S(1)}, bf16[2,2,16,512]{3,2,1,0:T(8,128)(2,1)S(1)}, u32[]{:S(2)}, u32[]{:S(2)}) collective-permute-start(bf16[2,2,16,512]{3,2,1,0:T(8,128)(2,1)S(1)} %relay_rows.1), channel_id=1, source_target_pairs={{0,1},{1,0},{2,3},{3,2},{4,5},{5,4},{6,7},{7,6},{8,9},{9,8},{10,11... | collective-permute-start | bytes 196616 | tf_op jit(solution)/shard_map/ppermute | solution.py:291

commit v4 on v3

--- a/solution.py
+++ b/solution.py
@@ -64,9 +64,32 @@
     return (me - (me ^ kind[1])) & (grp_count - 1)
 
 
-def plan_kernel(t, kinds, plane, len_hbm, task_hbm, slot_hbm, bank_hbm, mask_ref, *refs):
+def plan_kernel(
+    t,
+    kinds,
+    plane,
+    len_hbm,
+    task_hbm,
+    slot_hbm,
+    bank_hbm,
+    kv_hbm,
+    q_hbm,
+    mask_ref,
+    k_ref,
+    v_ref,
+    q_ref,
+    *refs,
+):
     (len_ref, task_ref, slot_ref, bank_ref, sems) = refs[-5:]
-    pairs = ((len_hbm, len_ref), (task_hbm, task_ref), (slot_hbm, slot_ref), (bank_hbm, bank_ref))
+    pairs = (
+        (len_hbm, len_ref),
+        (task_hbm, task_ref),
+        (slot_hbm, slot_ref),
+        (kv_hbm.at[pl.ds(0, 1)], k_ref),
+        (kv_hbm.at[pl.ds(1, 1)], v_ref),
+        (bank_hbm, bank_ref),
+        (q_hbm, q_ref),
+    )
     copies = [pltpu.make_async_copy(a, b, sems.at[i]) for i, (a, b) in enumerate(pairs)]
     for copy in copies:
         copy.start()
@@ -94,19 +117,21 @@
         jnp.where(is_b, a, b).astype(jnp.bfloat16) for a, b in ((FAR, 0.0), (0.0, FAR))
     ]
     mask_ref[...] = jnp.concatenate(blocks, axis=0)
+    for copy in copies[3:6]:
+        copy.wait()
     if not plane:
-        copies[3].wait()
+        copies[6].wait()
         return
     place_ref, out_refs = refs[0], refs[1:-5]
     rows = [slot_ref[task_ref[0, seg]] for seg, _ in found[2:]]
     for i, row in enumerate(rows[:4]):
         place_ref[i] = jnp.full(place_ref.shape[1:], (row // held) ^ me, jnp.int32)
-    copies[3].wait()
     for group, out_ref in zip(groups, out_refs):
         for i in range(len(group)):
             local = jnp.clip(rows.pop(0) - me * held, 0, held - 1)
             for part in range(2):
                 out_ref[i, part] = bank_ref[part, local]
+    copies[6].wait()
 
 
 def here(place_ref, i, place, shape):
@@ -157,26 +182,17 @@
     return slice(j * HD, (j + 1) * HD)
 
 
-def own_kernel(groups, mask_ref, q_hbm, own_hbm, *refs):
-    qt_ref, acc_ref, sum_ref, top_ref, q_ref, own_ref, q_sems, own_sem = refs
-    own_copy = pltpu.make_async_copy(own_hbm, own_ref, own_sem)
-    own_copy.start()
-    q_copies = []
-    for j in range(acc_ref.shape[0]):
-        cols = pl.ds(j * groups * HD, groups * HD)
-        q_copies.append(
-            pltpu.make_async_copy(q_hbm.at[:, :, cols], q_ref.at[:, :, cols], q_sems.at[j])
-        )
-        q_copies[-1].start()
-    t = q_ref.shape[1]
-    masks = mask_ref[:t, :]
-    own_copy.wait()
+def near_kernel(groups, mask_ref, q_ref, *refs):
+    kv_refs, (qt_ref, acc_ref, sum_ref, top_ref) = refs[:-4], refs[-4:]
+    masks = mask_ref[: len(kv_refs) // 2 * q_ref.shape[1], :]
+
+    def rows(part, j):
+        return jnp.concatenate([r[0, 0, :, lanes(j)] for r in kv_refs[part::2]], axis=0)
 
     def scored(j):
-        q_copies[j].wait()
         q = jnp.concatenate([q_ref[0, :, lanes(j * groups + g)].T for g in range(groups)], axis=1)
         qt_ref[j] = q
-        return score(own_ref[0, 0, :, lanes(j)], masks, q)
+        return score(rows(0, j), masks, q)
 
     def weighed(j, s):
         top = jnp.max(s, axis=0, keepdims=True) * SCALE
@@ -184,7 +200,7 @@
         return jnp.exp2(s * SCALE - top).astype(jnp.bfloat16)
 
     def mixed(j, w):
-        o = mix(own_ref[1, 0, :, lanes(j)], w)
+        o = mix(rows(1, j), w)
         acc_ref[j] = o[:HD]
         sum_ref[j : j + 1, :] = o[HD : HD + 1]
 
@@ -208,22 +224,6 @@
         finish(j, acc_ref[j], o[:HD], keep, sum_ref[j : j + 1, :] * keep + o[HD : HD + 1], top)
 
     staged(acc_ref.shape[0], scored, weighed, mixed)
-
-
-def near_kernel(mask_ref, qt_ref, *refs):
-    kv_refs, old, new = refs[:-6], refs[-6:-3], refs[-3:]
-    acc_ref, sum_ref, top_ref = new
-    t = mask_ref.shape[1]
-
-    def rows(part, j):
-        return jnp.concatenate([r[part, 0, :, lanes(j)] for r in kv_refs], axis=0)
-
-    def finish(j, acc, more, keep, total, top):
-        acc_ref[j] = acc * keep + more
-        sum_ref[j : j + 1, :] = total
-        top_ref[j : j + 1, :] = top
-
-    merge(rows, mask_ref[t : (1 + len(kv_refs)) * t, :], qt_ref, old, finish)
 
 
 def far_kernel(groups, plane, mask_ref, qt_ref, k_ref, v_ref, *refs):
@@ -297,68 +297,56 @@
             transcendentals=blocks * queries.size,
         )
 
-    got_near = lax.ppermute(keyvals, AXES, near)
-    got_side = lax.ppermute(keyvals, AXES, side)
-
     extra = [struct((4, 8, 128), jnp.int32)] + [rows_of(n) for n in (2, 2, 3)] if plane else []
-    masks, *planned = pl.pallas_call(
+    half = struct((1,) + keyvals.shape[1:], keyvals.dtype)
+    masks, keys, values, fetched, *planned = pl.pallas_call(
         functools.partial(plan_kernel, t, kinds, plane),
-        out_shape=[struct((len(kinds) * t + 2 * row_shape[1], t), jnp.bfloat16)] + extra,
-        in_specs=[HBM] * 4,
-        out_specs=[VMEM] * (1 + len(extra)),
+        out_shape=[struct((len(kinds) * t + 2 * row_shape[1], t), jnp.bfloat16)] + [half] * 2 + [struct(queries.shape, queries.dtype)] + extra,
+        in_specs=[HBM] * 6,
+        out_specs=[VMEM] * (4 + len(extra)),
         scratch_shapes=[pltpu.SMEM(a.shape, a.dtype) for a in (seg_len, seg_task, task_slot)]
-        + [pltpu.VMEM(prefix_bank.shape, prefix_bank.dtype), pltpu.SemaphoreType.DMA((4,))],
+        + [pltpu.VMEM(prefix_bank.shape, prefix_bank.dtype), pltpu.SemaphoreType.DMA((7,))],
         compiler_params=PARAMS,
         name="plan",
-    )(*(in_hbm(a) for a in (seg_len, seg_task, task_slot, prefix_bank)))
-
-    wide = struct((kv_heads, HD, groups * t), jnp.float32)
-    flat = struct((kv_heads, groups * t), jnp.float32)
-    turned, *state = pl.pallas_call(
-        functools.partial(own_kernel, groups),
-        out_shape=[struct(wide.shape, queries.dtype), wide, flat, flat],
-        in_specs=[VMEM, HBM, HBM],
-        out_specs=[VMEM] * 4,
-        scratch_shapes=[
-            pltpu.VMEM(queries.shape, queries.dtype),
-            pltpu.VMEM(keyvals.shape, keyvals.dtype),
-            pltpu.SemaphoreType.DMA((kv_heads,)),
-            pltpu.SemaphoreType.DMA,
-        ],
-        compiler_params=PARAMS,
-        cost_estimate=cost(1),
-        name="attend_own",
-    )(masks, in_hbm(queries), in_hbm(keyvals))
-
+    )(*(in_hbm(a) for a in (seg_len, seg_task, task_slot, prefix_bank, keyvals, queries)))
+
+    side_keys = lax.ppermute(keys, AXES, side)
+    near_values = lax.ppermute(values, AXES, near)
     if plane:
         place, own_rows, near_rows, side_rows = planned
         got_rows = flip(side_rows, 2)
-        ready, _ = lax.optimization_barrier((got_side, state[-1]))
-        far_keys = lax.ppermute(ready[0:1], AXES, compose_route(far, side))
-        far_values = lax.ppermute(got_near[1:2], AXES, compose_route(far, near))
+    near_keys = lax.ppermute(keys, AXES, near)
+    side_values = lax.ppermute(values, AXES, side)
+    if plane:
+        far_keys = lax.ppermute(side_keys, AXES, compose_route(far, side))
+        far_values = lax.ppermute(near_values, AXES, compose_route(far, near))
         relayed = pl.pallas_call(
             relay_kernel,
             out_shape=rows_of(2),
             in_specs=[VMEM] * 3,
             out_specs=VMEM,
             compiler_params=PARAMS,
+            cost_estimate=cost(16),
             name="relay_rows",
         )(place, near_rows, got_rows)
         prefix = [place, own_rows, got_rows, flip(relayed, 1)]
     else:
         prefix = [fetch_prefix(seg_len, seg_task, task_slot, prefix_bank, t)]
-        got_far = lax.ppermute(keyvals, AXES, far)
-        far_keys, far_values = got_far[0:1], got_far[1:2]
-
-    state = pl.pallas_call(
-        near_kernel,
-        out_shape=[wide, flat, flat],
-        in_specs=[VMEM] * 7,
-        out_specs=[VMEM] * 3,
+        far_keys = lax.ppermute(keys, AXES, far)
+        far_values = lax.ppermute(values, AXES, far)
+
+    wide = struct((kv_heads, HD, groups * t), jnp.float32)
+    flat = struct((kv_heads, groups * t), jnp.float32)
+    kv = [keys, values, near_keys, near_values, side_keys, side_values]
+    turned, *state = pl.pallas_call(
+        functools.partial(near_kernel, groups),
+        out_shape=[struct(wide.shape, queries.dtype), wide, flat, flat],
+        in_specs=[VMEM] * (2 + len(kv)),
+        out_specs=[VMEM] * 4,
         compiler_params=PARAMS,
-        cost_estimate=cost(2),
+        cost_estimate=cost(3),
         name="attend_near",
-    )(masks, turned, got_near, got_side, *state)
+    )(masks, fetched, *kv)
     return pl.pallas_call(
         functools.partial(far_kernel, groups, plane),
         out_shape=struct(queries.shape, queries.dtype),

time: 21.2 us -> 20.9 us (0.986)
  Pallas kernels: 8.03 us -> 6.16 us
  waiting for transfers between devices: 3.8 us -> 4.86 us
  starting transfers between devices: 9.12 us -> 9.73 us
    ppermute x4 -> x6, waiting for transfers between devices: 1.33 us -> 3.71 us  [the longest x1 1.75 us: on_device(): side_values = lax.ppermute(values, AXES, side)]
    pallas_call x2 -> x1, Pallas kernels: 4.82 us -> 2.49 us  [on_device(): pl.pallas_call(functools.partial(near_kernel, groups), out_shape=[struct(...]
    ppermute x2, waiting for transfers between devices: 2.47 us -> 1.16 us  [flip(): return lax.ppermute(array, 'grp', [(i, i ^ k) for i in range(grp_count)])]
    ppermute x4 -> x6, starting transfers between devices: 8.73 us -> 9.58 us  [the longest x1 3.03 us: on_device(): side_keys = lax.ppermute(keys, AXES, side)]
    pallas_call x1, Pallas kernels: 1.06 us -> 1.52 us  [on_device(): pl.pallas_call(functools.partial(plan_kernel, t, kinds, plane), out_shape...]
    ppermute x2, starting transfers between devices: 0.4 us -> 0.15 us  [flip(): return lax.ppermute(array, 'grp', [(i, i ^ k) for i in range(grp_count)])]
  transfers between devices with their start and end apart: 6 -> 8, of which waited for: 2 -> 4; matrix products, arithmetic and copies ran while one was open for 0% -> 0% of each run, Pallas kernels for 28% -> 12%
where the time goes in v4:
time: 20.9 us; the launch traced here: 20.8 us
  starting transfers between devices  9.73 us (47%)
  Pallas kernels  6.16 us (29%)
  waiting for transfers between devices  4.86 us (23%)
    ppermute x1, starting transfers between devices, on_device(): side_keys = lax.ppermute(keys, AXES, side)  3.03 us
    pallas_call x1, Pallas kernels, on_device(): pl.pallas_call(functools.partial(near_kernel, groups), out_shape=[struct(...  2.49 us
    pallas_call x1, Pallas kernels, on_device(): pl.pallas_call(functools.partial(far_kernel, groups, plane), out_shape=st...  2.11 us
    ppermute x1, starting transfers between devices, on_device(): far_keys = lax.ppermute(side_keys, AXES, compose_route(far, side))  1.93 us
    ppermute x1, waiting for transfers between devices, on_device(): side_values = lax.ppermute(values, AXES, side)  1.75 us
    ppermute x1, waiting for transfers between devices, on_device(): side_keys = lax.ppermute(keys, AXES, side)  1.72 us
    ppermute x1, starting transfers between devices, on_device(): near_keys = lax.ppermute(keys, AXES, near)  1.7 us
    pallas_call x1, Pallas kernels, on_device(): pl.pallas_call(functools.partial(plan_kernel, t, kinds, plane), out_shape...  1.52 us
  transfers between devices with their start and end apart: 8, of which 4 were waited for; matrix products, arithmetic and copies ran while one was open for 0% of the time, Pallas kernels for 12%

profile of v4, /device:TPU:0, one launch (start us, length us, event | category | flops | bytes accessed | tf_op | source)
XLA Modules:
  0.0 20.8 jit_solution(13914490528033962215)
XLA Ops:
  0.0 1.5 %plan.1 = (bf16[544,128]{1,0:T(8,128)(2,1)S(1)}, bf16[1,1,128,512]{3,2,1,0:T(8,128)(2,1)S(1)}, bf16[1,1,128,512]{3,2,1,0:T(8,128)(2,1)S(1)}, bf16[1,128,4096]{2,...) custom-call(s32[1,16]{1,0:T(1,128)} %len_hbm.1, ...), custom_call_target="tpu_custom_call" | custom-call | tf_op jit(solution)/shard_map/plan/pallas_call | solution.py:302
  1.5 3.0 %collective-permute-start.2 = (bf16[1,1,128,512]{3,2,1,0:T(8,128)(2,1)S(1)}, bf16[1,1,128,512]{3,2,1,0:T(8,128)(2,1)S(1)}, u32[]{:S(2)}, u32[]{:S(2)}) collective-permute-start(bf16[1,1,128,512]{3,2,1,0:T(8,128)(2,1)S(1)} %get-tuple-element.19.refs_0_), channel_id=1, source_target_pairs={{0,2},{1,3},{2,4},{3,5},{4,6},{5,7},{6,8},{7,9},{8,10},{9,11},{10,... | collective-permute-start | bytes 393224 | tf_op jit(solution)/shard_map/ppermute | solution.py:313
  4.6 1.5 %collective-permute-start.1 = (bf16[1,1,128,512]{3,2,1,0:T(8,128)(2,1)S(1)}, bf16[1,1,128,512]{3,2,1,0:T(8,128)(2,1)S(1)}, u32[]{:S(2)}, u32[]{:S(2)}) collective-permute-start(bf16[1,1,128,512]{3,2,1,0:T(8,128)(2,1)S(1)} %get-tuple-element.20.refs_1_), channel_id=1, source_target_pairs={{0,1},{1,4},{2,3},{3,6},{4,5},{5,8},{6,7},{7,10},{8,9},{9,12},{10,... | collective-permute-start | bytes 393224 | tf_op jit(solution)/shard_map/ppermute | solution.py:314
  6.1 0.1 collective-permute-start.6
  6.1 1.7 %collective-permute-start = (bf16[1,1,128,512]{3,2,1,0:T(8,128)(2,1)S(1)}, bf16[1,1,128,512]{3,2,1,0:T(8,128)(2,1)S(1)}, u32[]{:S(2)}, u32[]{:S(2)}) collective-permute-start(bf16[1,1,128,512]{3,2,1,0:T(8,128)(2,1)S(1)} %get-tuple-element.19.refs_0_), channel_id=1, source_target_pairs={{0,1},{1,4},{2,3},{3,6},{4,5},{5,8},{6,7},{7,10},{8,9},{9,12},{10,... | collective-permute-start | bytes 393224 | tf_op jit(solution)/shard_map/ppermute | solution.py:318
  7.8 0.3 %collective-permute-start.3 = (bf16[1,1,128,512]{3,2,1,0:T(8,128)(2,1)S(1)}, bf16[1,1,128,512]{3,2,1,0:T(8,128)(2,1)S(1)}, u32[]{:S(2)}, u32[]{:S(2)}) collective-permute-start(bf16[1,1,128,512]{3,2,1,0:T(8,128)(2,1)S(1)} %get-tuple-element.20.refs_1_), channel_id=1, source_target_pairs={{0,2},{1,3},{2,4},{3,5},{4,6},{5,7},{6,8},{7,9},{8,10},{9,11},{10,... | collective-permute-start | bytes 393224 | tf_op jit(solution)/shard_map/ppermute | solution.py:319
  8.1 1.7 %collective-permute-done.2.refs_4_ = bf16[1,1,128,512]{3,2,1,0:T(8,128)(2,1)S(1)} collective-permute-done((bf16[1,1,128,512]{3,2,1,0:T(8,128)(2,1)S(1)}, bf16[1,1,128,512]{3,2,1,0:T(8,128)(2,1)S(1)}, u32[]{:S(2)}, u32[]{:S(2)}) %collective-permute-start.2) | collective-permute-done | bytes 131104 | tf_op jit(solution)/shard_map/ppermute | solution.py:313
  9.8 1.9 %collective-permute-start.4 = (bf16[1,1,128,512]{3,2,1,0:T(8,128)(2,1)S(1)}, bf16[1,1,128,512]{3,2,1,0:T(8,128)(2,1)S(1)}, u32[]{:S(2)}, u32[]{:S(2)}) collective-permute-start(bf16[1,1,128,512]{3,2,1,0:T(8,128)(2,1)S(1)} %collective-permute-done.2.refs_4_), channel_id=1, source_target_pairs={{2,3},{3,2},{4,5},{5,4},{6,7},{7,6},{8,9},{9,8},{10,11},{11,10},{1... | collective-permute-start | bytes 393224 | tf_op jit(solution)/shard_map/ppermute | solution.py:321
  11.7 0.0 collective-permute-done.1.refs_3_
  11.8 1.2 %collective-permute-start.5 = (bf16[1,1,128,512]{3,2,1,0:T(8,128)(2,1)S(1)}, bf16[1,1,128,512]{3,2,1,0:T(8,128)(2,1)S(1)}, u32[]{:S(2)}, u32[]{:S(2)}) collective-permute-start(bf16[1,1,128,512]{3,2,1,0:T(8,128)(2,1)S(1)} %collective-permute-done.1.refs_3_), channel_id=1, source_target_pairs={{1,3},{4,2},{3,5},{6,4},{5,7},{8,6},{7,9},{10,8},{9,11},{12,10},{1... | collective-permute-start | bytes 393224 | tf_op jit(solution)/shard_map/ppermute | solution.py:322
  12.9 0.0 collective-permute-done.6.got_ref.refs_2_
  13.0 0.1 collective-permute-start.7
  13.1 0.2 %collective-permute-done.refs_2_ = bf16[1,1,128,512]{3,2,1,0:T(8,128)(2,1)S(1)} collective-permute-done((bf16[1,1,128,512]{3,2,1,0:T(8,128)(2,1)S(1)}, bf16[1,1,128,512]{3,2,1,0:T(8,128)(2,1)S(1)}, u32[]{:S(2)}, u32[]{:S(2)}) %collective-permute-start) | collective-permute-done | bytes 131104 | tf_op jit(solution)/shard_map/ppermute | solution.py:318
  13.3 1.8 %collective-permute-done.3.refs_5_ = bf16[1,1,128,512]{3,2,1,0:T(8,128)(2,1)S(1)} collective-permute-done((bf16[1,1,128,512]{3,2,1,0:T(8,128)(2,1)S(1)}, bf16[1,1,128,512]{3,2,1,0:T(8,128)(2,1)S(1)}, u32[]{:S(2)}, u32[]{:S(2)}) %collective-permute-start.3) | collective-permute-done | bytes 131104 | tf_op jit(solution)/shard_map/ppermute | solution.py:319
  15.0 2.5 %attend_near.1 = (bf16[4,128,1024]{2,1,0:T(8,128)(2,1)S(1)}, f32[4,128,1024]{2,1,0:T(8,128)S(1)}, f32[4,1024]{1,0:T(4,128)S(1)}, f32[4,1024]{1,0:T(4,128)S(1)}) custom-call(bf16[544,128]{1,0:T(8,128)(2,1)S(1)} %get-tuple-element.17.mask_ref, bf16[1,128,4096]{2,1,0:T(8,128)(2,1)S(1)} %get-tuple-element.18.q_ref, ...), custom_call_target="tpu_custom_call" | custom-call | flops 805306368 | bytes 1048576 | tf_op jit(solution)/shard_map/attend_near/pallas_call | solution.py:341
  17.5 1.2 %collective-permute-done.7.refs_3_ = bf16[2,2,16,512]{3,2,1,0:T(8,128)(2,1)S(1)} collective-permute-done((bf16[2,2,16,512]{3,2,1,0:T(8,128)(2,1)S(1)}, bf16[2,2,16,512]{3,2,1,0:T(8,128)(2,1)S(1)}, u32[]{:S(2)}, u32[]{:S(2)}) %collective-permute-start.7) | collective-permute-done | bytes 65568 | tf_op jit(solution)/shard_map/ppermute | solution.py:291
  18.7 0.0 collective-permute-done.4.k_ref
  18.7 0.0 collective-permute-done.5.v_ref
  18.7 2.1 %attend_far.1 = bf16[1,128,4096]{2,1,0:T(8,128)(2,1)} custom-call(bf16[544,128]{1,0:T(8,128)(2,1)S(1)} %get-tuple-element.17.mask_ref, bf16[4,128,1024]{2,1,0:T(8,128)(2,1)S(1)} %get-tuple-element.21.qt_ref, bf16[1,1,128,512]{3,2,1,0:T(8,128)(2,1)S(1)} %collective-permute-done.4.k_ref, bf16[1,1,128,512]{3,2,1,0:T(8,128)(2,1)S(1)} %collective-permute-done.5.v_ref, ...), custom_call_target="tpu_custom_call" | custom-call | flops 268435456 | bytes 1048576 | tf_op jit(solution)/shard_map/attend_far/pallas_call | solution.py:350
  (1 shorter events, 0.0 us)
Async XLA Ops:
  1.5 8.3 %collective-permute-start.2 = (bf16[1,1,128,512]{3,2,1,0:T(8,128)(2,1)S(1)}, bf16[1,1,128,512]{3,2,1,0:T(8,128)(2,1)S(1)}, u32[]{:S(2)}, u32[]{:S(2)}) collective-permute-start(bf16[1,1,128,512]{3,2,1,0:T(8,128)(2,1)S(1)} %get-tuple-element.19.refs_0_), channel_id=1, source_target_pairs={{0,2},{1,3},{2,4},{3,5},{4,6},{5,7},{6,8},{7,9},{8,10},{9,11},{10,... | collective-permute-start | bytes 393224 | tf_op jit(solution)/shard_map/ppermute | solution.py:313
  4.6 7.2 %collective-permute-start.1 = (bf16[1,1,128,512]{3,2,1,0:T(8,128)(2,1)S(1)}, bf16[1,1,128,512]{3,2,1,0:T(8,128)(2,1)S(1)}, u32[]{:S(2)}, u32[]{:S(2)}) collective-permute-start(bf16[1,1,128,512]{3,2,1,0:T(8,128)(2,1)S(1)} %get-tuple-element.20.refs_1_), channel_id=1, source_target_pairs={{0,1},{1,4},{2,3},{3,6},{4,5},{5,8},{6,7},{7,10},{8,9},{9,12},{10,... | collective-permute-start | bytes 393224 | tf_op jit(solution)/shard_map/ppermute | solution.py:314
  6.1 6.9 %collective-permute-start.6 = (bf16[3,2,16,512]{3,2,1,0:T(8,128)(2,1)S(1)}, bf16[3,2,16,512]{3,2,1,0:T(8,128)(2,1)S(1)}, u32[]{:S(2)}, u32[]{:S(2)}) collective-permute-start(bf16[3,2,16,512]{3,2,1,0:T(8,128)(2,1)S(1)} %get-tuple-element.24), channel_id=1, source_target_pairs={{0,2},{1,3},{2,0},{3,1},{4,6},{5,7},{6,4},{7,5},{8,10},{9,11},{10,... | collective-permute-start | bytes 294920 | tf_op jit(solution)/shard_map/ppermute | solution.py:291
  6.1 7.1 %collective-permute-start = (bf16[1,1,128,512]{3,2,1,0:T(8,128)(2,1)S(1)}, bf16[1,1,128,512]{3,2,1,0:T(8,128)(2,1)S(1)}, u32[]{:S(2)}, u32[]{:S(2)}) collective-permute-start(bf16[1,1,128,512]{3,2,1,0:T(8,128)(2,1)S(1)} %get-tuple-element.19.refs_0_), channel_id=1, source_target_pairs={{0,1},{1,4},{2,3},{3,6},{4,5},{5,8},{6,7},{7,10},{8,9},{9,12},{10,... | collective-permute-start | bytes 393224 | tf_op jit(solution)/shard_map/ppermute | solution.py:318
  7.8 7.2 %collective-permute-start.3 = (bf16[1,1,128,512]{3,2,1,0:T(8,128)(2,1)S(1)}, bf16[1,1,128,512]{3,2,1,0:T(8,128)(2,1)S(1)}, u32[]{:S(2)}, u32[]{:S(2)}) collective-permute-start(bf16[1,1,128,512]{3,2,1,0:T(8,128)(2,1)S(1)} %get-tuple-element.20.refs_1_), channel_id=1, source_target_pairs={{0,2},{1,3},{2,4},{3,5},{4,6},{5,7},{6,8},{7,9},{8,10},{9,11},{10,... | collective-permute-start | bytes 393224 | tf_op jit(solution)/shard_map/ppermute | solution.py:319
  9.8 8.9 %collective-permute-start.4 = (bf16[1,1,128,512]{3,2,1,0:T(8,128)(2,1)S(1)}, bf16[1,1,128,512]{3,2,1,0:T(8,128)(2,1)S(1)}, u32[]{:S(2)}, u32[]{:S(2)}) collective-permute-start(bf16[1,1,128,512]{3,2,1,0:T(8,128)(2,1)S(1)} %collective-permute-done.2.refs_4_), channel_id=1, source_target_pairs={{2,3},{3,2},{4,5},{5,4},{6,7},{7,6},{8,9},{9,8},{10,11},{11,10},{1... | collective-permute-start | bytes 393224 | tf_op jit(solution)/shard_map/ppermute | solution.py:321
  11.8 6.9 %collective-permute-start.5 = (bf16[1,1,128,512]{3,2,1,0:T(8,128)(2,1)S(1)}, bf16[1,1,128,512]{3,2,1,0:T(8,128)(2,1)S(1)}, u32[]{:S(2)}, u32[]{:S(2)}) collective-permute-start(bf16[1,1,128,512]{3,2,1,0:T(8,128)(2,1)S(1)} %collective-permute-done.1.refs_3_), channel_id=1, source_target_pairs={{1,3},{4,2},{3,5},{6,4},{5,7},{8,6},{7,9},{10,8},{9,11},{12,10},{1... | collective-permute-start | bytes 393224 | tf_op jit(solution)/shard_map/ppermute | solution.py:322
  13.0 5.7 %collective-permute-start.7 = (bf16[2,2,16,512]{3,2,1,0:T(8,128)(2,1)S(1)}, bf16[2,2,16,512]{3,2,1,0:T(8,128)(2,1)S(1)}, u32[]{:S(2)}, u32[]{:S(2)}) collective-permute-start(bf16[2,2,16,512]{3,2,1,0:T(8,128)(2,1)S(1)} %relay_rows.1), channel_id=1, source_target_pairs={{0,1},{1,0},{2,3},{3,2},{4,5},{5,4},{6,7},{7,6},{8,9},{9,8},{10,11... | collective-permute-start | bytes 196616 | tf_op jit(solution)/shard_map/ppermute | solution.py:291

commit v5 on v4

--- a/solution.py
+++ b/solution.py
@@ -35,26 +35,44 @@
     return [(holder[s], d) for s, d in wanted]
 
 
-def segments_at(len_ref, positions):
-    def step(s, carry):
-        start, found = carry
-        out = []
-        for position, (seg, begin) in zip(positions, found):
-            reached = start <= position
-            out.append((jnp.where(reached, s, seg), jnp.where(reached, start, begin)))
-        return start + len_ref[0, s], out
+def segments_at(len_ref, positions, starts_of):
+    steps = len_ref.shape[1]
+    unroll = math.gcd(steps, 16)
+
+    def step(block, carry):
+        start, segs, begins = carry
+        for k in range(unroll):
+            s = block * unroll + k
+            reached = [start <= position for position in positions]
+            segs = [jnp.where(r, s, seg) for r, seg in zip(reached, segs)]
+            begins = [jnp.where(r, start, begin) for r, begin in zip(reached, begins)]
+            start = start + len_ref[0, s]
+        return start, segs, begins
 
     zero = jnp.int32(0)
-    steps = len_ref.shape[1]
-    return lax.fori_loop(0, steps, step, (zero, [(zero, zero)] * len(positions)))[1]
-
-
-def block_mask(first, hop, start_a, start_b, t):
-    key = lax.broadcasted_iota(jnp.int32, (t, t), 0) - hop * t
-    query = lax.broadcasted_iota(jnp.int32, (t, t), 1)
-    from_b = start_b - first
-    start = jnp.where(query >= from_b, from_b, start_a - first)
+    carry = (zero, [zero] * len(positions), [zero] * starts_of)
+    _, segs, begins = lax.fori_loop(0, steps // unroll, step, carry)
+    return segs, begins
+
+
+def block_mask(shape, hop, from_a, from_b):
+    key = lax.broadcasted_iota(jnp.int32, shape, 0) - hop * shape[0]
+    query = lax.broadcasted_iota(jnp.int32, shape, 1)
+    start = jnp.where(query >= from_b, from_b, from_a)
     return jnp.where((key >= start) & (key <= query), 0.0, FAR).astype(jnp.bfloat16)
+
+
+def all_masks(kinds, t, size, place_ref):
+    from_a, from_b = (place_ref[i][:1, :1] for i in (4, 5))
+    grp_count = lax.axis_size("grp")
+    ends = [jnp.broadcast_to(x, (t, t)) for x in (from_a, from_b)]
+    blocks = [block_mask((t, t), hop_of(k, grp_count), *ends) for k in kinds]
+    b = jnp.broadcast_to(from_b, (size, t))
+    is_b = (lax.broadcasted_iota(jnp.int32, (size, t), 1) >= b) & (b > 0)
+    blocks[-1:-1] = [
+        jnp.where(is_b, x, y).astype(jnp.bfloat16) for x, y in ((FAR, 0.0), (0.0, FAR))
+    ]
+    return blocks
 
 
 def hop_of(kind, grp_count):
@@ -64,33 +82,20 @@
     return (me - (me ^ kind[1])) & (grp_count - 1)
 
 
-def plan_kernel(
-    t,
-    kinds,
-    plane,
-    len_hbm,
-    task_hbm,
-    slot_hbm,
-    bank_hbm,
-    kv_hbm,
-    q_hbm,
-    mask_ref,
-    k_ref,
-    v_ref,
-    q_ref,
-    *refs,
-):
-    (len_ref, task_ref, slot_ref, bank_ref, sems) = refs[-5:]
+def plan_kernel(t, plane, *refs):
+    len_hbm, task_hbm, slot_hbm, bank_hbm, kv_hbm = refs[:5]
+    place_ref, k_ref, v_ref = refs[5:8]
+    out_refs = refs[8:-5]
+    len_ref, task_ref, slot_ref, bank_ref, sems = refs[-5:]
     pairs = (
         (len_hbm, len_ref),
         (task_hbm, task_ref),
         (slot_hbm, slot_ref),
+        (bank_hbm, bank_ref),
         (kv_hbm.at[pl.ds(0, 1)], k_ref),
         (kv_hbm.at[pl.ds(1, 1)], v_ref),
-        (bank_hbm, bank_ref),
-        (q_hbm, q_ref),
     )
-    copies = [pltpu.make_async_copy(a, b, sems.at[i]) for i, (a, b) in enumerate(pairs)]
+    copies = [pltpu.make_async_copy(x, y, sems.at[i]) for i, (x, y) in enumerate(pairs)]
     for copy in copies:
         copy.start()
     for copy in copies[:3]:
@@ -106,36 +111,29 @@
         across = me ^ 2
         groups = [[me, me + 1], [me ^ 1, (me ^ 1) + 1], [(across & 2) + k for k in range(3)]]
         positions += [(row_base + k) * t for group in groups for k in group]
-    found = segments_at(len_ref, positions)
-    (_, start_a), (_, start_b) = found[:2]
-    size = bank_ref.shape[2]
-    query = lax.broadcasted_iota(jnp.int32, (size, t), 1)
-    from_b = start_b - first
-    is_b = (query >= from_b) & (from_b > 0)
-    blocks = [block_mask(first, hop_of(k, grp_count), start_a, start_b, t) for k in kinds]
-    blocks[-1:-1] = [
-        jnp.where(is_b, a, b).astype(jnp.bfloat16) for a, b in ((FAR, 0.0), (0.0, FAR))
-    ]
-    mask_ref[...] = jnp.concatenate(blocks, axis=0)
-    for copy in copies[3:6]:
+    segs, begins = segments_at(len_ref, positions, 2)
+    for i, begin in enumerate(begins):
+        place_ref[4 + i] = jnp.full(place_ref.shape[1:], begin - first, jnp.int32)
+    if plane:
+        rows = [slot_ref[task_ref[0, seg]] for seg in segs[2:]]
+        for i, row in enumerate(rows[:4]):
+            place_ref[i] = jnp.full(place_ref.shape[1:], (row // held) ^ me, jnp.int32)
+        copies[3].wait()
+        for group, out_ref in zip(groups, out_refs):
+            for i in range(len(group)):
+                local = jnp.clip(rows.pop(0) - me * held, 0, held - 1)
+                for part in range(2):
+                    out_ref[i, part] = bank_ref[part, local]
+    for copy in copies[4 if plane else 3 :]:
         copy.wait()
-    if not plane:
-        copies[6].wait()
-        return
-    place_ref, out_refs = refs[0], refs[1:-5]
-    rows = [slot_ref[task_ref[0, seg]] for seg, _ in found[2:]]
-    for i, row in enumerate(rows[:4]):
-        place_ref[i] = jnp.full(place_ref.shape[1:], (row // held) ^ me, jnp.int32)
-    for group, out_ref in zip(groups, out_refs):
-        for i in range(len(group)):
-            local = jnp.clip(rows.pop(0) - me * held, 0, held - 1)
-            for part in range(2):
-                out_ref[i, part] = bank_ref[part, local]
-    copies[6].wait()
 
 
 def here(place_ref, i, place, shape):
     return jnp.broadcast_to(place_ref[i][:1, :1] == place, shape)
+
+
+def pass_kernel(in_ref, out_ref):
+    out_ref[...] = in_ref[...]
 
 
 def relay_kernel(place_ref, mine_ref, got_ref, out_ref):
@@ -182,17 +180,19 @@
     return slice(j * HD, (j + 1) * HD)
 
 
-def near_kernel(groups, mask_ref, q_ref, *refs):
-    kv_refs, (qt_ref, acc_ref, sum_ref, top_ref) = refs[:-4], refs[-4:]
-    masks = mask_ref[: len(kv_refs) // 2 * q_ref.shape[1], :]
-
-    def rows(part, j):
-        return jnp.concatenate([r[0, 0, :, lanes(j)] for r in kv_refs[part::2]], axis=0)
+def own_kernel(groups, kinds, size, place_ref, q_hbm, k_ref, v_ref, *refs):
+    mask_ref, qt_ref, acc_ref, sum_ref, top_ref, q_ref, sem = refs
+    copy = pltpu.make_async_copy(q_hbm, q_ref, sem)
+    copy.start()
+    t = q_ref.shape[1]
+    blocks = all_masks(kinds, t, size, place_ref)
+    mask_ref[...] = jnp.concatenate(blocks, axis=0)
+    copy.wait()
 
     def scored(j):
         q = jnp.concatenate([q_ref[0, :, lanes(j * groups + g)].T for g in range(groups)], axis=1)
         qt_ref[j] = q
-        return score(rows(0, j), masks, q)
+        return score(k_ref[0, 0, :, lanes(j)], blocks[0], q)
 
     def weighed(j, s):
         top = jnp.max(s, axis=0, keepdims=True) * SCALE
@@ -200,7 +200,7 @@
         return jnp.exp2(s * SCALE - top).astype(jnp.bfloat16)
 
     def mixed(j, w):
-        o = mix(rows(1, j), w)
+        o = mix(v_ref[0, 0, :, lanes(j)], w)
         acc_ref[j] = o[:HD]
         sum_ref[j : j + 1, :] = o[HD : HD + 1]
 
@@ -224,6 +224,23 @@
         finish(j, acc_ref[j], o[:HD], keep, sum_ref[j : j + 1, :] * keep + o[HD : HD + 1], top)
 
     staged(acc_ref.shape[0], scored, weighed, mixed)
+
+
+def near_kernel(mask_ref, qt_ref, *refs):
+    kv_refs, old, new = refs[:-6], refs[-6:-3], refs[-3:]
+    acc_ref, sum_ref, top_ref = new
+    t = mask_ref.shape[1]
+    count = len(kv_refs) // 2
+
+    def rows(part, j):
+        return jnp.concatenate([r[0, 0, :, lanes(j)] for r in kv_refs[part::2]], axis=0)
+
+    def finish(j, acc, more, keep, total, top):
+        acc_ref[j] = acc * keep + more
+        sum_ref[j : j + 1, :] = total
+        top_ref[j : j + 1, :] = top
+
+    merge(rows, mask_ref[t : (1 + count) * t, :], qt_ref, old, finish)
 
 
 def far_kernel(groups, plane, mask_ref, qt_ref, k_ref, v_ref, *refs):
@@ -290,30 +307,33 @@
     def flip(array, k):
         return lax.ppermute(array, "grp", [(i, i ^ k) for i in range(grp_count)])
 
-    def cost(blocks):
+    def cost(quarters):
         return pl.CostEstimate(
-            flops=4 * blocks * queries.size * t,
-            bytes_accessed=2 * queries.size,
-            transcendentals=blocks * queries.size,
+            flops=quarters * queries.size * t,
+            bytes_accessed=quarters * queries.size // 2,
+            transcendentals=quarters * queries.size // 4,
         )
 
     extra = [struct((4, 8, 128), jnp.int32)] + [rows_of(n) for n in (2, 2, 3)] if plane else []
     half = struct((1,) + keyvals.shape[1:], keyvals.dtype)
-    masks, keys, values, fetched, *planned = pl.pallas_call(
-        functools.partial(plan_kernel, t, kinds, plane),
-        out_shape=[struct((len(kinds) * t + 2 * row_shape[1], t), jnp.bfloat16)] + [half] * 2 + [struct(queries.shape, queries.dtype)] + extra,
-        in_specs=[HBM] * 6,
-        out_specs=[VMEM] * (4 + len(extra)),
-        scratch_shapes=[pltpu.SMEM(a.shape, a.dtype) for a in (seg_len, seg_task, task_slot)]
-        + [pltpu.VMEM(prefix_bank.shape, prefix_bank.dtype), pltpu.SemaphoreType.DMA((7,))],
+    arguments = (seg_len, seg_task, task_slot, prefix_bank, keyvals)
+    outputs = [struct((6, 8, 128), jnp.int32), half, half]
+    outputs += [rows_of(n) for n in (2, 2, 3)] if plane else []
+    place, keys, values, *planned = pl.pallas_call(
+        functools.partial(plan_kernel, t, plane),
+        out_shape=outputs,
+        in_specs=[HBM] * len(arguments),
+        out_specs=[VMEM] * len(outputs),
+        scratch_shapes=[pltpu.SMEM(a.shape, a.dtype) for a in arguments[:3]]
+        + [pltpu.VMEM(prefix_bank.shape, prefix_bank.dtype), pltpu.SemaphoreType.DMA((6,))],
         compiler_params=PARAMS,
         name="plan",
-    )(*(in_hbm(a) for a in (seg_len, seg_task, task_slot, prefix_bank, keyvals, queries)))
+    )(*(in_hbm(a) for a in arguments))
 
     side_keys = lax.ppermute(keys, AXES, side)
     near_values = lax.ppermute(values, AXES, near)
     if plane:
-        place, own_rows, near_rows, side_rows = planned
+        own_rows, near_rows, side_rows = planned
         got_rows = flip(side_rows, 2)
     near_keys = lax.ppermute(keys, AXES, near)
     side_values = lax.ppermute(values, AXES, side)
@@ -326,10 +346,19 @@
             in_specs=[VMEM] * 3,
             out_specs=VMEM,
             compiler_params=PARAMS,
-            cost_estimate=cost(16),
+            cost_estimate=cost(32),
             name="relay_rows",
         )(place, near_rows, got_rows)
-        prefix = [place, own_rows, got_rows, flip(relayed, 1)]
+        relayed = pl.pallas_call(
+            pass_kernel,
+            out_shape=rows_of(2),
+            in_specs=[VMEM],
+            out_specs=VMEM,
+            compiler_params=PARAMS,
+            cost_estimate=cost(4),
+            name="settle",
+        )(flip(relayed, 1))
+        prefix = [place, own_rows, got_rows, relayed]
     else:
         prefix = [fetch_prefix(seg_len, seg_task, task_slot, prefix_bank, t)]
         far_keys = lax.ppermute(keys, AXES, far)
@@ -337,16 +366,31 @@
 
     wide = struct((kv_heads, HD, groups * t), jnp.float32)
     flat = struct((kv_heads, groups * t), jnp.float32)
-    kv = [keys, values, near_keys, near_values, side_keys, side_values]
-    turned, *state = pl.pallas_call(
-        functools.partial(near_kernel, groups),
-        out_shape=[struct(wide.shape, queries.dtype), wide, flat, flat],
-        in_specs=[VMEM] * (2 + len(kv)),
-        out_specs=[VMEM] * 4,
+    masks, turned, *state = pl.pallas_call(
+        functools.partial(own_kernel, groups, kinds, row_shape[1]),
+        out_shape=[
+            struct((len(kinds) * t + 2 * row_shape[1], t), jnp.bfloat16),
+            struct(wide.shape, queries.dtype),
+            wide,
+            flat,
+            flat,
+        ],
+        in_specs=[VMEM, HBM, VMEM, VMEM],
+        out_specs=[VMEM] * 5,
+        scratch_shapes=[pltpu.VMEM(queries.shape, queries.dtype), pltpu.SemaphoreType.DMA],
         compiler_params=PARAMS,
-        cost_estimate=cost(3),
+        cost_estimate=cost(8),
+        name="attend_own",
+    )(place, in_hbm(queries), keys, values)
+    state = pl.pallas_call(
+        near_kernel,
+        out_shape=[wide, flat, flat],
+        in_specs=[VMEM] * 9,
+        out_specs=[VMEM] * 3,
+        compiler_params=PARAMS,
+        cost_estimate=cost(2),
         name="attend_near",
-    )(masks, fetched, *kv)
+    )(masks, turned, near_keys, near_values, side_keys, side_values, *state)
     return pl.pallas_call(
         functools.partial(far_kernel, groups, plane),
         out_shape=struct(queries.shape, queries.dtype),
@@ -357,7 +401,7 @@
             pltpu.SemaphoreType.DMA((kv_heads,)),
         ],
         compiler_params=PARAMS,
-        cost_estimate=cost(1),
+        cost_estimate=cost(4),
         name="attend_far",
     )(masks, turned, far_keys, far_values, *prefix, *state)
 

time: 20.9 us -> 20.6 us (0.986)
  waiting for transfers between devices: 4.86 us -> 3.25 us
  Pallas kernels: 6.16 us -> 7.35 us
    ppermute x1, waiting for transfers between devices: 1.75 us -> 0.01 us  [on_device(): side_values = lax.ppermute(values, AXES, side)]
    pallas_call x2 -> x4, Pallas kernels: 4.01 us -> 5.2 us  [the longest x1 2.23 us: on_device(): pl.pallas_call(functools.partial(own_kernel, groups, kinds, row_shape[1])...]
    ppermute x2, waiting for transfers between devices: 1.16 us -> 1.5 us  [flip(): return lax.ppermute(array, 'grp', [(i, i ^ k) for i in range(grp_count)])]
  transfers between devices with their start and end apart: 8 -> 8, of which waited for: 4 -> 2; matrix products, arithmetic and copies ran while one was open for 0% -> 0% of each run, Pallas kernels for 12% -> 20%
where the time goes in v5:
time: 20.6 us; the launch traced here: 20.4 us
  starting transfers between devices  9.73 us (47%)
  Pallas kernels  7.35 us (36%)
  waiting for transfers between devices  3.25 us (16%)
    ppermute x1, starting transfers between devices, on_device(): side_keys = lax.ppermute(keys, AXES, side)  3.03 us
    pallas_call x1, Pallas kernels, on_device(): pl.pallas_call(functools.partial(own_kernel, groups, kinds, row_shape[1])...  2.23 us
    pallas_call x1, Pallas kernels, on_device(): pl.pallas_call(functools.partial(far_kernel, groups, plane), out_shape=st...  2.11 us
    ppermute x1, starting transfers between devices, on_device(): far_keys = lax.ppermute(side_keys, AXES, compose_route(far, side))  1.93 us
    pallas_call x1, Pallas kernels, on_device(): pl.pallas_call(near_kernel, out_shape=[wide, flat, flat], in_specs=[VMEM]...  1.85 us
    ppermute x1, waiting for transfers between devices, on_device(): side_keys = lax.ppermute(keys, AXES, side)  1.72 us
    ppermute x1, starting transfers between devices, on_device(): near_keys = lax.ppermute(keys, AXES, near)  1.7 us
    ppermute x2, waiting for transfers between devices, flip(): return lax.ppermute(array, 'grp', [(i, i ^ k) for i in range(grp_count)])  1.5 us
  transfers between devices with their start and end apart: 8, of which 2 were waited for; matrix products, arithmetic and copies ran while one was open for 0% of the time, Pallas kernels for 20%

profile of v5, /device:TPU:0, one launch (start us, length us, event | category | flops | bytes accessed | tf_op | source)
XLA Modules:
  0.0 20.4 jit_solution(14937816921057710124)
XLA Ops:
  0.0 1.1 %plan.1 = (s32[6,8,128]{2,1,0:T(8,128)S(1)}, bf16[1,1,128,512]{3,2,1,0:T(8,128)(2,1)S(1)}, bf16[1,1,128,512]{3,2,1,0:T(8,128)(2,1)S(1)}, bf16[2,2,16,512]{3,2,1,...) custom-call(s32[1,16]{1,0:T(1,128)} %refs_0_.1, s32[1,16]{1,0:T(1,128)} %refs_1_.1, ...), custom_call_target="tpu_custom_call" | custom-call | tf_op jit(solution)/shard_map/plan/pallas_call | solution.py:322
  1.1 3.0 %collective-permute-start = (bf16[1,1,128,512]{3,2,1,0:T(8,128)(2,1)S(1)}, bf16[1,1,128,512]{3,2,1,0:T(8,128)(2,1)S(1)}, u32[]{:S(2)}, u32[]{:S(2)}) collective-permute-start(bf16[1,1,128,512]{3,2,1,0:T(8,128)(2,1)S(1)} %get-tuple-element.20.k_ref), channel_id=1, source_target_pairs={{0,2},{1,3},{2,4},{3,5},{4,6},{5,7},{6,8},{7,9},{8,10},{9,11},{10,... | collective-permute-start | bytes 393224 | tf_op jit(solution)/shard_map/ppermute | solution.py:333
  4.2 1.5 %collective-permute-start.2 = (bf16[1,1,128,512]{3,2,1,0:T(8,128)(2,1)S(1)}, bf16[1,1,128,512]{3,2,1,0:T(8,128)(2,1)S(1)}, u32[]{:S(2)}, u32[]{:S(2)}) collective-permute-start(bf16[1,1,128,512]{3,2,1,0:T(8,128)(2,1)S(1)} %get-tuple-element.21.v_ref), channel_id=1, source_target_pairs={{0,1},{1,4},{2,3},{3,6},{4,5},{5,8},{6,7},{7,10},{8,9},{9,12},{10,... | collective-permute-start | bytes 393224 | tf_op jit(solution)/shard_map/ppermute | solution.py:334
  5.6 0.1 collective-permute-start.4
  5.7 1.7 %collective-permute-start.6 = (bf16[1,1,128,512]{3,2,1,0:T(8,128)(2,1)S(1)}, bf16[1,1,128,512]{3,2,1,0:T(8,128)(2,1)S(1)}, u32[]{:S(2)}, u32[]{:S(2)}) collective-permute-start(bf16[1,1,128,512]{3,2,1,0:T(8,128)(2,1)S(1)} %get-tuple-element.20.k_ref), channel_id=1, source_target_pairs={{0,1},{1,4},{2,3},{3,6},{4,5},{5,8},{6,7},{7,10},{8,9},{9,12},{10,... | collective-permute-start | bytes 393224 | tf_op jit(solution)/shard_map/ppermute | solution.py:338
  7.4 0.3 %collective-permute-start.7 = (bf16[1,1,128,512]{3,2,1,0:T(8,128)(2,1)S(1)}, bf16[1,1,128,512]{3,2,1,0:T(8,128)(2,1)S(1)}, u32[]{:S(2)}, u32[]{:S(2)}) collective-permute-start(bf16[1,1,128,512]{3,2,1,0:T(8,128)(2,1)S(1)} %get-tuple-element.21.v_ref), channel_id=1, source_target_pairs={{0,2},{1,3},{2,4},{3,5},{4,6},{5,7},{6,8},{7,9},{8,10},{9,11},{10,... | collective-permute-start | bytes 393224 | tf_op jit(solution)/shard_map/ppermute | solution.py:339
  7.7 1.7 %collective-permute-done.refs_2_ = bf16[1,1,128,512]{3,2,1,0:T(8,128)(2,1)S(1)} collective-permute-done((bf16[1,1,128,512]{3,2,1,0:T(8,128)(2,1)S(1)}, bf16[1,1,128,512]{3,2,1,0:T(8,128)(2,1)S(1)}, u32[]{:S(2)}, u32[]{:S(2)}) %collective-permute-start) | collective-permute-done | bytes 131104 | tf_op jit(solution)/shard_map/ppermute | solution.py:333
  9.4 1.9 %collective-permute-start.1 = (bf16[1,1,128,512]{3,2,1,0:T(8,128)(2,1)S(1)}, bf16[1,1,128,512]{3,2,1,0:T(8,128)(2,1)S(1)}, u32[]{:S(2)}, u32[]{:S(2)}) collective-permute-start(bf16[1,1,128,512]{3,2,1,0:T(8,128)(2,1)S(1)} %collective-permute-done.refs_2_), channel_id=1, source_target_pairs={{2,3},{3,2},{4,5},{5,4},{6,7},{7,6},{8,9},{9,8},{10,11},{11,10},{1... | collective-permute-start | bytes 393224 | tf_op jit(solution)/shard_map/ppermute | solution.py:341
  11.3 0.0 collective-permute-done.2.refs_1_
  11.3 1.2 %collective-permute-start.3 = (bf16[1,1,128,512]{3,2,1,0:T(8,128)(2,1)S(1)}, bf16[1,1,128,512]{3,2,1,0:T(8,128)(2,1)S(1)}, u32[]{:S(2)}, u32[]{:S(2)}) collective-permute-start(bf16[1,1,128,512]{3,2,1,0:T(8,128)(2,1)S(1)} %collective-permute-done.2.refs_1_), channel_id=1, source_target_pairs={{1,3},{4,2},{3,5},{6,4},{5,7},{8,6},{7,9},{10,8},{9,11},{12,10},{1... | collective-permute-start | bytes 393224 | tf_op jit(solution)/shard_map/ppermute | solution.py:342
  12.5 0.0 collective-permute-done.4.got_ref.refs_2_
  12.6 0.1 collective-permute-start.5
  12.7 2.2 %attend_own.1 = (bf16[544,128]{1,0:T(8,128)(2,1)S(1)}, bf16[4,128,1024]{2,1,0:T(8,128)(2,1)S(1)}, f32[4,128,1024]{2,1,0:T(8,128)S(1)}, f32[4,1024]{1,0:T(4,128)S(1)}, f32[4,1024]{1,0:T(4,128)S(1)}) custom-call(s32[6,8,128]{2,1,0:T(8,128)S(1)} %get-tuple-element.19.place_ref.refs_0_, bf16[1,128,4096]{2,1,0:T(8,128)(2,1)} %q_hbm.1, ...), custom_call_target="tpu_custom_call" | custom-call | flops 536870912 | bytes 2097152 | tf_op jit(solution)/shard_map/attend_own/pallas_call | solution.py:369
  14.9 0.0 collective-permute-done.6.refs_0_
  14.9 0.0 collective-permute-done.7.refs_3_
  14.9 1.9 %attend_near.1 = (f32[4,128,1024]{2,1,0:T(8,128)S(1)}, f32[4,1024]{1,0:T(4,128)S(1)}, f32[4,1024]{1,0:T(4,128)S(1)}) custom-call(bf16[544,128]{1,0:T(8,128)(2,1)S(1)} %get-tuple-element.22.mask_ref, bf16[4,128,1024]{2,1,0:T(8,128)(2,1)S(1)} %get-tuple-element.23.qt_ref, bf16[1,1,128,512]{3,2,1,0:T(8,128)(2,1)S(1)} %collective-permute-done.6.refs_0_, ...), custom_call_target="tpu_custom_call" | custom-call | flops 134217728 | bytes 524288 | tf_op jit(solution)/shard_map/attend_near/pallas_call | solution.py:385
  16.8 1.5 %collective-permute-done.5.in_ref = bf16[2,2,16,512]{3,2,1,0:T(8,128)(2,1)S(1)} collective-permute-done((bf16[2,2,16,512]{3,2,1,0:T(8,128)(2,1)S(1)}, bf16[2,2,16,512]{3,2,1,0:T(8,128)(2,1)S(1)}, u32[]{:S(2)}, u32[]{:S(2)}) %collective-permute-start.5) | collective-permute-done | bytes 65568 | tf_op jit(solution)/shard_map/ppermute | solution.py:308
  18.3 0.0 collective-permute-done.1.k_ref
  18.3 0.0 collective-permute-done.3.v_ref
  18.3 2.1 %attend_far.1 = bf16[1,128,4096]{2,1,0:T(8,128)(2,1)} custom-call(bf16[544,128]{1,0:T(8,128)(2,1)S(1)} %get-tuple-element.22.mask_ref, bf16[4,128,1024]{2,1,0:T(8,128)(2,1)S(1)} %get-tuple-element.23.qt_ref, bf16[1,1,128,512]{3,2,1,0:T(8,128)(2,1)S(1)} %collective-permute-done.1.k_ref, bf16[1,1,128,512]{3,2,1,0:T(8,128)(2,1)S(1)} %collective-permute-done.3.v_ref, ...), custom_call_target="tpu_custom_call" | custom-call | flops 268435456 | bytes 1048576 | tf_op jit(solution)/shard_map/attend_far/pallas_call | solution.py:394
  (2 shorter events, 0.0 us)
Async XLA Ops:
  1.1 8.3 %collective-permute-start = (bf16[1,1,128,512]{3,2,1,0:T(8,128)(2,1)S(1)}, bf16[1,1,128,512]{3,2,1,0:T(8,128)(2,1)S(1)}, u32[]{:S(2)}, u32[]{:S(2)}) collective-permute-start(bf16[1,1,128,512]{3,2,1,0:T(8,128)(2,1)S(1)} %get-tuple-element.20.k_ref), channel_id=1, source_target_pairs={{0,2},{1,3},{2,4},{3,5},{4,6},{5,7},{6,8},{7,9},{8,10},{9,11},{10,... | collective-permute-start | bytes 393224 | tf_op jit(solution)/shard_map/ppermute | solution.py:333
  4.2 7.2 %collective-permute-start.2 = (bf16[1,1,128,512]{3,2,1,0:T(8,128)(2,1)S(1)}, bf16[1,1,128,512]{3,2,1,0:T(8,128)(2,1)S(1)}, u32[]{:S(2)}, u32[]{:S(2)}) collective-permute-start(bf16[1,1,128,512]{3,2,1,0:T(8,128)(2,1)S(1)} %get-tuple-element.21.v_ref), channel_id=1, source_target_pairs={{0,1},{1,4},{2,3},{3,6},{4,5},{5,8},{6,7},{7,10},{8,9},{9,12},{10,... | collective-permute-start | bytes 393224 | tf_op jit(solution)/shard_map/ppermute | solution.py:334
  5.6 6.9 %collective-permute-start.4 = (bf16[3,2,16,512]{3,2,1,0:T(8,128)(2,1)S(1)}, bf16[3,2,16,512]{3,2,1,0:T(8,128)(2,1)S(1)}, u32[]{:S(2)}, u32[]{:S(2)}) collective-permute-start(bf16[3,2,16,512]{3,2,1,0:T(8,128)(2,1)S(1)} %get-tuple-element.25), channel_id=1, source_target_pairs={{0,2},{1,3},{2,0},{3,1},{4,6},{5,7},{6,4},{7,5},{8,10},{9,11},{10,... | collective-permute-start | bytes 294920 | tf_op jit(solution)/shard_map/ppermute | solution.py:308
  5.7 9.2 %collective-permute-start.6 = (bf16[1,1,128,512]{3,2,1,0:T(8,128)(2,1)S(1)}, bf16[1,1,128,512]{3,2,1,0:T(8,128)(2,1)S(1)}, u32[]{:S(2)}, u32[]{:S(2)}) collective-permute-start(bf16[1,1,128,512]{3,2,1,0:T(8,128)(2,1)S(1)} %get-tuple-element.20.k_ref), channel_id=1, source_target_pairs={{0,1},{1,4},{2,3},{3,6},{4,5},{5,8},{6,7},{7,10},{8,9},{9,12},{10,... | collective-permute-start | bytes 393224 | tf_op jit(solution)/shard_map/ppermute | solution.py:338
  7.4 7.5 %collective-permute-start.7 = (bf16[1,1,128,512]{3,2,1,0:T(8,128)(2,1)S(1)}, bf16[1,1,128,512]{3,2,1,0:T(8,128)(2,1)S(1)}, u32[]{:S(2)}, u32[]{:S(2)}) collective-permute-start(bf16[1,1,128,512]{3,2,1,0:T(8,128)(2,1)S(1)} %get-tuple-element.21.v_ref), channel_id=1, source_target_pairs={{0,2},{1,3},{2,4},{3,5},{4,6},{5,7},{6,8},{7,9},{8,10},{9,11},{10,... | collective-permute-start | bytes 393224 | tf_op jit(solution)/shard_map/ppermute | solution.py:339
  9.4 8.9 %collective-permute-start.1 = (bf16[1,1,128,512]{3,2,1,0:T(8,128)(2,1)S(1)}, bf16[1,1,128,512]{3,2,1,0:T(8,128)(2,1)S(1)}, u32[]{:S(2)}, u32[]{:S(2)}) collective-permute-start(bf16[1,1,128,512]{3,2,1,0:T(8,128)(2,1)S(1)} %collective-permute-done.refs_2_), channel_id=1, source_target_pairs={{2,3},{3,2},{4,5},{5,4},{6,7},{7,6},{8,9},{9,8},{10,11},{11,10},{1... | collective-permute-start | bytes 393224 | tf_op jit(solution)/shard_map/ppermute | solution.py:341
  11.3 6.9 %collective-permute-start.3 = (bf16[1,1,128,512]{3,2,1,0:T(8,128)(2,1)S(1)}, bf16[1,1,128,512]{3,2,1,0:T(8,128)(2,1)S(1)}, u32[]{:S(2)}, u32[]{:S(2)}) collective-permute-start(bf16[1,1,128,512]{3,2,1,0:T(8,128)(2,1)S(1)} %collective-permute-done.2.refs_1_), channel_id=1, source_target_pairs={{1,3},{4,2},{3,5},{6,4},{5,7},{8,6},{7,9},{10,8},{9,11},{12,10},{1... | collective-permute-start | bytes 393224 | tf_op jit(solution)/shard_map/ppermute | solution.py:342
  12.6 5.7 %collective-permute-start.5 = (bf16[2,2,16,512]{3,2,1,0:T(8,128)(2,1)S(1)}, bf16[2,2,16,512]{3,2,1,0:T(8,128)(2,1)S(1)}, u32[]{:S(2)}, u32[]{:S(2)}) collective-permute-start(bf16[2,2,16,512]{3,2,1,0:T(8,128)(2,1)S(1)} %relay_rows.1), channel_id=1, source_target_pairs={{0,1},{1,0},{2,3},{3,2},{4,5},{5,4},{6,7},{7,6},{8,9},{9,8},{10,11... | collective-permute-start | bytes 196616 | tf_op jit(solution)/shard_map/ppermute | solution.py:308

commit v6 on v5

--- a/solution.py
+++ b/solution.py
@@ -243,7 +243,7 @@
     merge(rows, mask_ref[t : (1 + count) * t, :], qt_ref, old, finish)
 
 
-def far_kernel(groups, plane, mask_ref, qt_ref, k_ref, v_ref, *refs):
+def far_kernel(groups, plane, kind, mask_ref, qt_ref, k_ref, v_ref, *refs):
     prefix_refs, old, (out_hbm, out_ref, sems) = refs[:-6], refs[-6:-3], refs[-3:]
     t = mask_ref.shape[1]
     size = prefix_refs[-1].shape[2]
@@ -257,28 +257,40 @@
                 value = jnp.where(here(place_ref, slot, 2, value.shape), got, value)
                 value = jnp.where(here(place_ref, slot, 0, value.shape), own_ref[slot, part], value)
             picked[part].append(value)
-    copies = []
-
-    def rows(part, j):
-        block = (k_ref, v_ref)[part][0, 0, :, lanes(j)]
-        return jnp.concatenate([p[:, lanes(j)] for p in picked[part]] + [block], axis=0)
-
-    def finish(j, acc, more, keep, total, top):
-        part = 1.0 / total
-        done = acc * (keep * part) + more * part
-        for g in range(groups):
-            out_ref[0, :, lanes(j * groups + g)] = (
-                done[:, g * t : (g + 1) * t].T.astype(out_ref.dtype)
+
+    def attend_to(with_block):
+        copies = []
+
+        def rows(part, j):
+            parts = [p[:, lanes(j)] for p in picked[part]]
+            if with_block:
+                parts.append((k_ref, v_ref)[part][0, 0, :, lanes(j)])
+            return jnp.concatenate(parts, axis=0)
+
+        def finish(j, acc, more, keep, total, top):
+            part = 1.0 / total
+            done = acc * (keep * part) + more * part
+            for g in range(groups):
+                out_ref[0, :, lanes(j * groups + g)] = (
+                    done[:, g * t : (g + 1) * t].T.astype(out_ref.dtype)
+                )
+            cols = pl.ds(j * groups * HD, groups * HD)
+            copies.append(
+                pltpu.make_async_copy(out_ref.at[:, :, cols], out_hbm.at[:, :, cols], sems.at[j])
             )
-        cols = pl.ds(j * groups * HD, groups * HD)
-        copies.append(
-            pltpu.make_async_copy(out_ref.at[:, :, cols], out_hbm.at[:, :, cols], sems.at[j])
-        )
-        copies[-1].start()
-
-    merge(rows, mask_ref[mask_ref.shape[0] - t - 2 * size :, :], qt_ref, old, finish)
-    for copy in copies:
-        copy.wait()
+            copies[-1].start()
+
+        start = mask_ref.shape[0] - t - 2 * size
+        count = 2 * size + (t if with_block else 0)
+        merge(rows, mask_ref[start : start + count, :], qt_ref, old, finish)
+        for copy in copies:
+            copy.wait()
+
+    grp_count = lax.axis_size("grp")
+    shard = lax.axis_index("ctx") * grp_count + lax.axis_index("grp")
+    exists = shard >= hop_of(kind, grp_count)
+    pl.when(exists)(functools.partial(attend_to, True))
+    pl.when(jnp.logical_not(exists))(functools.partial(attend_to, False))
 
 
 def on_device(queries, keyvals, seg_len, seg_task, task_slot, prefix_bank):
@@ -392,7 +404,7 @@
         name="attend_near",
     )(masks, turned, near_keys, near_values, side_keys, side_values, *state)
     return pl.pallas_call(
-        functools.partial(far_kernel, groups, plane),
+        functools.partial(far_kernel, groups, plane, kinds[-1]),
         out_shape=struct(queries.shape, queries.dtype),
         in_specs=[VMEM] * (7 + len(prefix)),
         out_specs=HBM,

time: 20.6 us -> 20.3 us (0.985)
  Pallas kernels: 7.35 us -> 7.12 us
    pallas_call x1, Pallas kernels: 2.11 us -> 1.87 us  [on_device(): pl.pallas_call(functools.partial(far_kernel, groups, plane, kinds[-1]), o...]
where the time goes in v6:
time: 20.3 us; the launch traced here: 20.2 us
  starting transfers between devices  9.73 us (48%)
  Pallas kernels  7.12 us (35%)
  waiting for transfers between devices  3.25 us (16%)
    ppermute x1, starting transfers between devices, on_device(): side_keys = lax.ppermute(keys, AXES, side)  3.03 us
    pallas_call x1, Pallas kernels, on_device(): pl.pallas_call(functools.partial(own_kernel, groups, kinds, row_shape[1])...  2.23 us
    ppermute x1, starting transfers between devices, on_device(): far_keys = lax.ppermute(side_keys, AXES, compose_route(far, side))  1.93 us
    pallas_call x1, Pallas kernels, on_device(): pl.pallas_call(functools.partial(far_kernel, groups, plane, kinds[-1]), o...  1.87 us
    pallas_call x1, Pallas kernels, on_device(): pl.pallas_call(near_kernel, out_shape=[wide, flat, flat], in_specs=[VMEM]...  1.85 us
    ppermute x1, waiting for transfers between devices, on_device(): side_keys = lax.ppermute(keys, AXES, side)  1.72 us
    ppermute x1, starting transfers between devices, on_device(): near_keys = lax.ppermute(keys, AXES, near)  1.7 us
    ppermute x2, waiting for transfers between devices, flip(): return lax.ppermute(array, 'grp', [(i, i ^ k) for i in range(grp_count)])  1.5 us
  transfers between devices with their start and end apart: 8, of which 2 were waited for; matrix products, arithmetic and copies ran while one was open for 0% of the time, Pallas kernels for 20%

profile of v6, /device:TPU:0, one launch (start us, length us, event | category | flops | bytes accessed | tf_op | source)
XLA Modules:
  0.0 20.2 jit_solution(8567464495043835414)
XLA Ops:
  0.0 1.1 %plan.1 = (s32[6,8,128]{2,1,0:T(8,128)S(1)}, bf16[1,1,128,512]{3,2,1,0:T(8,128)(2,1)S(1)}, bf16[1,1,128,512]{3,2,1,0:T(8,128)(2,1)S(1)}, bf16[2,2,16,512]{3,2,1,...) custom-call(s32[1,16]{1,0:T(1,128)} %refs_0_.1, s32[1,16]{1,0:T(1,128)} %refs_1_.1, ...), custom_call_target="tpu_custom_call" | custom-call | tf_op jit(solution)/shard_map/plan/pallas_call | solution.py:334
  1.1 3.0 %collective-permute-start = (bf16[1,1,128,512]{3,2,1,0:T(8,128)(2,1)S(1)}, bf16[1,1,128,512]{3,2,1,0:T(8,128)(2,1)S(1)}, u32[]{:S(2)}, u32[]{:S(2)}) collective-permute-start(bf16[1,1,128,512]{3,2,1,0:T(8,128)(2,1)S(1)} %get-tuple-element.20.k_ref), channel_id=1, source_target_pairs={{0,2},{1,3},{2,4},{3,5},{4,6},{5,7},{6,8},{7,9},{8,10},{9,11},{10,... | collective-permute-start | bytes 393224 | tf_op jit(solution)/shard_map/ppermute | solution.py:345
  4.2 1.5 %collective-permute-start.2 = (bf16[1,1,128,512]{3,2,1,0:T(8,128)(2,1)S(1)}, bf16[1,1,128,512]{3,2,1,0:T(8,128)(2,1)S(1)}, u32[]{:S(2)}, u32[]{:S(2)}) collective-permute-start(bf16[1,1,128,512]{3,2,1,0:T(8,128)(2,1)S(1)} %get-tuple-element.21.v_ref), channel_id=1, source_target_pairs={{0,1},{1,4},{2,3},{3,6},{4,5},{5,8},{6,7},{7,10},{8,9},{9,12},{10,... | collective-permute-start | bytes 393224 | tf_op jit(solution)/shard_map/ppermute | solution.py:346
  5.6 0.1 collective-permute-start.4
  5.7 1.7 %collective-permute-start.6 = (bf16[1,1,128,512]{3,2,1,0:T(8,128)(2,1)S(1)}, bf16[1,1,128,512]{3,2,1,0:T(8,128)(2,1)S(1)}, u32[]{:S(2)}, u32[]{:S(2)}) collective-permute-start(bf16[1,1,128,512]{3,2,1,0:T(8,128)(2,1)S(1)} %get-tuple-element.20.k_ref), channel_id=1, source_target_pairs={{0,1},{1,4},{2,3},{3,6},{4,5},{5,8},{6,7},{7,10},{8,9},{9,12},{10,... | collective-permute-start | bytes 393224 | tf_op jit(solution)/shard_map/ppermute | solution.py:350
  7.4 0.3 %collective-permute-start.7 = (bf16[1,1,128,512]{3,2,1,0:T(8,128)(2,1)S(1)}, bf16[1,1,128,512]{3,2,1,0:T(8,128)(2,1)S(1)}, u32[]{:S(2)}, u32[]{:S(2)}) collective-permute-start(bf16[1,1,128,512]{3,2,1,0:T(8,128)(2,1)S(1)} %get-tuple-element.21.v_ref), channel_id=1, source_target_pairs={{0,2},{1,3},{2,4},{3,5},{4,6},{5,7},{6,8},{7,9},{8,10},{9,11},{10,... | collective-permute-start | bytes 393224 | tf_op jit(solution)/shard_map/ppermute | solution.py:351
  7.7 1.7 %collective-permute-done.refs_2_ = bf16[1,1,128,512]{3,2,1,0:T(8,128)(2,1)S(1)} collective-permute-done((bf16[1,1,128,512]{3,2,1,0:T(8,128)(2,1)S(1)}, bf16[1,1,128,512]{3,2,1,0:T(8,128)(2,1)S(1)}, u32[]{:S(2)}, u32[]{:S(2)}) %collective-permute-start) | collective-permute-done | bytes 131104 | tf_op jit(solution)/shard_map/ppermute | solution.py:345
  9.4 1.9 %collective-permute-start.1 = (bf16[1,1,128,512]{3,2,1,0:T(8,128)(2,1)S(1)}, bf16[1,1,128,512]{3,2,1,0:T(8,128)(2,1)S(1)}, u32[]{:S(2)}, u32[]{:S(2)}) collective-permute-start(bf16[1,1,128,512]{3,2,1,0:T(8,128)(2,1)S(1)} %collective-permute-done.refs_2_), channel_id=1, source_target_pairs={{2,3},{3,2},{4,5},{5,4},{6,7},{7,6},{8,9},{9,8},{10,11},{11,10},{1... | collective-permute-start | bytes 393224 | tf_op jit(solution)/shard_map/ppermute | solution.py:353
  11.3 0.0 collective-permute-done.2.refs_1_
  11.3 1.2 %collective-permute-start.3 = (bf16[1,1,128,512]{3,2,1,0:T(8,128)(2,1)S(1)}, bf16[1,1,128,512]{3,2,1,0:T(8,128)(2,1)S(1)}, u32[]{:S(2)}, u32[]{:S(2)}) collective-permute-start(bf16[1,1,128,512]{3,2,1,0:T(8,128)(2,1)S(1)} %collective-permute-done.2.refs_1_), channel_id=1, source_target_pairs={{1,3},{4,2},{3,5},{6,4},{5,7},{8,6},{7,9},{10,8},{9,11},{12,10},{1... | collective-permute-start | bytes 393224 | tf_op jit(solution)/shard_map/ppermute | solution.py:354
  12.5 0.0 collective-permute-done.4.got_ref.refs_2_
  12.6 0.1 collective-permute-start.5
  12.7 2.2 %attend_own.1 = (bf16[544,128]{1,0:T(8,128)(2,1)S(1)}, bf16[4,128,1024]{2,1,0:T(8,128)(2,1)S(1)}, f32[4,128,1024]{2,1,0:T(8,128)S(1)}, f32[4,1024]{1,0:T(4,128)S(1)}, f32[4,1024]{1,0:T(4,128)S(1)}) custom-call(s32[6,8,128]{2,1,0:T(8,128)S(1)} %get-tuple-element.19.place_ref.refs_0_, bf16[1,128,4096]{2,1,0:T(8,128)(2,1)} %q_hbm.1, ...), custom_call_target="tpu_custom_call" | custom-call | flops 536870912 | bytes 2097152 | tf_op jit(solution)/shard_map/attend_own/pallas_call | solution.py:381
  14.9 0.0 collective-permute-done.6.refs_0_
  14.9 0.0 collective-permute-done.7.refs_3_
  14.9 1.9 %attend_near.1 = (f32[4,128,1024]{2,1,0:T(8,128)S(1)}, f32[4,1024]{1,0:T(4,128)S(1)}, f32[4,1024]{1,0:T(4,128)S(1)}) custom-call(bf16[544,128]{1,0:T(8,128)(2,1)S(1)} %get-tuple-element.22.mask_ref, bf16[4,128,1024]{2,1,0:T(8,128)(2,1)S(1)} %get-tuple-element.23.qt_ref, bf16[1,1,128,512]{3,2,1,0:T(8,128)(2,1)S(1)} %collective-permute-done.6.refs_0_, ...), custom_call_target="tpu_custom_call" | custom-call | flops 134217728 | bytes 524288 | tf_op jit(solution)/shard_map/attend_near/pallas_call | solution.py:397
  16.8 1.5 %collective-permute-done.5.in_ref = bf16[2,2,16,512]{3,2,1,0:T(8,128)(2,1)S(1)} collective-permute-done((bf16[2,2,16,512]{3,2,1,0:T(8,128)(2,1)S(1)}, bf16[2,2,16,512]{3,2,1,0:T(8,128)(2,1)S(1)}, u32[]{:S(2)}, u32[]{:S(2)}) %collective-permute-start.5) | collective-permute-done | bytes 65568 | tf_op jit(solution)/shard_map/ppermute | solution.py:320
  18.3 0.0 collective-permute-done.1.k_ref
  18.3 0.0 collective-permute-done.3.v_ref
  18.3 1.9 %attend_far.1 = bf16[1,128,4096]{2,1,0:T(8,128)(2,1)} custom-call(bf16[544,128]{1,0:T(8,128)(2,1)S(1)} %get-tuple-element.22.mask_ref, bf16[4,128,1024]{2,1,0:T(8,128)(2,1)S(1)} %get-tuple-element.23.qt_ref, bf16[1,1,128,512]{3,2,1,0:T(8,128)(2,1)S(1)} %collective-permute-done.1.k_ref, bf16[1,1,128,512]{3,2,1,0:T(8,128)(2,1)S(1)} %collective-permute-done.3.v_ref, ...), custom_call_target="tpu_custom_call" | custom-call | flops 268435456 | bytes 1048576 | tf_op jit(solution)/shard_map/attend_far/pallas_call | solution.py:406
  (2 shorter events, 0.0 us)
Async XLA Ops:
  1.1 8.3 %collective-permute-start = (bf16[1,1,128,512]{3,2,1,0:T(8,128)(2,1)S(1)}, bf16[1,1,128,512]{3,2,1,0:T(8,128)(2,1)S(1)}, u32[]{:S(2)}, u32[]{:S(2)}) collective-permute-start(bf16[1,1,128,512]{3,2,1,0:T(8,128)(2,1)S(1)} %get-tuple-element.20.k_ref), channel_id=1, source_target_pairs={{0,2},{1,3},{2,4},{3,5},{4,6},{5,7},{6,8},{7,9},{8,10},{9,11},{10,... | collective-permute-start | bytes 393224 | tf_op jit(solution)/shard_map/ppermute | solution.py:345
  4.2 7.2 %collective-permute-start.2 = (bf16[1,1,128,512]{3,2,1,0:T(8,128)(2,1)S(1)}, bf16[1,1,128,512]{3,2,1,0:T(8,128)(2,1)S(1)}, u32[]{:S(2)}, u32[]{:S(2)}) collective-permute-start(bf16[1,1,128,512]{3,2,1,0:T(8,128)(2,1)S(1)} %get-tuple-element.21.v_ref), channel_id=1, source_target_pairs={{0,1},{1,4},{2,3},{3,6},{4,5},{5,8},{6,7},{7,10},{8,9},{9,12},{10,... | collective-permute-start | bytes 393224 | tf_op jit(solution)/shard_map/ppermute | solution.py:346
  5.6 6.9 %collective-permute-start.4 = (bf16[3,2,16,512]{3,2,1,0:T(8,128)(2,1)S(1)}, bf16[3,2,16,512]{3,2,1,0:T(8,128)(2,1)S(1)}, u32[]{:S(2)}, u32[]{:S(2)}) collective-permute-start(bf16[3,2,16,512]{3,2,1,0:T(8,128)(2,1)S(1)} %get-tuple-element.25), channel_id=1, source_target_pairs={{0,2},{1,3},{2,0},{3,1},{4,6},{5,7},{6,4},{7,5},{8,10},{9,11},{10,... | collective-permute-start | bytes 294920 | tf_op jit(solution)/shard_map/ppermute | solution.py:320
  5.7 9.2 %collective-permute-start.6 = (bf16[1,1,128,512]{3,2,1,0:T(8,128)(2,1)S(1)}, bf16[1,1,128,512]{3,2,1,0:T(8,128)(2,1)S(1)}, u32[]{:S(2)}, u32[]{:S(2)}) collective-permute-start(bf16[1,1,128,512]{3,2,1,0:T(8,128)(2,1)S(1)} %get-tuple-element.20.k_ref), channel_id=1, source_target_pairs={{0,1},{1,4},{2,3},{3,6},{4,5},{5,8},{6,7},{7,10},{8,9},{9,12},{10,... | collective-permute-start | bytes 393224 | tf_op jit(solution)/shard_map/ppermute | solution.py:350
  7.4 7.5 %collective-permute-start.7 = (bf16[1,1,128,512]{3,2,1,0:T(8,128)(2,1)S(1)}, bf16[1,1,128,512]{3,2,1,0:T(8,128)(2,1)S(1)}, u32[]{:S(2)}, u32[]{:S(2)}) collective-permute-start(bf16[1,1,128,512]{3,2,1,0:T(8,128)(2,1)S(1)} %get-tuple-element.21.v_ref), channel_id=1, source_target_pairs={{0,2},{1,3},{2,4},{3,5},{4,6},{5,7},{6,8},{7,9},{8,10},{9,11},{10,... | collective-permute-start | bytes 393224 | tf_op jit(solution)/shard_map/ppermute | solution.py:351
  9.4 8.9 %collective-permute-start.1 = (bf16[1,1,128,512]{3,2,1,0:T(8,128)(2,1)S(1)}, bf16[1,1,128,512]{3,2,1,0:T(8,128)(2,1)S(1)}, u32[]{:S(2)}, u32[]{:S(2)}) collective-permute-start(bf16[1,1,128,512]{3,2,1,0:T(8,128)(2,1)S(1)} %collective-permute-done.refs_2_), channel_id=1, source_target_pairs={{2,3},{3,2},{4,5},{5,4},{6,7},{7,6},{8,9},{9,8},{10,11},{11,10},{1... | collective-permute-start | bytes 393224 | tf_op jit(solution)/shard_map/ppermute | solution.py:353
  11.3 6.9 %collective-permute-start.3 = (bf16[1,1,128,512]{3,2,1,0:T(8,128)(2,1)S(1)}, bf16[1,1,128,512]{3,2,1,0:T(8,128)(2,1)S(1)}, u32[]{:S(2)}, u32[]{:S(2)}) collective-permute-start(bf16[1,1,128,512]{3,2,1,0:T(8,128)(2,1)S(1)} %collective-permute-done.2.refs_1_), channel_id=1, source_target_pairs={{1,3},{4,2},{3,5},{6,4},{5,7},{8,6},{7,9},{10,8},{9,11},{12,10},{1... | collective-permute-start | bytes 393224 | tf_op jit(solution)/shard_map/ppermute | solution.py:354
  12.6 5.7 %collective-permute-start.5 = (bf16[2,2,16,512]{3,2,1,0:T(8,128)(2,1)S(1)}, bf16[2,2,16,512]{3,2,1,0:T(8,128)(2,1)S(1)}, u32[]{:S(2)}, u32[]{:S(2)}) collective-permute-start(bf16[2,2,16,512]{3,2,1,0:T(8,128)(2,1)S(1)} %relay_rows.1), channel_id=1, source_target_pairs={{0,1},{1,0},{2,3},{3,2},{4,5},{5,4},{6,7},{7,6},{8,9},{9,8},{10,11... | collective-permute-start | bytes 196616 | tf_op jit(solution)/shard_map/ppermute | solution.py:320

commit v7 on v6

--- a/solution.py
+++ b/solution.py
@@ -163,7 +163,11 @@
 
 def score(keys, masks, q):
     t = masks.shape[1]
-    ones = jnp.concatenate([eye(t)] * (q.shape[1] // t), axis=1)
+    groups = q.shape[1] // t
+    if keys.shape[0] < t:
+        s = jnp.dot(keys, q, preferred_element_type=jnp.float32)
+        return s + jnp.concatenate([masks.astype(jnp.float32)] * groups, axis=1)
+    ones = jnp.concatenate([eye(t)] * groups, axis=1)
     return jnp.dot(
         jnp.concatenate([keys, masks], axis=1),
         jnp.concatenate([q, ones], axis=0),

time: 20.3 us -> 20.2 us (level)
  transfers between devices with their start and end apart: 8 -> 8, of which waited for: 2 -> 2; matrix products, arithmetic and copies ran while one was open for 0% -> 0% of each run, Pallas kernels for 20% -> 21%
where the time goes in v7:
time: 20.2 us; the launch traced here: 20.1 us
  starting transfers between devices  9.73 us (48%)
  Pallas kernels  7.03 us (35%)
  waiting for transfers between devices  3.25 us (16%)
    ppermute x1, starting transfers between devices, on_device(): side_keys = lax.ppermute(keys, AXES, side)  3.03 us
    pallas_call x1, Pallas kernels, on_device(): pl.pallas_call(functools.partial(own_kernel, groups, kinds, row_shape[1])...  2.23 us
    ppermute x1, starting transfers between devices, on_device(): far_keys = lax.ppermute(side_keys, AXES, compose_route(far, side))  1.93 us
    pallas_call x1, Pallas kernels, on_device(): pl.pallas_call(near_kernel, out_shape=[wide, flat, flat], in_specs=[VMEM]...  1.85 us
    pallas_call x1, Pallas kernels, on_device(): pl.pallas_call(functools.partial(far_kernel, groups, plane, kinds[-1]), o...  1.79 us
    ppermute x1, waiting for transfers between devices, on_device(): side_keys = lax.ppermute(keys, AXES, side)  1.72 us
    ppermute x1, starting transfers between devices, on_device(): near_keys = lax.ppermute(keys, AXES, near)  1.7 us
    ppermute x2, waiting for transfers between devices, flip(): return lax.ppermute(array, 'grp', [(i, i ^ k) for i in range(grp_count)])  1.5 us
  transfers between devices with their start and end apart: 8, of which 2 were waited for; matrix products, arithmetic and copies ran while one was open for 0% of the time, Pallas kernels for 21%

profile of v7, /device:TPU:0, one launch (start us, length us, event | category | flops | bytes accessed | tf_op | source)
XLA Modules:
  0.0 20.1 jit_solution(16083655939966070674)
XLA Ops:
  0.0 1.1 %plan.1 = (s32[6,8,128]{2,1,0:T(8,128)S(1)}, bf16[1,1,128,512]{3,2,1,0:T(8,128)(2,1)S(1)}, bf16[1,1,128,512]{3,2,1,0:T(8,128)(2,1)S(1)}, bf16[2,2,16,512]{3,2,1,...) custom-call(s32[1,16]{1,0:T(1,128)} %refs_0_.1, s32[1,16]{1,0:T(1,128)} %refs_1_.1, ...), custom_call_target="tpu_custom_call" | custom-call | tf_op jit(solution)/shard_map/plan/pallas_call | solution.py:338
  1.1 3.0 %collective-permute-start = (bf16[1,1,128,512]{3,2,1,0:T(8,128)(2,1)S(1)}, bf16[1,1,128,512]{3,2,1,0:T(8,128)(2,1)S(1)}, u32[]{:S(2)}, u32[]{:S(2)}) collective-permute-start(bf16[1,1,128,512]{3,2,1,0:T(8,128)(2,1)S(1)} %get-tuple-element.20.k_ref), channel_id=1, source_target_pairs={{0,2},{1,3},{2,4},{3,5},{4,6},{5,7},{6,8},{7,9},{8,10},{9,11},{10,... | collective-permute-start | bytes 393224 | tf_op jit(solution)/shard_map/ppermute | solution.py:349
  4.2 1.5 %collective-permute-start.2 = (bf16[1,1,128,512]{3,2,1,0:T(8,128)(2,1)S(1)}, bf16[1,1,128,512]{3,2,1,0:T(8,128)(2,1)S(1)}, u32[]{:S(2)}, u32[]{:S(2)}) collective-permute-start(bf16[1,1,128,512]{3,2,1,0:T(8,128)(2,1)S(1)} %get-tuple-element.21.v_ref), channel_id=1, source_target_pairs={{0,1},{1,4},{2,3},{3,6},{4,5},{5,8},{6,7},{7,10},{8,9},{9,12},{10,... | collective-permute-start | bytes 393224 | tf_op jit(solution)/shard_map/ppermute | solution.py:350
  5.6 0.1 collective-permute-start.4
  5.7 1.7 %collective-permute-start.6 = (bf16[1,1,128,512]{3,2,1,0:T(8,128)(2,1)S(1)}, bf16[1,1,128,512]{3,2,1,0:T(8,128)(2,1)S(1)}, u32[]{:S(2)}, u32[]{:S(2)}) collective-permute-start(bf16[1,1,128,512]{3,2,1,0:T(8,128)(2,1)S(1)} %get-tuple-element.20.k_ref), channel_id=1, source_target_pairs={{0,1},{1,4},{2,3},{3,6},{4,5},{5,8},{6,7},{7,10},{8,9},{9,12},{10,... | collective-permute-start | bytes 393224 | tf_op jit(solution)/shard_map/ppermute | solution.py:354
  7.4 0.3 %collective-permute-start.7 = (bf16[1,1,128,512]{3,2,1,0:T(8,128)(2,1)S(1)}, bf16[1,1,128,512]{3,2,1,0:T(8,128)(2,1)S(1)}, u32[]{:S(2)}, u32[]{:S(2)}) collective-permute-start(bf16[1,1,128,512]{3,2,1,0:T(8,128)(2,1)S(1)} %get-tuple-element.21.v_ref), channel_id=1, source_target_pairs={{0,2},{1,3},{2,4},{3,5},{4,6},{5,7},{6,8},{7,9},{8,10},{9,11},{10,... | collective-permute-start | bytes 393224 | tf_op jit(solution)/shard_map/ppermute | solution.py:355
  7.7 1.7 %collective-permute-done.refs_2_ = bf16[1,1,128,512]{3,2,1,0:T(8,128)(2,1)S(1)} collective-permute-done((bf16[1,1,128,512]{3,2,1,0:T(8,128)(2,1)S(1)}, bf16[1,1,128,512]{3,2,1,0:T(8,128)(2,1)S(1)}, u32[]{:S(2)}, u32[]{:S(2)}) %collective-permute-start) | collective-permute-done | bytes 131104 | tf_op jit(solution)/shard_map/ppermute | solution.py:349
  9.4 1.9 %collective-permute-start.1 = (bf16[1,1,128,512]{3,2,1,0:T(8,128)(2,1)S(1)}, bf16[1,1,128,512]{3,2,1,0:T(8,128)(2,1)S(1)}, u32[]{:S(2)}, u32[]{:S(2)}) collective-permute-start(bf16[1,1,128,512]{3,2,1,0:T(8,128)(2,1)S(1)} %collective-permute-done.refs_2_), channel_id=1, source_target_pairs={{2,3},{3,2},{4,5},{5,4},{6,7},{7,6},{8,9},{9,8},{10,11},{11,10},{1... | collective-permute-start | bytes 393224 | tf_op jit(solution)/shard_map/ppermute | solution.py:357
  11.3 0.0 collective-permute-done.2.refs_1_
  11.3 1.2 %collective-permute-start.3 = (bf16[1,1,128,512]{3,2,1,0:T(8,128)(2,1)S(1)}, bf16[1,1,128,512]{3,2,1,0:T(8,128)(2,1)S(1)}, u32[]{:S(2)}, u32[]{:S(2)}) collective-permute-start(bf16[1,1,128,512]{3,2,1,0:T(8,128)(2,1)S(1)} %collective-permute-done.2.refs_1_), channel_id=1, source_target_pairs={{1,3},{4,2},{3,5},{6,4},{5,7},{8,6},{7,9},{10,8},{9,11},{12,10},{1... | collective-permute-start | bytes 393224 | tf_op jit(solution)/shard_map/ppermute | solution.py:358
  12.5 0.0 collective-permute-done.4.got_ref.refs_2_
  12.6 0.1 collective-permute-start.5
  12.7 2.2 %attend_own.1 = (bf16[544,128]{1,0:T(8,128)(2,1)S(1)}, bf16[4,128,1024]{2,1,0:T(8,128)(2,1)S(1)}, f32[4,128,1024]{2,1,0:T(8,128)S(1)}, f32[4,1024]{1,0:T(4,128)S(1)}, f32[4,1024]{1,0:T(4,128)S(1)}) custom-call(s32[6,8,128]{2,1,0:T(8,128)S(1)} %get-tuple-element.19.place_ref.refs_0_, bf16[1,128,4096]{2,1,0:T(8,128)(2,1)} %q_hbm.1, ...), custom_call_target="tpu_custom_call" | custom-call | flops 536870912 | bytes 2097152 | tf_op jit(solution)/shard_map/attend_own/pallas_call | solution.py:385
  14.9 0.0 collective-permute-done.6.refs_0_
  14.9 0.0 collective-permute-done.7.refs_3_
  14.9 1.9 %attend_near.1 = (f32[4,128,1024]{2,1,0:T(8,128)S(1)}, f32[4,1024]{1,0:T(4,128)S(1)}, f32[4,1024]{1,0:T(4,128)S(1)}) custom-call(bf16[544,128]{1,0:T(8,128)(2,1)S(1)} %get-tuple-element.22.mask_ref, bf16[4,128,1024]{2,1,0:T(8,128)(2,1)S(1)} %get-tuple-element.23.qt_ref, bf16[1,1,128,512]{3,2,1,0:T(8,128)(2,1)S(1)} %collective-permute-done.6.refs_0_, ...), custom_call_target="tpu_custom_call" | custom-call | flops 134217728 | bytes 524288 | tf_op jit(solution)/shard_map/attend_near/pallas_call | solution.py:401
  16.8 1.5 %collective-permute-done.5.in_ref = bf16[2,2,16,512]{3,2,1,0:T(8,128)(2,1)S(1)} collective-permute-done((bf16[2,2,16,512]{3,2,1,0:T(8,128)(2,1)S(1)}, bf16[2,2,16,512]{3,2,1,0:T(8,128)(2,1)S(1)}, u32[]{:S(2)}, u32[]{:S(2)}) %collective-permute-start.5) | collective-permute-done | bytes 65568 | tf_op jit(solution)/shard_map/ppermute | solution.py:324
  18.3 0.0 collective-permute-done.1.k_ref
  18.3 0.0 collective-permute-done.3.v_ref
  18.3 1.8 %attend_far.1 = bf16[1,128,4096]{2,1,0:T(8,128)(2,1)} custom-call(bf16[544,128]{1,0:T(8,128)(2,1)S(1)} %get-tuple-element.22.mask_ref, bf16[4,128,1024]{2,1,0:T(8,128)(2,1)S(1)} %get-tuple-element.23.qt_ref, bf16[1,1,128,512]{3,2,1,0:T(8,128)(2,1)S(1)} %collective-permute-done.1.k_ref, bf16[1,1,128,512]{3,2,1,0:T(8,128)(2,1)S(1)} %collective-permute-done.3.v_ref, ...), custom_call_target="tpu_custom_call" | custom-call | flops 268435456 | bytes 1048576 | tf_op jit(solution)/shard_map/attend_far/pallas_call | solution.py:410
  (2 shorter events, 0.0 us)
Async XLA Ops:
  1.1 8.3 %collective-permute-start = (bf16[1,1,128,512]{3,2,1,0:T(8,128)(2,1)S(1)}, bf16[1,1,128,512]{3,2,1,0:T(8,128)(2,1)S(1)}, u32[]{:S(2)}, u32[]{:S(2)}) collective-permute-start(bf16[1,1,128,512]{3,2,1,0:T(8,128)(2,1)S(1)} %get-tuple-element.20.k_ref), channel_id=1, source_target_pairs={{0,2},{1,3},{2,4},{3,5},{4,6},{5,7},{6,8},{7,9},{8,10},{9,11},{10,... | collective-permute-start | bytes 393224 | tf_op jit(solution)/shard_map/ppermute | solution.py:349
  4.2 7.2 %collective-permute-start.2 = (bf16[1,1,128,512]{3,2,1,0:T(8,128)(2,1)S(1)}, bf16[1,1,128,512]{3,2,1,0:T(8,128)(2,1)S(1)}, u32[]{:S(2)}, u32[]{:S(2)}) collective-permute-start(bf16[1,1,128,512]{3,2,1,0:T(8,128)(2,1)S(1)} %get-tuple-element.21.v_ref), channel_id=1, source_target_pairs={{0,1},{1,4},{2,3},{3,6},{4,5},{5,8},{6,7},{7,10},{8,9},{9,12},{10,... | collective-permute-start | bytes 393224 | tf_op jit(solution)/shard_map/ppermute | solution.py:350
  5.6 6.9 %collective-permute-start.4 = (bf16[3,2,16,512]{3,2,1,0:T(8,128)(2,1)S(1)}, bf16[3,2,16,512]{3,2,1,0:T(8,128)(2,1)S(1)}, u32[]{:S(2)}, u32[]{:S(2)}) collective-permute-start(bf16[3,2,16,512]{3,2,1,0:T(8,128)(2,1)S(1)} %get-tuple-element.25), channel_id=1, source_target_pairs={{0,2},{1,3},{2,0},{3,1},{4,6},{5,7},{6,4},{7,5},{8,10},{9,11},{10,... | collective-permute-start | bytes 294920 | tf_op jit(solution)/shard_map/ppermute | solution.py:324
  5.7 9.2 %collective-permute-start.6 = (bf16[1,1,128,512]{3,2,1,0:T(8,128)(2,1)S(1)}, bf16[1,1,128,512]{3,2,1,0:T(8,128)(2,1)S(1)}, u32[]{:S(2)}, u32[]{:S(2)}) collective-permute-start(bf16[1,1,128,512]{3,2,1,0:T(8,128)(2,1)S(1)} %get-tuple-element.20.k_ref), channel_id=1, source_target_pairs={{0,1},{1,4},{2,3},{3,6},{4,5},{5,8},{6,7},{7,10},{8,9},{9,12},{10,... | collective-permute-start | bytes 393224 | tf_op jit(solution)/shard_map/ppermute | solution.py:354
  7.4 7.5 %collective-permute-start.7 = (bf16[1,1,128,512]{3,2,1,0:T(8,128)(2,1)S(1)}, bf16[1,1,128,512]{3,2,1,0:T(8,128)(2,1)S(1)}, u32[]{:S(2)}, u32[]{:S(2)}) collective-permute-start(bf16[1,1,128,512]{3,2,1,0:T(8,128)(2,1)S(1)} %get-tuple-element.21.v_ref), channel_id=1, source_target_pairs={{0,2},{1,3},{2,4},{3,5},{4,6},{5,7},{6,8},{7,9},{8,10},{9,11},{10,... | collective-permute-start | bytes 393224 | tf_op jit(solution)/shard_map/ppermute | solution.py:355
  9.4 8.9 %collective-permute-start.1 = (bf16[1,1,128,512]{3,2,1,0:T(8,128)(2,1)S(1)}, bf16[1,1,128,512]{3,2,1,0:T(8,128)(2,1)S(1)}, u32[]{:S(2)}, u32[]{:S(2)}) collective-permute-start(bf16[1,1,128,512]{3,2,1,0:T(8,128)(2,1)S(1)} %collective-permute-done.refs_2_), channel_id=1, source_target_pairs={{2,3},{3,2},{4,5},{5,4},{6,7},{7,6},{8,9},{9,8},{10,11},{11,10},{1... | collective-permute-start | bytes 393224 | tf_op jit(solution)/shard_map/ppermute | solution.py:357
  11.3 6.9 %collective-permute-start.3 = (bf16[1,1,128,512]{3,2,1,0:T(8,128)(2,1)S(1)}, bf16[1,1,128,512]{3,2,1,0:T(8,128)(2,1)S(1)}, u32[]{:S(2)}, u32[]{:S(2)}) collective-permute-start(bf16[1,1,128,512]{3,2,1,0:T(8,128)(2,1)S(1)} %collective-permute-done.2.refs_1_), channel_id=1, source_target_pairs={{1,3},{4,2},{3,5},{6,4},{5,7},{8,6},{7,9},{10,8},{9,11},{12,10},{1... | collective-permute-start | bytes 393224 | tf_op jit(solution)/shard_map/ppermute | solution.py:358
  12.6 5.7 %collective-permute-start.5 = (bf16[2,2,16,512]{3,2,1,0:T(8,128)(2,1)S(1)}, bf16[2,2,16,512]{3,2,1,0:T(8,128)(2,1)S(1)}, u32[]{:S(2)}, u32[]{:S(2)}) collective-permute-start(bf16[2,2,16,512]{3,2,1,0:T(8,128)(2,1)S(1)} %relay_rows.1), channel_id=1, source_target_pairs={{0,1},{1,0},{2,3},{3,2},{4,5},{5,4},{6,7},{7,6},{8,9},{9,8},{10,11... | collective-permute-start | bytes 196616 | tf_op jit(solution)/shard_map/ppermute | solution.py:324

commit v8 on v7

--- a/solution.py
+++ b/solution.py
@@ -132,10 +132,6 @@
     return jnp.broadcast_to(place_ref[i][:1, :1] == place, shape)
 
 
-def pass_kernel(in_ref, out_ref):
-    out_ref[...] = in_ref[...]
-
-
 def relay_kernel(place_ref, mine_ref, got_ref, out_ref):
     at = (lax.axis_index("grp") ^ 1) & 1
     for slot in range(2):
@@ -365,15 +361,7 @@
             cost_estimate=cost(32),
             name="relay_rows",
         )(place, near_rows, got_rows)
-        relayed = pl.pallas_call(
-            pass_kernel,
-            out_shape=rows_of(2),
-            in_specs=[VMEM],
-            out_specs=VMEM,
-            compiler_params=PARAMS,
-            cost_estimate=cost(4),
-            name="settle",
-        )(flip(relayed, 1))
+        relayed = flip(relayed, 1)
         prefix = [place, own_rows, got_rows, relayed]
     else:
         prefix = [fetch_prefix(seg_len, seg_task, task_slot, prefix_bank, t)]

time: 20.2 us -> 20.2 us (level)
  transfers between devices with their start and end apart: 8 -> 8, of which waited for: 2 -> 2; matrix products, arithmetic and copies ran while one was open for 0% -> 0% of each run, Pallas kernels for 21% -> 20%
where the time goes in v8:
time: 20.2 us; the launch traced here: 20.1 us
  starting transfers between devices  9.73 us (48%)
  Pallas kernels  7.02 us (35%)
  waiting for transfers between devices  3.25 us (16%)
    ppermute x1, starting transfers between devices, on_device(): side_keys = lax.ppermute(keys, AXES, side)  3.03 us
    pallas_call x1, Pallas kernels, on_device(): pl.pallas_call(functools.partial(own_kernel, groups, kinds, row_shape[1])...  2.23 us
    ppermute x1, starting transfers between devices, on_device(): far_keys = lax.ppermute(side_keys, AXES, compose_route(far, side))  1.93 us
    pallas_call x1, Pallas kernels, on_device(): pl.pallas_call(near_kernel, out_shape=[wide, flat, flat], in_specs=[VMEM]...  1.85 us
    pallas_call x1, Pallas kernels, on_device(): pl.pallas_call(functools.partial(far_kernel, groups, plane, kinds[-1]), o...  1.79 us
    ppermute x1, waiting for transfers between devices, on_device(): side_keys = lax.ppermute(keys, AXES, side)  1.72 us
    ppermute x1, starting transfers between devices, on_device(): near_keys = lax.ppermute(keys, AXES, near)  1.7 us
    ppermute x2, waiting for transfers between devices, flip(): return lax.ppermute(array, 'grp', [(i, i ^ k) for i in range(grp_count)])  1.5 us
  transfers between devices with their start and end apart: 8, of which 2 were waited for; matrix products, arithmetic and copies ran while one was open for 0% of the time, Pallas kernels for 20%

profile of v8, /device:TPU:0, one launch (start us, length us, event | category | flops | bytes accessed | tf_op | source)
XLA Modules:
  0.0 20.1 jit_solution(18298061369048418123)
XLA Ops:
  0.0 1.1 %plan.1 = (s32[6,8,128]{2,1,0:T(8,128)S(1)}, bf16[1,1,128,512]{3,2,1,0:T(8,128)(2,1)S(1)}, bf16[1,1,128,512]{3,2,1,0:T(8,128)(2,1)S(1)}, bf16[2,2,16,512]{3,2,1,...) custom-call(s32[1,16]{1,0:T(1,128)} %refs_0_.1, s32[1,16]{1,0:T(1,128)} %refs_1_.1, ...), custom_call_target="tpu_custom_call" | custom-call | tf_op jit(solution)/shard_map/plan/pallas_call | solution.py:334
  1.1 3.0 %collective-permute-start = (bf16[1,1,128,512]{3,2,1,0:T(8,128)(2,1)S(1)}, bf16[1,1,128,512]{3,2,1,0:T(8,128)(2,1)S(1)}, u32[]{:S(2)}, u32[]{:S(2)}) collective-permute-start(bf16[1,1,128,512]{3,2,1,0:T(8,128)(2,1)S(1)} %get-tuple-element.20.k_ref), channel_id=1, source_target_pairs={{0,2},{1,3},{2,4},{3,5},{4,6},{5,7},{6,8},{7,9},{8,10},{9,11},{10,... | collective-permute-start | bytes 393224 | tf_op jit(solution)/shard_map/ppermute | solution.py:345
  4.2 1.5 %collective-permute-start.2 = (bf16[1,1,128,512]{3,2,1,0:T(8,128)(2,1)S(1)}, bf16[1,1,128,512]{3,2,1,0:T(8,128)(2,1)S(1)}, u32[]{:S(2)}, u32[]{:S(2)}) collective-permute-start(bf16[1,1,128,512]{3,2,1,0:T(8,128)(2,1)S(1)} %get-tuple-element.21.v_ref), channel_id=1, source_target_pairs={{0,1},{1,4},{2,3},{3,6},{4,5},{5,8},{6,7},{7,10},{8,9},{9,12},{10,... | collective-permute-start | bytes 393224 | tf_op jit(solution)/shard_map/ppermute | solution.py:346
  5.6 0.1 collective-permute-start.4
  5.7 1.7 %collective-permute-start.6 = (bf16[1,1,128,512]{3,2,1,0:T(8,128)(2,1)S(1)}, bf16[1,1,128,512]{3,2,1,0:T(8,128)(2,1)S(1)}, u32[]{:S(2)}, u32[]{:S(2)}) collective-permute-start(bf16[1,1,128,512]{3,2,1,0:T(8,128)(2,1)S(1)} %get-tuple-element.20.k_ref), channel_id=1, source_target_pairs={{0,1},{1,4},{2,3},{3,6},{4,5},{5,8},{6,7},{7,10},{8,9},{9,12},{10,... | collective-permute-start | bytes 393224 | tf_op jit(solution)/shard_map/ppermute | solution.py:350
  7.4 0.3 %collective-permute-start.7 = (bf16[1,1,128,512]{3,2,1,0:T(8,128)(2,1)S(1)}, bf16[1,1,128,512]{3,2,1,0:T(8,128)(2,1)S(1)}, u32[]{:S(2)}, u32[]{:S(2)}) collective-permute-start(bf16[1,1,128,512]{3,2,1,0:T(8,128)(2,1)S(1)} %get-tuple-element.21.v_ref), channel_id=1, source_target_pairs={{0,2},{1,3},{2,4},{3,5},{4,6},{5,7},{6,8},{7,9},{8,10},{9,11},{10,... | collective-permute-start | bytes 393224 | tf_op jit(solution)/shard_map/ppermute | solution.py:351
  7.7 1.7 %collective-permute-done.refs_2_ = bf16[1,1,128,512]{3,2,1,0:T(8,128)(2,1)S(1)} collective-permute-done((bf16[1,1,128,512]{3,2,1,0:T(8,128)(2,1)S(1)}, bf16[1,1,128,512]{3,2,1,0:T(8,128)(2,1)S(1)}, u32[]{:S(2)}, u32[]{:S(2)}) %collective-permute-start) | collective-permute-done | bytes 131104 | tf_op jit(solution)/shard_map/ppermute | solution.py:345
  9.4 1.9 %collective-permute-start.1 = (bf16[1,1,128,512]{3,2,1,0:T(8,128)(2,1)S(1)}, bf16[1,1,128,512]{3,2,1,0:T(8,128)(2,1)S(1)}, u32[]{:S(2)}, u32[]{:S(2)}) collective-permute-start(bf16[1,1,128,512]{3,2,1,0:T(8,128)(2,1)S(1)} %collective-permute-done.refs_2_), channel_id=1, source_target_pairs={{2,3},{3,2},{4,5},{5,4},{6,7},{7,6},{8,9},{9,8},{10,11},{11,10},{1... | collective-permute-start | bytes 393224 | tf_op jit(solution)/shard_map/ppermute | solution.py:353
  11.3 0.0 collective-permute-done.2.refs_1_
  11.3 1.2 %collective-permute-start.3 = (bf16[1,1,128,512]{3,2,1,0:T(8,128)(2,1)S(1)}, bf16[1,1,128,512]{3,2,1,0:T(8,128)(2,1)S(1)}, u32[]{:S(2)}, u32[]{:S(2)}) collective-permute-start(bf16[1,1,128,512]{3,2,1,0:T(8,128)(2,1)S(1)} %collective-permute-done.2.refs_1_), channel_id=1, source_target_pairs={{1,3},{4,2},{3,5},{6,4},{5,7},{8,6},{7,9},{10,8},{9,11},{12,10},{1... | collective-permute-start | bytes 393224 | tf_op jit(solution)/shard_map/ppermute | solution.py:354
  12.5 0.0 collective-permute-done.4.got_ref.refs_2_
  12.6 0.1 collective-permute-start.5
  12.7 2.2 %attend_own.1 = (bf16[544,128]{1,0:T(8,128)(2,1)S(1)}, bf16[4,128,1024]{2,1,0:T(8,128)(2,1)S(1)}, f32[4,128,1024]{2,1,0:T(8,128)S(1)}, f32[4,1024]{1,0:T(4,128)S(1)}, f32[4,1024]{1,0:T(4,128)S(1)}) custom-call(s32[6,8,128]{2,1,0:T(8,128)S(1)} %get-tuple-element.19.place_ref.refs_0_, bf16[1,128,4096]{2,1,0:T(8,128)(2,1)} %q_hbm.1, ...), custom_call_target="tpu_custom_call" | custom-call | flops 536870912 | bytes 2097152 | tf_op jit(solution)/shard_map/attend_own/pallas_call | solution.py:373
  14.9 0.0 collective-permute-done.6.refs_0_
  14.9 0.0 collective-permute-done.7.refs_3_
  14.9 1.8 %attend_near.1 = (f32[4,128,1024]{2,1,0:T(8,128)S(1)}, f32[4,1024]{1,0:T(4,128)S(1)}, f32[4,1024]{1,0:T(4,128)S(1)}) custom-call(bf16[544,128]{1,0:T(8,128)(2,1)S(1)} %get-tuple-element.22.mask_ref, bf16[4,128,1024]{2,1,0:T(8,128)(2,1)S(1)} %get-tuple-element.23.qt_ref, bf16[1,1,128,512]{3,2,1,0:T(8,128)(2,1)S(1)} %collective-permute-done.6.refs_0_, ...), custom_call_target="tpu_custom_call" | custom-call | flops 134217728 | bytes 524288 | tf_op jit(solution)/shard_map/attend_near/pallas_call | solution.py:389
  16.8 1.5 %collective-permute-done.5.refs_3_ = bf16[2,2,16,512]{3,2,1,0:T(8,128)(2,1)S(1)} collective-permute-done((bf16[2,2,16,512]{3,2,1,0:T(8,128)(2,1)S(1)}, bf16[2,2,16,512]{3,2,1,0:T(8,128)(2,1)S(1)}, u32[]{:S(2)}, u32[]{:S(2)}) %collective-permute-start.5) | collective-permute-done | bytes 65568 | tf_op jit(solution)/shard_map/ppermute | solution.py:320
  18.3 0.0 collective-permute-done.1.k_ref
  18.3 0.0 collective-permute-done.3.v_ref
  18.3 1.8 %attend_far.1 = bf16[1,128,4096]{2,1,0:T(8,128)(2,1)} custom-call(bf16[544,128]{1,0:T(8,128)(2,1)S(1)} %get-tuple-element.22.mask_ref, bf16[4,128,1024]{2,1,0:T(8,128)(2,1)S(1)} %get-tuple-element.23.qt_ref, bf16[1,1,128,512]{3,2,1,0:T(8,128)(2,1)S(1)} %collective-permute-done.1.k_ref, bf16[1,1,128,512]{3,2,1,0:T(8,128)(2,1)S(1)} %collective-permute-done.3.v_ref, ...), custom_call_target="tpu_custom_call" | custom-call | flops 268435456 | bytes 1048576 | tf_op jit(solution)/shard_map/attend_far/pallas_call | solution.py:398
  (1 shorter events, 0.0 us)
Async XLA Ops:
  1.1 8.3 %collective-permute-start = (bf16[1,1,128,512]{3,2,1,0:T(8,128)(2,1)S(1)}, bf16[1,1,128,512]{3,2,1,0:T(8,128)(2,1)S(1)}, u32[]{:S(2)}, u32[]{:S(2)}) collective-permute-start(bf16[1,1,128,512]{3,2,1,0:T(8,128)(2,1)S(1)} %get-tuple-element.20.k_ref), channel_id=1, source_target_pairs={{0,2},{1,3},{2,4},{3,5},{4,6},{5,7},{6,8},{7,9},{8,10},{9,11},{10,... | collective-permute-start | bytes 393224 | tf_op jit(solution)/shard_map/ppermute | solution.py:345
  4.2 7.2 %collective-permute-start.2 = (bf16[1,1,128,512]{3,2,1,0:T(8,128)(2,1)S(1)}, bf16[1,1,128,512]{3,2,1,0:T(8,128)(2,1)S(1)}, u32[]{:S(2)}, u32[]{:S(2)}) collective-permute-start(bf16[1,1,128,512]{3,2,1,0:T(8,128)(2,1)S(1)} %get-tuple-element.21.v_ref), channel_id=1, source_target_pairs={{0,1},{1,4},{2,3},{3,6},{4,5},{5,8},{6,7},{7,10},{8,9},{9,12},{10,... | collective-permute-start | bytes 393224 | tf_op jit(solution)/shard_map/ppermute | solution.py:346
  5.6 6.9 %collective-permute-start.4 = (bf16[3,2,16,512]{3,2,1,0:T(8,128)(2,1)S(1)}, bf16[3,2,16,512]{3,2,1,0:T(8,128)(2,1)S(1)}, u32[]{:S(2)}, u32[]{:S(2)}) collective-permute-start(bf16[3,2,16,512]{3,2,1,0:T(8,128)(2,1)S(1)} %get-tuple-element.25), channel_id=1, source_target_pairs={{0,2},{1,3},{2,0},{3,1},{4,6},{5,7},{6,4},{7,5},{8,10},{9,11},{10,... | collective-permute-start | bytes 294920 | tf_op jit(solution)/shard_map/ppermute | solution.py:320
  5.7 9.2 %collective-permute-start.6 = (bf16[1,1,128,512]{3,2,1,0:T(8,128)(2,1)S(1)}, bf16[1,1,128,512]{3,2,1,0:T(8,128)(2,1)S(1)}, u32[]{:S(2)}, u32[]{:S(2)}) collective-permute-start(bf16[1,1,128,512]{3,2,1,0:T(8,128)(2,1)S(1)} %get-tuple-element.20.k_ref), channel_id=1, source_target_pairs={{0,1},{1,4},{2,3},{3,6},{4,5},{5,8},{6,7},{7,10},{8,9},{9,12},{10,... | collective-permute-start | bytes 393224 | tf_op jit(solution)/shard_map/ppermute | solution.py:350
  7.4 7.5 %collective-permute-start.7 = (bf16[1,1,128,512]{3,2,1,0:T(8,128)(2,1)S(1)}, bf16[1,1,128,512]{3,2,1,0:T(8,128)(2,1)S(1)}, u32[]{:S(2)}, u32[]{:S(2)}) collective-permute-start(bf16[1,1,128,512]{3,2,1,0:T(8,128)(2,1)S(1)} %get-tuple-element.21.v_ref), channel_id=1, source_target_pairs={{0,2},{1,3},{2,4},{3,5},{4,6},{5,7},{6,8},{7,9},{8,10},{9,11},{10,... | collective-permute-start | bytes 393224 | tf_op jit(solution)/shard_map/ppermute | solution.py:351
  9.4 8.9 %collective-permute-start.1 = (bf16[1,1,128,512]{3,2,1,0:T(8,128)(2,1)S(1)}, bf16[1,1,128,512]{3,2,1,0:T(8,128)(2,1)S(1)}, u32[]{:S(2)}, u32[]{:S(2)}) collective-permute-start(bf16[1,1,128,512]{3,2,1,0:T(8,128)(2,1)S(1)} %collective-permute-done.refs_2_), channel_id=1, source_target_pairs={{2,3},{3,2},{4,5},{5,4},{6,7},{7,6},{8,9},{9,8},{10,11},{11,10},{1... | collective-permute-start | bytes 393224 | tf_op jit(solution)/shard_map/ppermute | solution.py:353
  11.3 6.9 %collective-permute-start.3 = (bf16[1,1,128,512]{3,2,1,0:T(8,128)(2,1)S(1)}, bf16[1,1,128,512]{3,2,1,0:T(8,128)(2,1)S(1)}, u32[]{:S(2)}, u32[]{:S(2)}) collective-permute-start(bf16[1,1,128,512]{3,2,1,0:T(8,128)(2,1)S(1)} %collective-permute-done.2.refs_1_), channel_id=1, source_target_pairs={{1,3},{4,2},{3,5},{6,4},{5,7},{8,6},{7,9},{10,8},{9,11},{12,10},{1... | collective-permute-start | bytes 393224 | tf_op jit(solution)/shard_map/ppermute | solution.py:354
  12.6 5.7 %collective-permute-start.5 = (bf16[2,2,16,512]{3,2,1,0:T(8,128)(2,1)S(1)}, bf16[2,2,16,512]{3,2,1,0:T(8,128)(2,1)S(1)}, u32[]{:S(2)}, u32[]{:S(2)}) collective-permute-start(bf16[2,2,16,512]{3,2,1,0:T(8,128)(2,1)S(1)} %relay_rows.1), channel_id=1, source_target_pairs={{0,1},{1,0},{2,3},{3,2},{4,5},{5,4},{6,7},{7,6},{8,9},{9,8},{10,11... | collective-permute-start | bytes 196616 | tf_op jit(solution)/shard_map/ppermute | solution.py:320
